TPU v7x, 256 devices: a whole 4x4x8 slice. The times are simulated.
256 devices in a mesh: dp: 16 (over z, y_lo), blk: 16 (over x, y_hi, core).
Axes of the slice: x: 4, y: 4 (y_hi: 2, y_lo: 2; y = y_hi * 2 + y_lo), z: 8, core: 2. Of those that a mesh axis runs over, the one named last changes fastest.
Arguments:
- image: bfloat16 [65536, 768], P(('dp', 'blk')), may hold values from -100 to 100
- text: bfloat16 [65536, 768], P(('dp', 'blk')), may hold values from -100 to 100
- positive: int32 [65536], P(('dp', 'blk')), may hold values from 0 to 255, as said below
- logit_scale: float32 [1], replicated, may hold values from 10 to 300
Outputs:
- loss: float32 [1], replicated
- scale_grad: float32 [1], replicated
- image_grad: bfloat16 [65536, 768], P(('dp', 'blk'))
- text_grad: bfloat16 [65536, 768], P(('dp', 'blk'))
Inputs may be any that keep to these rules, and one draw needn't show every extreme that they name: `positive`: within each aligned block of 256 rows (the rows of one device) the entries are a permutation of 0 to 255.
All inputs are finite; a program needn't handle non-finite values.
Results may differ from a plain program's by a relative error of at most 0.0055.
The roundings to bfloat16 on the way count: a program that leaves them out, or rounds other values in their place, can miss the bound.
Values may be sent and summed in bfloat16 or wider, within the bound.
No kernel may reach another device: no remote copies, remote signals or barrier semaphores. Data moves between devices by JAX's collectives and lax.ppermute only.
A program may use at most 64 MiB of HBM per device.

v0:
```python
import jax
import jax.numpy as jnp
from jax import lax
from jax.sharding import PartitionSpec as P

EPSILON = 1e-06


def passed_along(value, axis, by):
    peers = lax.axis_size(axis)
    return lax.ppermute(value, axis, [(i, (i + by) % peers) for i in range(peers)])


def unit_rows(values):
    wide = values.astype(jnp.float32)
    inverse = lax.rsqrt(jnp.sum(wide * wide, axis=-1, keepdims=True) + EPSILON)
    direction = wide * inverse
    return (direction, direction.astype(jnp.bfloat16), inverse)


def back_rows(direction, inverse, incoming):
    along = jnp.sum(direction * incoming, axis=-1, keepdims=True)
    return ((incoming - direction * along) * inverse).astype(jnp.bfloat16)


def fold_blocks(piece, stride, carry, visit):
    count = piece.shape[0]
    stacked = piece.reshape(count // stride, stride, piece.shape[1])
    begins = stride * jnp.arange(count // stride, dtype=jnp.int32)

    def advance(state, item):
        block, begin = item
        return (visit(state, block, begin), None)

    state, unused = lax.scan(advance, carry, (stacked, begins))
    return state


def shards(image, text, positive, logit_scale):
    scale = logit_scale[0]
    rows = image.shape[0]
    width_d = image.shape[1]
    blocks = lax.axis_size("blk")
    me = lax.axis_index("blk")
    stride = rows * max(1, 1024 // rows)
    img_dir, img_unit, img_inv = unit_rows(image)
    txt_dir, txt_unit, txt_inv = unit_rows(text)
    target = me * rows + positive

    def tile_weight(left, right, left_lse, right_lse, left_target, right_begin):
        logits = scale * jnp.einsum("rd,cd->rc", left, right, preferred_element_type=jnp.float32)
        columns = right_begin + jnp.arange(right.shape[0], dtype=jnp.int32)
        hit = (left_target[:, None] == columns[None, :]).astype(jnp.float32)
        weight = (
            0.5 * (jnp.exp(logits - left_lse[:, None]) + jnp.exp(logits - right_lse[None, :])) - hit
        )
        return (weight, logits)

    def column_visit(state, block, begin):
        row_top, row_total, col_top, col_total = state
        logits = scale * jnp.einsum(
            "rd,cd->rc", img_unit, block, preferred_element_type=jnp.float32
        )
        new_top = jnp.maximum(row_top, jnp.max(logits, axis=1))
        row_total = row_total * jnp.exp(row_top - new_top) + jnp.sum(
            jnp.exp(logits - new_top[:, None]), axis=1
        )
        block_top = jnp.max(logits, axis=0)
        block_total = jnp.sum(jnp.exp(logits - block_top[None, :]), axis=0)
        col_top = lax.dynamic_update_slice_in_dim(col_top, block_top, begin, 0)
        col_total = lax.dynamic_update_slice_in_dim(col_total, block_total, begin, 0)
        return (new_top, row_total, col_top, col_total)

    group = rows * blocks
    start_state = (
        jnp.full((rows,), -1e30, jnp.float32),
        jnp.zeros((rows,), jnp.float32),
        jnp.zeros((group,), jnp.float32),
        jnp.zeros((group,), jnp.float32),
    )
    forward_state = fold_blocks(
        lax.all_gather(txt_unit, "blk", axis=0, tiled=True), stride, start_state, column_visit
    )
    row_top, row_total, col_top, col_total = forward_state
    row_lse = row_top + jnp.log(row_total)
    tops, totals_part = (
        lax.all_to_all(
            col_top.reshape(blocks, rows), "blk", split_axis=0, concat_axis=0, tiled=True
        ),
        lax.all_to_all(
            col_total.reshape(blocks, rows), "blk", split_axis=0, concat_axis=0, tiled=True
        ),
    )
    highest = jnp.max(tops, axis=0)
    col_lse = highest + jnp.log(jnp.sum(totals_part * jnp.exp(tops - highest[None, :]), axis=0))
    matched = scale * jnp.einsum(
        "rd,rd->r", img_unit, txt_unit[positive], preferred_element_type=jnp.float32
    )
    loss_part = 0.5 * (jnp.sum(row_lse) + jnp.sum(col_lse)) - jnp.sum(matched)

    def cycle_turn(turn, state):
        block, carried, block_lse, grad_img, slope = state
        arriving = passed_along(block, "blk", 1)
        owner = (me - turn + blocks) % blocks
        weight, logits = tile_weight(img_unit, block, row_lse, block_lse, target, owner * rows)
        weight_bf = weight.astype(jnp.bfloat16)
        grad_img = grad_img + jnp.einsum(
            "rc,cd->rd", weight_bf, block, preferred_element_type=jnp.float32
        )
        carried = carried + jnp.einsum(
            "rc,rd->cd", weight_bf, img_unit, preferred_element_type=jnp.float32
        )
        slope = slope + jnp.sum(weight * logits)
        carried, block_lse = passed_along((carried, block_lse), "blk", 1)
        return (arriving, carried, block_lse, grad_img, slope)

    cycle_state = (
        txt_unit,
        jnp.zeros((rows, width_d), jnp.float32),
        col_lse,
        jnp.zeros((rows, width_d), jnp.float32),
        jnp.zeros((), jnp.float32),
    )
    unused_block, text_sum, unused_lse, image_sum, slope = lax.fori_loop(
        0, blocks, cycle_turn, cycle_state
    )
    image_grad = back_rows(img_dir, img_inv, scale * image_sum)
    text_grad = back_rows(txt_dir, txt_inv, scale * text_sum)
    loss_sum, slope_sum = lax.psum((loss_part, slope), ("dp", "blk"))
    total_rows = rows * blocks * lax.axis_size("dp")
    loss = (loss_sum / total_rows).reshape(1)
    scale_grad = (slope_sum / (total_rows * scale)).reshape(1)
    return (loss, scale_grad, image_grad, text_grad)


def solution(mesh):
    in_specs = (P(("dp", "blk"), None), P(("dp", "blk"), None), P(("dp", "blk")), P())
    out_specs = (P(), P(), P(("dp", "blk"), None), P(("dp", "blk"), None))
    return jax.shard_map(shards, mesh=mesh, in_specs=in_specs, out_specs=out_specs, check_vma=False)
```

profile of v0, /device:TPU:1, one launch (start us, length us, event | category | flops | bytes accessed | tf_op | source)
XLA Modules:
  0.0 611.5 jit_solution(11986840413571342906)
XLA Ops:
  17.2 67.6 %all-gather.2.cloned.1.call-done = bf16[4096,768]{1,0:T(8,128)(2,1)} async-done(((bf16[256,768]{1,0:T(8,128)(2,1)}), bf16[4096,768]{1,0:T(8,128)(2,1)}) %all-gather.2.cloned.1.call-update) | async-done | bytes 6291472 | tf_op jit(solution)/shard_map/all_gather | solution.py:82
  86.0 33.6 %while.41 = (s32[]{:T(128)}, f32[256]{0:T(256)S(1)}, f32[256]{0:T(256)S(1)}, f32[4096]{0:T(1024)}, f32[4096]{0:T(1024)}, /*index=5*/f32[]{:T(128)}, bf16[4,1024,...) while((s32[]{:T(128)}, f32[256]{0:T(256)S(1)}, ...), condition=%wide.region_7.8_spmd.clone, body=%wide.region_2.7_spmd.clone.sunk | while | flops 404487424 | bytes 4106422 | solution.py:35
  86.0 2.9 fusion.52
  94.5 2.8 fusion.52
  102.9 2.8 fusion.52
  111.4 2.8 fusion.52
  119.6 3.6 all-to-all-start
  123.9 6.6 %all-to-all-done = f32[16,1,256]{2,1,0:T(1,128)S(1)} async-done(((f32[16,1,256]{2,1,0:T(1,128)}), f32[16,1,256]{2,1,0:T(1,128)S(1)}, u32[]{:S(2)}, u32[]{:S(2)}) %all-to-all-start) | async-done | bytes 16416 | tf_op jit(solution)/shard_map/all_to_all | solution.py:87
  130.5 3.7 all-to-all-start.1
  134.8 6.7 %all-to-all-done.1 = f32[16,1,256]{2,1,0:T(1,128)S(1)} async-done(((f32[16,1,256]{2,1,0:T(1,128)}), f32[16,1,256]{2,1,0:T(1,128)S(1)}, u32[]{:S(2)}, u32[]{:S(2)}) %all-to-all-start.1) | async-done | bytes 16416 | tf_op jit(solution)/shard_map/all_to_all | solution.py:90
  142.2 359.8 %while.42 = (s32[]{:T(128)}, bf16[256,768]{1,0:T(8,128)(2,1)S(1)}, f32[256,768]{1,0:T(8,128)S(1)}, f32[256]{0:T(256)S(1)}, f32[256,768]{1,0:T(8,128)S(1)}, /*ind...) while((s32[]{:T(128)}, bf16[256,768]{1,0:T(8,128)(2,1)S(1)}, ...), condition=%wide.region_16.17_spmd.clone, body=%wide.region_14.16_spmd.clone.sunk | while | flops 304283904 | bytes 11029952 | solution.py:124
  142.3 2.7 multiply_reduce_fusion.3
  147.2 3.0 collective-permute-start.2
  151.3 8.9 %collective-permute-done.2 = f32[256]{0:T(256)S(1)} collective-permute-done((f32[256]{0:T(256)S(1)}, f32[256]{0:T(256)S(1)}, u32[]{:S(2)}, u32[]{:S(2)}) %collective-permute-start.2) | collective-permute-done | bytes 1056 | tf_op jit(solution)/shard_map/while/body/eval_jaxpr/ppermute | solution.py:11
  160.3 2.7 multiply_reduce_fusion.3
  164.4 4.1 collective-permute-start.1
  168.5 3.9 collective-permute-start.2
  173.6 8.0 %collective-permute-done.2 = f32[256]{0:T(256)S(1)} collective-permute-done((f32[256]{0:T(256)S(1)}, f32[256]{0:T(256)S(1)}, u32[]{:S(2)}, u32[]{:S(2)}) %collective-permute-start.2) | collective-permute-done | bytes 1056 | tf_op jit(solution)/shard_map/while/body/eval_jaxpr/ppermute | solution.py:11
  181.7 2.7 multiply_reduce_fusion.3
  185.8 4.1 collective-permute-start.1
  189.9 4.8 collective-permute-start.2
  195.9 7.1 %collective-permute-done.2 = f32[256]{0:T(256)S(1)} collective-permute-done((f32[256]{0:T(256)S(1)}, f32[256]{0:T(256)S(1)}, u32[]{:S(2)}, u32[]{:S(2)}) %collective-permute-start.2) | collective-permute-done | bytes 1056 | tf_op jit(solution)/shard_map/while/body/eval_jaxpr/ppermute | solution.py:11
  203.1 2.7 multiply_reduce_fusion.3
  207.2 4.1 collective-permute-start.1
  212.1 4.9 collective-permute-start.2
  218.2 6.2 %collective-permute-done.2 = f32[256]{0:T(256)S(1)} collective-permute-done((f32[256]{0:T(256)S(1)}, f32[256]{0:T(256)S(1)}, u32[]{:S(2)}, u32[]{:S(2)}) %collective-permute-start.2) | collective-permute-done | bytes 1056 | tf_op jit(solution)/shard_map/while/body/eval_jaxpr/ppermute | solution.py:11
  224.5 2.7 multiply_reduce_fusion.3
  228.6 4.1 collective-permute-start.1
  234.5 4.9 collective-permute-start.2
  240.5 5.3 collective-permute-done.2
  245.9 2.7 multiply_reduce_fusion.3
  250.0 4.1 collective-permute-start.1
  254.1 2.7 collective-permute-start
  256.8 4.9 collective-permute-start.2
  262.8 4.4 collective-permute-done.2
  267.3 2.7 multiply_reduce_fusion.3
  271.4 4.1 collective-permute-start.1
  275.5 3.6 collective-permute-start
  279.1 4.9 collective-permute-start.2
  285.1 5.2 collective-permute-done.2
  290.4 2.7 multiply_reduce_fusion.3
  296.9 4.5 collective-permute-start
  301.4 4.9 collective-permute-start.2
  307.4 6.4 %collective-permute-done.2 = f32[256]{0:T(256)S(1)} collective-permute-done((f32[256]{0:T(256)S(1)}, f32[256]{0:T(256)S(1)}, u32[]{:S(2)}, u32[]{:S(2)}) %collective-permute-start.2) | collective-permute-done | bytes 1056 | tf_op jit(solution)/shard_map/while/body/eval_jaxpr/ppermute | solution.py:11
  313.9 2.7 multiply_reduce_fusion.3
  318.3 5.4 collective-permute-start
  323.7 4.9 collective-permute-start.2
  329.7 7.7 %collective-permute-done.2 = f32[256]{0:T(256)S(1)} collective-permute-done((f32[256]{0:T(256)S(1)}, f32[256]{0:T(256)S(1)}, u32[]{:S(2)}, u32[]{:S(2)}) %collective-permute-start.2) | collective-permute-done | bytes 1056 | tf_op jit(solution)/shard_map/while/body/eval_jaxpr/ppermute | solution.py:11
  341.6 4.4 collective-permute-start
  346.0 4.9 collective-permute-start.2
  352.0 8.9 %collective-permute-done.2 = f32[256]{0:T(256)S(1)} collective-permute-done((f32[256]{0:T(256)S(1)}, f32[256]{0:T(256)S(1)}, u32[]{:S(2)}, u32[]{:S(2)}) %collective-permute-start.2) | collective-permute-done | bytes 1056 | tf_op jit(solution)/shard_map/while/body/eval_jaxpr/ppermute | solution.py:11
  365.1 3.2 collective-permute-start
  368.3 4.9 collective-permute-start.2
  374.3 10.1 %collective-permute-done.2 = f32[256]{0:T(256)S(1)} collective-permute-done((f32[256]{0:T(256)S(1)}, f32[256]{0:T(256)S(1)}, u32[]{:S(2)}, u32[]{:S(2)}) %collective-permute-start.2) | collective-permute-done | bytes 1056 | tf_op jit(solution)/shard_map/while/body/eval_jaxpr/ppermute | solution.py:11
  390.6 4.9 collective-permute-start.2
  396.6 11.3 %collective-permute-done.2 = f32[256]{0:T(256)S(1)} collective-permute-done((f32[256]{0:T(256)S(1)}, f32[256]{0:T(256)S(1)}, u32[]{:S(2)}, u32[]{:S(2)}) %collective-permute-start.2) | collective-permute-done | bytes 1056 | tf_op jit(solution)/shard_map/while/body/eval_jaxpr/ppermute | solution.py:11
  412.9 4.9 collective-permute-start.2
  418.9 12.5 %collective-permute-done.2 = f32[256]{0:T(256)S(1)} collective-permute-done((f32[256]{0:T(256)S(1)}, f32[256]{0:T(256)S(1)}, u32[]{:S(2)}, u32[]{:S(2)}) %collective-permute-start.2) | collective-permute-done | bytes 1056 | tf_op jit(solution)/shard_map/while/body/eval_jaxpr/ppermute | solution.py:11
  435.8 4.3 collective-permute-start.2
  441.2 13.7 %collective-permute-done.2 = f32[256]{0:T(256)S(1)} collective-permute-done((f32[256]{0:T(256)S(1)}, f32[256]{0:T(256)S(1)}, u32[]{:S(2)}, u32[]{:S(2)}) %collective-permute-start.2) | collective-permute-done | bytes 1056 | tf_op jit(solution)/shard_map/while/body/eval_jaxpr/ppermute | solution.py:11
  459.3 3.1 collective-permute-start.2
  463.5 15.0 %collective-permute-done.2 = f32[256]{0:T(256)S(1)} collective-permute-done((f32[256]{0:T(256)S(1)}, f32[256]{0:T(256)S(1)}, u32[]{:S(2)}, u32[]{:S(2)}) %collective-permute-start.2) | collective-permute-done | bytes 1056 | tf_op jit(solution)/shard_map/while/body/eval_jaxpr/ppermute | solution.py:11
  485.8 16.2 %collective-permute-done.2 = f32[256]{0:T(256)S(1)} collective-permute-done((f32[256]{0:T(256)S(1)}, f32[256]{0:T(256)S(1)}, u32[]{:S(2)}, u32[]{:S(2)}) %collective-permute-start.2) | collective-permute-done | bytes 1056 | tf_op jit(solution)/shard_map/while/body/eval_jaxpr/ppermute | solution.py:11
  509.4 91.7 %all-reduce = (f32[]{:T(128)}, f32[]{:T(128)}) all-reduce(f32[]{:T(128)S(6)} %sub.112, f32[]{:T(128)} %get-tuple-element.325), channel_id=1, replica_groups=mesh['dp'=16,'blk'=16] {'dp','blk'}, use_global_device_ids=true, to_apply=%region_13.14 | all-reduce | flops 2 | bytes 16 | tf_op jit(solution)/shard_map/psum | solution.py:129
  (196 shorter events, 94.8 us)
Async XLA Ops:
  7.2 77.7 %all-gather.2.cloned.1.call-start = ((), (), s32[]{:S(2)}) async-start(), calls=%async_computation.2 | async-start | bytes 6684672 | tf_op jit(solution)/shard_map/all_gather | solution.py:82
  86.0 56.2 %copy-start = (bf16[256,768]{1,0:T(8,128)(2,1)S(1)}, bf16[256,768]{1,0:T(8,128)(2,1)}, u32[]{:S(2)}) copy-start(bf16[256,768]{1,0:T(8,128)(2,1)} %fusion.17) | copy-start | bytes 1179652
  119.6 10.9 %all-to-all-start = ((f32[16,1,256]{2,1,0:T(1,128)}), f32[16,1,256]{2,1,0:T(1,128)S(1)}, u32[]{:S(2)}, u32[]{:S(2)}) async-start(f32[16,1,256]{2,1,0:T(1,128)} %bitcast.2), calls=%async_computation | async-start | bytes 32768 | tf_op jit(solution)/shard_map/all_to_all | solution.py:87
  130.5 11.0 %all-to-all-start.1 = ((f32[16,1,256]{2,1,0:T(1,128)}), f32[16,1,256]{2,1,0:T(1,128)S(1)}, u32[]{:S(2)}, u32[]{:S(2)}) async-start(f32[16,1,256]{2,1,0:T(1,128)} %bitcast.3), calls=%async_computation.1 | async-start | bytes 32768 | tf_op jit(solution)/shard_map/all_to_all | solution.py:90
  146.4 13.8 %collective-permute-start.1 = (f32[256,768]{1,0:T(8,128)S(1)}, f32[256,768]{1,0:T(8,128)S(1)}, u32[]{:S(2)}, u32[]{:S(2)}) collective-permute-start(f32[256,768]{1,0:T(8,128)S(1)} %convolution_add_fusion.4), channel_id=1, source_target_pairs={{0,1},{1,2},{2,3},{3,4},{4,5},{5,6},{6,7},{7,8},{8,9},{9,10},{10,1... | collective-permute-start | bytes 2359304 | tf_op jit(solution)/shard_map/while/body/eval_jaxpr/ppermute | solution.py:11
  147.0 13.2 %collective-permute-start = (bf16[256,768]{1,0:T(8,128)(2,1)S(1)}, bf16[256,768]{1,0:T(8,128)(2,1)S(1)}, u32[]{:S(2)}, u32[]{:S(2)}) collective-permute-start(bf16[256,768]{1,0:T(8,128)(2,1)S(1)} %copy.41), channel_id=1, source_target_pairs={{0,1},{1,2},{2,3},{3,4},{4,5},{5,6},{6,7},{7,8},{8,9},{9,10},{10,1... | collective-permute-start | bytes 1179656 | tf_op jit(solution)/shard_map/while/body/eval_jaxpr/ppermute | solution.py:11
  147.2 13.1 %collective-permute-start.2 = (f32[256]{0:T(256)S(1)}, f32[256]{0:T(256)S(1)}, u32[]{:S(2)}, u32[]{:S(2)}) collective-permute-start(f32[256]{0:T(256)S(1)} %copy.43), channel_id=1, source_target_pairs={{0,1},{1,2},{2,3},{3,4},{4,5},{5,6},{6,7},{7,8},{8,9},{9,10},{10,1... | collective-permute-start | bytes 3080 | tf_op jit(solution)/shard_map/while/body/eval_jaxpr/ppermute | solution.py:11
  164.4 17.3 %collective-permute-start.1 = (f32[256,768]{1,0:T(8,128)S(1)}, f32[256,768]{1,0:T(8,128)S(1)}, u32[]{:S(2)}, u32[]{:S(2)}) collective-permute-start(f32[256,768]{1,0:T(8,128)S(1)} %convolution_add_fusion.4), channel_id=1, source_target_pairs={{0,1},{1,2},{2,3},{3,4},{4,5},{5,6},{6,7},{7,8},{8,9},{9,10},{10,1... | collective-permute-start | bytes 2359304 | tf_op jit(solution)/shard_map/while/body/eval_jaxpr/ppermute | solution.py:11
  168.4 13.2 %collective-permute-start = (bf16[256,768]{1,0:T(8,128)(2,1)S(1)}, bf16[256,768]{1,0:T(8,128)(2,1)S(1)}, u32[]{:S(2)}, u32[]{:S(2)}) collective-permute-start(bf16[256,768]{1,0:T(8,128)(2,1)S(1)} %copy.41), channel_id=1, source_target_pairs={{0,1},{1,2},{2,3},{3,4},{4,5},{5,6},{6,7},{7,8},{8,9},{9,10},{10,1... | collective-permute-start | bytes 1179656 | tf_op jit(solution)/shard_map/while/body/eval_jaxpr/ppermute | solution.py:11
  168.5 13.1 %collective-permute-start.2 = (f32[256]{0:T(256)S(1)}, f32[256]{0:T(256)S(1)}, u32[]{:S(2)}, u32[]{:S(2)}) collective-permute-start(f32[256]{0:T(256)S(1)} %copy.43), channel_id=1, source_target_pairs={{0,1},{1,2},{2,3},{3,4},{4,5},{5,6},{6,7},{7,8},{8,9},{9,10},{10,1... | collective-permute-start | bytes 3080 | tf_op jit(solution)/shard_map/while/body/eval_jaxpr/ppermute | solution.py:11
  185.8 17.3 %collective-permute-start.1 = (f32[256,768]{1,0:T(8,128)S(1)}, f32[256,768]{1,0:T(8,128)S(1)}, u32[]{:S(2)}, u32[]{:S(2)}) collective-permute-start(f32[256,768]{1,0:T(8,128)S(1)} %convolution_add_fusion.4), channel_id=1, source_target_pairs={{0,1},{1,2},{2,3},{3,4},{4,5},{5,6},{6,7},{7,8},{8,9},{9,10},{10,1... | collective-permute-start | bytes 2359304 | tf_op jit(solution)/shard_map/while/body/eval_jaxpr/ppermute | solution.py:11
  189.8 13.2 %collective-permute-start = (bf16[256,768]{1,0:T(8,128)(2,1)S(1)}, bf16[256,768]{1,0:T(8,128)(2,1)S(1)}, u32[]{:S(2)}, u32[]{:S(2)}) collective-permute-start(bf16[256,768]{1,0:T(8,128)(2,1)S(1)} %copy.41), channel_id=1, source_target_pairs={{0,1},{1,2},{2,3},{3,4},{4,5},{5,6},{6,7},{7,8},{8,9},{9,10},{10,1... | collective-permute-start | bytes 1179656 | tf_op jit(solution)/shard_map/while/body/eval_jaxpr/ppermute | solution.py:11
  189.9 13.1 %collective-permute-start.2 = (f32[256]{0:T(256)S(1)}, f32[256]{0:T(256)S(1)}, u32[]{:S(2)}, u32[]{:S(2)}) collective-permute-start(f32[256]{0:T(256)S(1)} %copy.43), channel_id=1, source_target_pairs={{0,1},{1,2},{2,3},{3,4},{4,5},{5,6},{6,7},{7,8},{8,9},{9,10},{10,1... | collective-permute-start | bytes 3080 | tf_op jit(solution)/shard_map/while/body/eval_jaxpr/ppermute | solution.py:11
  207.2 17.3 %collective-permute-start.1 = (f32[256,768]{1,0:T(8,128)S(1)}, f32[256,768]{1,0:T(8,128)S(1)}, u32[]{:S(2)}, u32[]{:S(2)}) collective-permute-start(f32[256,768]{1,0:T(8,128)S(1)} %convolution_add_fusion.4), channel_id=1, source_target_pairs={{0,1},{1,2},{2,3},{3,4},{4,5},{5,6},{6,7},{7,8},{8,9},{9,10},{10,1... | collective-permute-start | bytes 2359304 | tf_op jit(solution)/shard_map/while/body/eval_jaxpr/ppermute | solution.py:11
  211.3 13.2 %collective-permute-start = (bf16[256,768]{1,0:T(8,128)(2,1)S(1)}, bf16[256,768]{1,0:T(8,128)(2,1)S(1)}, u32[]{:S(2)}, u32[]{:S(2)}) collective-permute-start(bf16[256,768]{1,0:T(8,128)(2,1)S(1)} %copy.41), channel_id=1, source_target_pairs={{0,1},{1,2},{2,3},{3,4},{4,5},{5,6},{6,7},{7,8},{8,9},{9,10},{10,1... | collective-permute-start | bytes 1179656 | tf_op jit(solution)/shard_map/while/body/eval_jaxpr/ppermute | solution.py:11
  212.1 12.3 %collective-permute-start.2 = (f32[256]{0:T(256)S(1)}, f32[256]{0:T(256)S(1)}, u32[]{:S(2)}, u32[]{:S(2)}) collective-permute-start(f32[256]{0:T(256)S(1)} %copy.43), channel_id=1, source_target_pairs={{0,1},{1,2},{2,3},{3,4},{4,5},{5,6},{6,7},{7,8},{8,9},{9,10},{10,1... | collective-permute-start | bytes 3080 | tf_op jit(solution)/shard_map/while/body/eval_jaxpr/ppermute | solution.py:11
  228.6 17.3 %collective-permute-start.1 = (f32[256,768]{1,0:T(8,128)S(1)}, f32[256,768]{1,0:T(8,128)S(1)}, u32[]{:S(2)}, u32[]{:S(2)}) collective-permute-start(f32[256,768]{1,0:T(8,128)S(1)} %convolution_add_fusion.4), channel_id=1, source_target_pairs={{0,1},{1,2},{2,3},{3,4},{4,5},{5,6},{6,7},{7,8},{8,9},{9,10},{10,1... | collective-permute-start | bytes 2359304 | tf_op jit(solution)/shard_map/while/body/eval_jaxpr/ppermute | solution.py:11
  232.7 13.2 %collective-permute-start = (bf16[256,768]{1,0:T(8,128)(2,1)S(1)}, bf16[256,768]{1,0:T(8,128)(2,1)S(1)}, u32[]{:S(2)}, u32[]{:S(2)}) collective-permute-start(bf16[256,768]{1,0:T(8,128)(2,1)S(1)} %copy.41), channel_id=1, source_target_pairs={{0,1},{1,2},{2,3},{3,4},{4,5},{5,6},{6,7},{7,8},{8,9},{9,10},{10,1... | collective-permute-start | bytes 1179656 | tf_op jit(solution)/shard_map/while/body/eval_jaxpr/ppermute | solution.py:11
  234.5 11.4 %collective-permute-start.2 = (f32[256]{0:T(256)S(1)}, f32[256]{0:T(256)S(1)}, u32[]{:S(2)}, u32[]{:S(2)}) collective-permute-start(f32[256]{0:T(256)S(1)} %copy.43), channel_id=1, source_target_pairs={{0,1},{1,2},{2,3},{3,4},{4,5},{5,6},{6,7},{7,8},{8,9},{9,10},{10,1... | collective-permute-start | bytes 3080 | tf_op jit(solution)/shard_map/while/body/eval_jaxpr/ppermute | solution.py:11
  250.0 17.3 %collective-permute-start.1 = (f32[256,768]{1,0:T(8,128)S(1)}, f32[256,768]{1,0:T(8,128)S(1)}, u32[]{:S(2)}, u32[]{:S(2)}) collective-permute-start(f32[256,768]{1,0:T(8,128)S(1)} %convolution_add_fusion.4), channel_id=1, source_target_pairs={{0,1},{1,2},{2,3},{3,4},{4,5},{5,6},{6,7},{7,8},{8,9},{9,10},{10,1... | collective-permute-start | bytes 2359304 | tf_op jit(solution)/shard_map/while/body/eval_jaxpr/ppermute | solution.py:11
  254.1 13.2 %collective-permute-start = (bf16[256,768]{1,0:T(8,128)(2,1)S(1)}, bf16[256,768]{1,0:T(8,128)(2,1)S(1)}, u32[]{:S(2)}, u32[]{:S(2)}) collective-permute-start(bf16[256,768]{1,0:T(8,128)(2,1)S(1)} %copy.41), channel_id=1, source_target_pairs={{0,1},{1,2},{2,3},{3,4},{4,5},{5,6},{6,7},{7,8},{8,9},{9,10},{10,1... | collective-permute-start | bytes 1179656 | tf_op jit(solution)/shard_map/while/body/eval_jaxpr/ppermute | solution.py:11
  256.8 10.5 %collective-permute-start.2 = (f32[256]{0:T(256)S(1)}, f32[256]{0:T(256)S(1)}, u32[]{:S(2)}, u32[]{:S(2)}) collective-permute-start(f32[256]{0:T(256)S(1)} %copy.43), channel_id=1, source_target_pairs={{0,1},{1,2},{2,3},{3,4},{4,5},{5,6},{6,7},{7,8},{8,9},{9,10},{10,1... | collective-permute-start | bytes 3080 | tf_op jit(solution)/shard_map/while/body/eval_jaxpr/ppermute | solution.py:11
  271.4 18.9 %collective-permute-start.1 = (f32[256,768]{1,0:T(8,128)S(1)}, f32[256,768]{1,0:T(8,128)S(1)}, u32[]{:S(2)}, u32[]{:S(2)}) collective-permute-start(f32[256,768]{1,0:T(8,128)S(1)} %convolution_add_fusion.4), channel_id=1, source_target_pairs={{0,1},{1,2},{2,3},{3,4},{4,5},{5,6},{6,7},{7,8},{8,9},{9,10},{10,1... | collective-permute-start | bytes 2359304 | tf_op jit(solution)/shard_map/while/body/eval_jaxpr/ppermute | solution.py:11
  275.5 14.8 %collective-permute-start = (bf16[256,768]{1,0:T(8,128)(2,1)S(1)}, bf16[256,768]{1,0:T(8,128)(2,1)S(1)}, u32[]{:S(2)}, u32[]{:S(2)}) collective-permute-start(bf16[256,768]{1,0:T(8,128)(2,1)S(1)} %copy.41), channel_id=1, source_target_pairs={{0,1},{1,2},{2,3},{3,4},{4,5},{5,6},{6,7},{7,8},{8,9},{9,10},{10,1... | collective-permute-start | bytes 1179656 | tf_op jit(solution)/shard_map/while/body/eval_jaxpr/ppermute | solution.py:11
  279.1 11.3 %collective-permute-start.2 = (f32[256]{0:T(256)S(1)}, f32[256]{0:T(256)S(1)}, u32[]{:S(2)}, u32[]{:S(2)}) collective-permute-start(f32[256]{0:T(256)S(1)} %copy.43), channel_id=1, source_target_pairs={{0,1},{1,2},{2,3},{3,4},{4,5},{5,6},{6,7},{7,8},{8,9},{9,10},{10,1... | collective-permute-start | bytes 3080 | tf_op jit(solution)/shard_map/while/body/eval_jaxpr/ppermute | solution.py:11
  294.5 19.4 %collective-permute-start.1 = (f32[256,768]{1,0:T(8,128)S(1)}, f32[256,768]{1,0:T(8,128)S(1)}, u32[]{:S(2)}, u32[]{:S(2)}) collective-permute-start(f32[256,768]{1,0:T(8,128)S(1)} %convolution_add_fusion.4), channel_id=1, source_target_pairs={{0,1},{1,2},{2,3},{3,4},{4,5},{5,6},{6,7},{7,8},{8,9},{9,10},{10,1... | collective-permute-start | bytes 2359304 | tf_op jit(solution)/shard_map/while/body/eval_jaxpr/ppermute | solution.py:11
  296.9 17.0 %collective-permute-start = (bf16[256,768]{1,0:T(8,128)(2,1)S(1)}, bf16[256,768]{1,0:T(8,128)(2,1)S(1)}, u32[]{:S(2)}, u32[]{:S(2)}) collective-permute-start(bf16[256,768]{1,0:T(8,128)(2,1)S(1)} %copy.41), channel_id=1, source_target_pairs={{0,1},{1,2},{2,3},{3,4},{4,5},{5,6},{6,7},{7,8},{8,9},{9,10},{10,1... | collective-permute-start | bytes 1179656 | tf_op jit(solution)/shard_map/while/body/eval_jaxpr/ppermute | solution.py:11
  301.4 12.5 %collective-permute-start.2 = (f32[256]{0:T(256)S(1)}, f32[256]{0:T(256)S(1)}, u32[]{:S(2)}, u32[]{:S(2)}) collective-permute-start(f32[256]{0:T(256)S(1)} %copy.43), channel_id=1, source_target_pairs={{0,1},{1,2},{2,3},{3,4},{4,5},{5,6},{6,7},{7,8},{8,9},{9,10},{10,1... | collective-permute-start | bytes 3080 | tf_op jit(solution)/shard_map/while/body/eval_jaxpr/ppermute | solution.py:11
  318.0 19.4 %collective-permute-start.1 = (f32[256,768]{1,0:T(8,128)S(1)}, f32[256,768]{1,0:T(8,128)S(1)}, u32[]{:S(2)}, u32[]{:S(2)}) collective-permute-start(f32[256,768]{1,0:T(8,128)S(1)} %convolution_add_fusion.4), channel_id=1, source_target_pairs={{0,1},{1,2},{2,3},{3,4},{4,5},{5,6},{6,7},{7,8},{8,9},{9,10},{10,1... | collective-permute-start | bytes 2359304 | tf_op jit(solution)/shard_map/while/body/eval_jaxpr/ppermute | solution.py:11
  318.3 19.1 %collective-permute-start = (bf16[256,768]{1,0:T(8,128)(2,1)S(1)}, bf16[256,768]{1,0:T(8,128)(2,1)S(1)}, u32[]{:S(2)}, u32[]{:S(2)}) collective-permute-start(bf16[256,768]{1,0:T(8,128)(2,1)S(1)} %copy.41), channel_id=1, source_target_pairs={{0,1},{1,2},{2,3},{3,4},{4,5},{5,6},{6,7},{7,8},{8,9},{9,10},{10,1... | collective-permute-start | bytes 1179656 | tf_op jit(solution)/shard_map/while/body/eval_jaxpr/ppermute | solution.py:11
  323.7 13.7 %collective-permute-start.2 = (f32[256]{0:T(256)S(1)}, f32[256]{0:T(256)S(1)}, u32[]{:S(2)}, u32[]{:S(2)}) collective-permute-start(f32[256]{0:T(256)S(1)} %copy.43), channel_id=1, source_target_pairs={{0,1},{1,2},{2,3},{3,4},{4,5},{5,6},{6,7},{7,8},{8,9},{9,10},{10,1... | collective-permute-start | bytes 3080 | tf_op jit(solution)/shard_map/while/body/eval_jaxpr/ppermute | solution.py:11
  341.5 19.4 %collective-permute-start.1 = (f32[256,768]{1,0:T(8,128)S(1)}, f32[256,768]{1,0:T(8,128)S(1)}, u32[]{:S(2)}, u32[]{:S(2)}) collective-permute-start(f32[256,768]{1,0:T(8,128)S(1)} %convolution_add_fusion.4), channel_id=1, source_target_pairs={{0,1},{1,2},{2,3},{3,4},{4,5},{5,6},{6,7},{7,8},{8,9},{9,10},{10,1... | collective-permute-start | bytes 2359304 | tf_op jit(solution)/shard_map/while/body/eval_jaxpr/ppermute | solution.py:11
  341.6 19.3 %collective-permute-start = (bf16[256,768]{1,0:T(8,128)(2,1)S(1)}, bf16[256,768]{1,0:T(8,128)(2,1)S(1)}, u32[]{:S(2)}, u32[]{:S(2)}) collective-permute-start(bf16[256,768]{1,0:T(8,128)(2,1)S(1)} %copy.41), channel_id=1, source_target_pairs={{0,1},{1,2},{2,3},{3,4},{4,5},{5,6},{6,7},{7,8},{8,9},{9,10},{10,1... | collective-permute-start | bytes 1179656 | tf_op jit(solution)/shard_map/while/body/eval_jaxpr/ppermute | solution.py:11
  346.0 14.9 %collective-permute-start.2 = (f32[256]{0:T(256)S(1)}, f32[256]{0:T(256)S(1)}, u32[]{:S(2)}, u32[]{:S(2)}) collective-permute-start(f32[256]{0:T(256)S(1)} %copy.43), channel_id=1, source_target_pairs={{0,1},{1,2},{2,3},{3,4},{4,5},{5,6},{6,7},{7,8},{8,9},{9,10},{10,1... | collective-permute-start | bytes 3080 | tf_op jit(solution)/shard_map/while/body/eval_jaxpr/ppermute | solution.py:11
  365.0 19.4 %collective-permute-start.1 = (f32[256,768]{1,0:T(8,128)S(1)}, f32[256,768]{1,0:T(8,128)S(1)}, u32[]{:S(2)}, u32[]{:S(2)}) collective-permute-start(f32[256,768]{1,0:T(8,128)S(1)} %convolution_add_fusion.4), channel_id=1, source_target_pairs={{0,1},{1,2},{2,3},{3,4},{4,5},{5,6},{6,7},{7,8},{8,9},{9,10},{10,1... | collective-permute-start | bytes 2359304 | tf_op jit(solution)/shard_map/while/body/eval_jaxpr/ppermute | solution.py:11
  365.1 19.3 %collective-permute-start = (bf16[256,768]{1,0:T(8,128)(2,1)S(1)}, bf16[256,768]{1,0:T(8,128)(2,1)S(1)}, u32[]{:S(2)}, u32[]{:S(2)}) collective-permute-start(bf16[256,768]{1,0:T(8,128)(2,1)S(1)} %copy.41), channel_id=1, source_target_pairs={{0,1},{1,2},{2,3},{3,4},{4,5},{5,6},{6,7},{7,8},{8,9},{9,10},{10,1... | collective-permute-start | bytes 1179656 | tf_op jit(solution)/shard_map/while/body/eval_jaxpr/ppermute | solution.py:11
  368.3 16.1 %collective-permute-start.2 = (f32[256]{0:T(256)S(1)}, f32[256]{0:T(256)S(1)}, u32[]{:S(2)}, u32[]{:S(2)}) collective-permute-start(f32[256]{0:T(256)S(1)} %copy.43), channel_id=1, source_target_pairs={{0,1},{1,2},{2,3},{3,4},{4,5},{5,6},{6,7},{7,8},{8,9},{9,10},{10,1... | collective-permute-start | bytes 3080 | tf_op jit(solution)/shard_map/while/body/eval_jaxpr/ppermute | solution.py:11
  388.5 19.4 %collective-permute-start.1 = (f32[256,768]{1,0:T(8,128)S(1)}, f32[256,768]{1,0:T(8,128)S(1)}, u32[]{:S(2)}, u32[]{:S(2)}) collective-permute-start(f32[256,768]{1,0:T(8,128)S(1)} %convolution_add_fusion.4), channel_id=1, source_target_pairs={{0,1},{1,2},{2,3},{3,4},{4,5},{5,6},{6,7},{7,8},{8,9},{9,10},{10,1... | collective-permute-start | bytes 2359304 | tf_op jit(solution)/shard_map/while/body/eval_jaxpr/ppermute | solution.py:11
  388.6 19.3 %collective-permute-start = (bf16[256,768]{1,0:T(8,128)(2,1)S(1)}, bf16[256,768]{1,0:T(8,128)(2,1)S(1)}, u32[]{:S(2)}, u32[]{:S(2)}) collective-permute-start(bf16[256,768]{1,0:T(8,128)(2,1)S(1)} %copy.41), channel_id=1, source_target_pairs={{0,1},{1,2},{2,3},{3,4},{4,5},{5,6},{6,7},{7,8},{8,9},{9,10},{10,1... | collective-permute-start | bytes 1179656 | tf_op jit(solution)/shard_map/while/body/eval_jaxpr/ppermute | solution.py:11
  390.6 17.3 %collective-permute-start.2 = (f32[256]{0:T(256)S(1)}, f32[256]{0:T(256)S(1)}, u32[]{:S(2)}, u32[]{:S(2)}) collective-permute-start(f32[256]{0:T(256)S(1)} %copy.43), channel_id=1, source_target_pairs={{0,1},{1,2},{2,3},{3,4},{4,5},{5,6},{6,7},{7,8},{8,9},{9,10},{10,1... | collective-permute-start | bytes 3080 | tf_op jit(solution)/shard_map/while/body/eval_jaxpr/ppermute | solution.py:11
  412.1 19.4 %collective-permute-start.1 = (f32[256,768]{1,0:T(8,128)S(1)}, f32[256,768]{1,0:T(8,128)S(1)}, u32[]{:S(2)}, u32[]{:S(2)}) collective-permute-start(f32[256,768]{1,0:T(8,128)S(1)} %convolution_add_fusion.4), channel_id=1, source_target_pairs={{0,1},{1,2},{2,3},{3,4},{4,5},{5,6},{6,7},{7,8},{8,9},{9,10},{10,1... | collective-permute-start | bytes 2359304 | tf_op jit(solution)/shard_map/while/body/eval_jaxpr/ppermute | solution.py:11
  412.1 19.3 %collective-permute-start = (bf16[256,768]{1,0:T(8,128)(2,1)S(1)}, bf16[256,768]{1,0:T(8,128)(2,1)S(1)}, u32[]{:S(2)}, u32[]{:S(2)}) collective-permute-start(bf16[256,768]{1,0:T(8,128)(2,1)S(1)} %copy.41), channel_id=1, source_target_pairs={{0,1},{1,2},{2,3},{3,4},{4,5},{5,6},{6,7},{7,8},{8,9},{9,10},{10,1... | collective-permute-start | bytes 1179656 | tf_op jit(solution)/shard_map/while/body/eval_jaxpr/ppermute | solution.py:11
  412.9 18.6 %collective-permute-start.2 = (f32[256]{0:T(256)S(1)}, f32[256]{0:T(256)S(1)}, u32[]{:S(2)}, u32[]{:S(2)}) collective-permute-start(f32[256]{0:T(256)S(1)} %copy.43), channel_id=1, source_target_pairs={{0,1},{1,2},{2,3},{3,4},{4,5},{5,6},{6,7},{7,8},{8,9},{9,10},{10,1... | collective-permute-start | bytes 3080 | tf_op jit(solution)/shard_map/while/body/eval_jaxpr/ppermute | solution.py:11
  435.6 19.4 %collective-permute-start.1 = (f32[256,768]{1,0:T(8,128)S(1)}, f32[256,768]{1,0:T(8,128)S(1)}, u32[]{:S(2)}, u32[]{:S(2)}) collective-permute-start(f32[256,768]{1,0:T(8,128)S(1)} %convolution_add_fusion.4), channel_id=1, source_target_pairs={{0,1},{1,2},{2,3},{3,4},{4,5},{5,6},{6,7},{7,8},{8,9},{9,10},{10,1... | collective-permute-start | bytes 2359304 | tf_op jit(solution)/shard_map/while/body/eval_jaxpr/ppermute | solution.py:11
  435.7 19.3 %collective-permute-start = (bf16[256,768]{1,0:T(8,128)(2,1)S(1)}, bf16[256,768]{1,0:T(8,128)(2,1)S(1)}, u32[]{:S(2)}, u32[]{:S(2)}) collective-permute-start(bf16[256,768]{1,0:T(8,128)(2,1)S(1)} %copy.41), channel_id=1, source_target_pairs={{0,1},{1,2},{2,3},{3,4},{4,5},{5,6},{6,7},{7,8},{8,9},{9,10},{10,1... | collective-permute-start | bytes 1179656 | tf_op jit(solution)/shard_map/while/body/eval_jaxpr/ppermute | solution.py:11
  435.8 19.2 %collective-permute-start.2 = (f32[256]{0:T(256)S(1)}, f32[256]{0:T(256)S(1)}, u32[]{:S(2)}, u32[]{:S(2)}) collective-permute-start(f32[256]{0:T(256)S(1)} %copy.43), channel_id=1, source_target_pairs={{0,1},{1,2},{2,3},{3,4},{4,5},{5,6},{6,7},{7,8},{8,9},{9,10},{10,1... | collective-permute-start | bytes 3080 | tf_op jit(solution)/shard_map/while/body/eval_jaxpr/ppermute | solution.py:11
  459.1 19.4 %collective-permute-start.1 = (f32[256,768]{1,0:T(8,128)S(1)}, f32[256,768]{1,0:T(8,128)S(1)}, u32[]{:S(2)}, u32[]{:S(2)}) collective-permute-start(f32[256,768]{1,0:T(8,128)S(1)} %convolution_add_fusion.4), channel_id=1, source_target_pairs={{0,1},{1,2},{2,3},{3,4},{4,5},{5,6},{6,7},{7,8},{8,9},{9,10},{10,1... | collective-permute-start | bytes 2359304 | tf_op jit(solution)/shard_map/while/body/eval_jaxpr/ppermute | solution.py:11
  459.2 19.3 %collective-permute-start = (bf16[256,768]{1,0:T(8,128)(2,1)S(1)}, bf16[256,768]{1,0:T(8,128)(2,1)S(1)}, u32[]{:S(2)}, u32[]{:S(2)}) collective-permute-start(bf16[256,768]{1,0:T(8,128)(2,1)S(1)} %copy.41), channel_id=1, source_target_pairs={{0,1},{1,2},{2,3},{3,4},{4,5},{5,6},{6,7},{7,8},{8,9},{9,10},{10,1... | collective-permute-start | bytes 1179656 | tf_op jit(solution)/shard_map/while/body/eval_jaxpr/ppermute | solution.py:11
  459.3 19.2 %collective-permute-start.2 = (f32[256]{0:T(256)S(1)}, f32[256]{0:T(256)S(1)}, u32[]{:S(2)}, u32[]{:S(2)}) collective-permute-start(f32[256]{0:T(256)S(1)} %copy.43), channel_id=1, source_target_pairs={{0,1},{1,2},{2,3},{3,4},{4,5},{5,6},{6,7},{7,8},{8,9},{9,10},{10,1... | collective-permute-start | bytes 3080 | tf_op jit(solution)/shard_map/while/body/eval_jaxpr/ppermute | solution.py:11
  482.6 19.4 %collective-permute-start.1 = (f32[256,768]{1,0:T(8,128)S(1)}, f32[256,768]{1,0:T(8,128)S(1)}, u32[]{:S(2)}, u32[]{:S(2)}) collective-permute-start(f32[256,768]{1,0:T(8,128)S(1)} %convolution_add_fusion.4), channel_id=1, source_target_pairs={{0,1},{1,2},{2,3},{3,4},{4,5},{5,6},{6,7},{7,8},{8,9},{9,10},{10,1... | collective-permute-start | bytes 2359304 | tf_op jit(solution)/shard_map/while/body/eval_jaxpr/ppermute | solution.py:11
  482.7 19.3 %collective-permute-start = (bf16[256,768]{1,0:T(8,128)(2,1)S(1)}, bf16[256,768]{1,0:T(8,128)(2,1)S(1)}, u32[]{:S(2)}, u32[]{:S(2)}) collective-permute-start(bf16[256,768]{1,0:T(8,128)(2,1)S(1)} %copy.41), channel_id=1, source_target_pairs={{0,1},{1,2},{2,3},{3,4},{4,5},{5,6},{6,7},{7,8},{8,9},{9,10},{10,1... | collective-permute-start | bytes 1179656 | tf_op jit(solution)/shard_map/while/body/eval_jaxpr/ppermute | solution.py:11
  482.8 19.2 %collective-permute-start.2 = (f32[256]{0:T(256)S(1)}, f32[256]{0:T(256)S(1)}, u32[]{:S(2)}, u32[]{:S(2)}) collective-permute-start(f32[256]{0:T(256)S(1)} %copy.43), channel_id=1, source_target_pairs={{0,1},{1,2},{2,3},{3,4},{4,5},{5,6},{6,7},{7,8},{8,9},{9,10},{10,1... | collective-permute-start | bytes 3080 | tf_op jit(solution)/shard_map/while/body/eval_jaxpr/ppermute | solution.py:11
Sparse Core Ops, SparseCore 0:
  11.3 73.5 all-gather.1
where the time goes:
time: 614 us; the launch traced here: 612 us
  waiting for transfers between devices  228 us (37%)
  starting transfers between devices  135 us (22%)
  blocking collectives  91.7 us (15%)
  matrix products  84.2 us (14%)
  between operations  20.2 us (3%)
  loops' own time  18.1 us (3%)
  local copies, waits for them, and re-layouts  17.8 us (3%)
  other arithmetic  16.2 us (3%)
    ppermute x48, waiting for transfers between devices, passed_along(): lax.ppermute(value, axis, [(i, (i + by) % peers) for i in range(peers)])  147 us
    ppermute x48, starting transfers between devices, passed_along(): lax.ppermute(value, axis, [(i, (i + by) % peers) for i in range(peers)])  128 us
    psum x1, blocking collectives, shards(): loss_sum, slope_sum = lax.psum((loss_part, slope), ('dp', 'blk'))  91.7 us
    all_gather x1, waiting for transfers between devices, shards(): lax.all_gather(txt_unit, 'blk', axis=0, tiled=True)  67.6 us
    dot_general x16, matrix products, tile_weight(): jnp.einsum('rd,cd->rc', left, right, preferred_element_type=jnp.float32)  42.6 us
    dot_general x16, matrix products, cycle_turn(): jnp.einsum('rc,rd->cd', weight_bf, img_unit, preferred_element_type=jnp.f...  22.7 us
  transfers between devices with their start and end apart: 51, of which 19 were waited for; matrix products, arithmetic and copies ran while one was open for 2% of the time, Pallas kernels for 0%

commit v1 on v0

v1 whole, which is shorter than its diff:
```python
import functools

import jax
import jax.numpy as jnp
from jax import lax
from jax.experimental import pallas as pl
from jax.experimental.pallas import tpu as pltpu
from jax.sharding import PartitionSpec as P

EPSILON = 1e-06
PART = jnp.float32
VMEM = pl.BlockSpec(memory_space=pltpu.VMEM)
SMEM = pl.BlockSpec(memory_space=pltpu.SMEM)
PARAMS = pltpu.CompilerParams(vmem_limit_bytes=40 * 1024 * 1024)
SLOTS = 4


def swapped(value, axis, bits):
    return lax.ppermute(value, axis, [(i, i ^ bits) for i in range(lax.axis_size(axis))])


def eye(n):
    return lax.broadcasted_iota(jnp.int32, (n, n), 0) == lax.broadcasted_iota(jnp.int32, (n, n), 1)


def to_row(column, diagonal):
    return jnp.sum(jnp.where(diagonal, column, 0.0), axis=0, keepdims=True)


def to_column(row, diagonal):
    return jnp.sum(jnp.where(diagonal, row, 0.0), axis=1, keepdims=True)


def unit_rows(values):
    wide = values.astype(jnp.float32)
    inverse = lax.rsqrt(jnp.sum(wide * wide, axis=-1, keepdims=True) + EPSILON)
    return wide * inverse, inverse


def scores(scale, left, right):
    return scale * lax.dot_general(
        left, right, (((1,), (1,)), ((), ())), preferred_element_type=jnp.float32
    )


def unit_kernel(image, text, img_unit, txt_unit):
    img_unit[...] = unit_rows(image[...])[0].astype(jnp.bfloat16)
    txt_unit[...] = unit_rows(text[...])[0].astype(jnp.bfloat16)


def stats_kernel(scale, *refs):
    imgs, txts = refs[:SLOTS], refs[SLOTS : 2 * SLOTS]
    row_part, col_part, logits = refs[2 * SLOTS :]
    rows = imgs[0].shape[0]
    diagonal = eye(rows)
    span = lambda k: pl.ds(k * rows, rows)
    row_top, col_top = [None] * SLOTS, [None] * SLOTS
    for k in range(SLOTS):
        for l in range(SLOTS):
            tile = scores(scale[0], imgs[k][...], txts[l][...])
            logits[span(k), span(l)] = tile
            right = jnp.max(tile, axis=1, keepdims=True)
            down = jnp.max(tile, axis=0, keepdims=True)
            row_top[k] = right if l == 0 else jnp.maximum(row_top[k], right)
            col_top[l] = down if k == 0 else jnp.maximum(col_top[l], down)
    col_sum = [jnp.zeros((1, rows), jnp.float32)] * SLOTS
    for k in range(SLOTS):
        row_sum = jnp.zeros((rows, 1), jnp.float32)
        for l in range(SLOTS):
            tile = logits[span(k), span(l)]
            row_sum += jnp.sum(jnp.exp(tile - row_top[k]), axis=1, keepdims=True)
            col_sum[l] += jnp.sum(jnp.exp(tile - col_top[l]), axis=0, keepdims=True)
        row_part[pl.ds(k, 1), :] = to_row(row_top[k], diagonal) + jnp.log(to_row(row_sum, diagonal))
    for l in range(SLOTS):
        col_part[pl.ds(l, 1), :] = col_top[l] + jnp.log(col_sum[l])


def joined(parts):
    top = functools.reduce(jnp.maximum, parts)
    return top + jnp.log(sum(jnp.exp(part - top) for part in parts))


def back_kernel(scale, *refs):
    imgs, txts = refs[:SLOTS], refs[SLOTS : 2 * SLOTS]
    row_parts, col_parts = refs[2 * SLOTS : 3 * SLOTS], refs[3 * SLOTS : 4 * SLOTS]
    positive = refs[4 * SLOTS]
    outs = refs[4 * SLOTS + 1 :]
    img_back, txt_back, sums = outs[:SLOTS], outs[SLOTS : 2 * SLOTS], outs[2 * SLOTS]
    rows = imgs[0].shape[0]
    diagonal = eye(rows)
    lse = lambda parts, k: joined([parts[m][pl.ds(k ^ m, 1), :] for m in range(SLOTS)])
    row_lse = [lse(row_parts, k) for k in range(SLOTS)]
    col_lse = [lse(col_parts, l) for l in range(SLOTS)]
    target = to_column(positive[...].astype(jnp.float32), diagonal).astype(jnp.int32)
    hit = lax.broadcasted_iota(jnp.int32, (rows, rows), 1) == target
    slope = jnp.zeros((1, 1), jnp.float32)
    txt_sum = [None] * SLOTS
    for k in (1, 2, 3, 0):
        img_sum = None
        right = to_column(row_lse[k], diagonal)
        for l in range(SLOTS):
            tile = scores(scale[0], imgs[k][...], txts[l][...])
            weight = 0.5 * (jnp.exp(tile - right) + jnp.exp(tile - col_lse[l]))
            if k == 0 and l == 0:
                weight = weight - hit.astype(jnp.float32)
                matched = jnp.sum(jnp.where(hit, tile, 0.0), keepdims=True)
            slope += jnp.sum(weight * tile, keepdims=True)
            narrow = weight.astype(jnp.bfloat16)
            img_term = jnp.dot(narrow, txts[l][...], preferred_element_type=jnp.float32)
            txt_term = lax.dot_general(
                narrow, imgs[k][...], (((0,), (0,)), ((), ())), preferred_element_type=jnp.float32
            )
            img_sum = img_term if l == 0 else img_sum + img_term
            if k == 1:
                txt_back_acc = txt_term
            else:
                txt_back_acc = txt_sum[l][...] + txt_term
            if k == 0:
                txt_back[l][...] = txt_back_acc.astype(txt_back[l].dtype)
            else:
                refs[-1][l] = txt_back_acc
                txt_sum[l] = refs[-1].at[l]
        img_back[k][...] = img_sum.astype(img_back[k].dtype)
    loss = 0.5 * (
        jnp.sum(row_lse[0], keepdims=True) + jnp.sum(col_lse[0], keepdims=True)
    ) - matched
    lane = lax.broadcasted_iota(jnp.int32, sums.shape, 1)
    sums[...] = jnp.where(lane == 0, loss, jnp.where(lane == 1, slope, 0.0))


def grad_kernel(scale, image, text, *refs):
    img_parts, txt_parts = refs[:SLOTS], refs[SLOTS : 2 * SLOTS]
    for values, parts, out in zip((image, text), (img_parts, txt_parts), refs[2 * SLOTS :]):
        direction, inverse = unit_rows(values[...])
        incoming = scale[0] * sum(part[...].astype(jnp.float32) for part in parts)
        along = jnp.sum(direction * incoming, axis=-1, keepdims=True)
        out[...] = ((incoming - direction * along) * inverse).astype(out.dtype)


def shards(image, text, positive, logit_scale):
    rows, width = image.shape
    shape = jax.ShapeDtypeStruct
    block = shape((rows, width), jnp.bfloat16)
    img_unit, txt_unit = pl.pallas_call(
        unit_kernel, out_shape=[block] * 2, in_specs=[VMEM] * 2, out_specs=[VMEM] * 2,
        compiler_params=PARAMS, name="unit",
    )(image, text)
    along_x = [m << 2 for m in range(SLOTS)]
    along_y = list(range(SLOTS))
    spread = lambda value, bits: [value] + [swapped(value, "blk", b) for b in bits[1:]]
    imgs = spread(img_unit, along_x)
    txts = spread(txt_unit, along_y)
    part = shape((SLOTS, rows), jnp.float32)
    row_part, col_part = pl.pallas_call(
        stats_kernel, out_shape=[part] * 2,
        in_specs=[SMEM] + [VMEM] * (2 * SLOTS), out_specs=[VMEM] * 2,
        scratch_shapes=[pltpu.VMEM((SLOTS * rows, SLOTS * rows), jnp.float32)],
        compiler_params=PARAMS, name="stats",
    )(logit_scale, *imgs, *txts)
    row_parts = spread(row_part, along_x)
    col_parts = spread(col_part, along_y)
    wide = shape((rows, width), jnp.float32)
    sent = shape((rows, width), PART)
    outs = pl.pallas_call(
        back_kernel,
        out_shape=([wide] + [sent] * (SLOTS - 1)) * 2 + [shape((8, 128), jnp.float32)],
        in_specs=[SMEM] + [VMEM] * (4 * SLOTS + 1), out_specs=[VMEM] * (2 * SLOTS + 1),
        scratch_shapes=[pltpu.VMEM((SLOTS, rows, width), jnp.float32)],
        compiler_params=PARAMS, name="back",
    )(logit_scale, *imgs, *txts, *row_parts, *col_parts, positive.reshape(1, rows))
    img_back, txt_back, sums = outs[:SLOTS], outs[SLOTS : 2 * SLOTS], outs[2 * SLOTS]
    collect = lambda parts, bits: [parts[0]] + [
        swapped(p, "blk", b) for p, b in zip(parts[1:], bits[1:])
    ]
    img_parts = collect(img_back, along_x)
    txt_parts = collect(txt_back, along_y)
    for axis in ("blk", "dp"):
        step = 1
        while step < lax.axis_size(axis):
            sums = sums + swapped(sums, axis, step)
            step *= 2
    image_grad, text_grad = pl.pallas_call(
        grad_kernel, out_shape=[block] * 2,
        in_specs=[SMEM] + [VMEM] * (2 + 2 * SLOTS), out_specs=[VMEM] * 2,
        compiler_params=PARAMS, name="grad",
    )(logit_scale, image, text, *img_parts, *txt_parts)
    total_rows = rows * lax.axis_size("blk") * lax.axis_size("dp")
    loss = sums[0, :1] / total_rows
    scale_grad = sums[0, 1:2] / (total_rows * logit_scale)
    return (loss, scale_grad, image_grad, text_grad)


def solution(mesh):
    in_specs = (P(("dp", "blk"), None), P(("dp", "blk"), None), P(("dp", "blk")), P())
    out_specs = (P(), P(), P(("dp", "blk"), None), P(("dp", "blk"), None))
    return jax.shard_map(shards, mesh=mesh, in_specs=in_specs, out_specs=out_specs, check_vma=False)
```

time: 614 us -> 140 us (0.23)
  waiting for transfers between devices: 228 us -> 62 us
  blocking collectives: 91.7 us -> 0 us
  matrix products: 84.2 us -> 0 us
  starting transfers between devices: 135 us -> 58.1 us
  loops' own time: 18.1 us -> 0 us
  other arithmetic: 16.2 us -> 0.03 us
  between operations: 20.2 us -> 4.93 us
  local copies, waits for them, and re-layouts: 17.8 us -> 2.59 us
  Pallas kernels: 0 us -> 12.6 us
    psum x1 -> x0, blocking collectives: 91.7 us -> none  [shards(): loss_sum, slope_sum = lax.psum((loss_part, slope), ('dp', 'blk'))]
    ppermute x48 -> x26, waiting for transfers between devices: 147 us -> 62 us  [swapped(): lax.ppermute(value, axis, [(i, i ^ bits) for i in range(lax.axis_size(axi...]
    dot_general x52 -> x0, matrix products: 84.2 us -> none  [the longest x16 42.6 us: tile_weight(): jnp.einsum('rd,cd->rc', left, right, preferred_element_type=jnp.float32)]
    ppermute x48 -> x26, starting transfers between devices: 128 us -> 58.1 us  [swapped(): lax.ppermute(value, axis, [(i, i ^ bits) for i in range(lax.axis_size(axi...]
    all_gather x1 -> x0, waiting for transfers between devices: 67.6 us -> none  [shards(): lax.all_gather(txt_unit, 'blk', axis=0, tiled=True)]
    another operation x2 -> x0, loops' own time: 18.1 us -> none  [the longest x1 11.1 us: shards(): lax.fori_loop(0, blocks, cycle_turn, cycle_state)]
    all_to_all x2 -> x0, waiting for transfers between devices: 13.3 us -> none  [the longest x1 6.71 us: shards(): lax.all_to_all(col_total.reshape(blocks, rows), 'blk', split_axis=0, conc...]
    pallas_call x0 -> x4, Pallas kernels: none -> 12.6 us  [the longest x1 8.02 us: shards(): pl.pallas_call(back_kernel, out_shape=([wide] + [sent] * (SLOTS - 1)) * 2...]
  transfers between devices with their start and end apart: 51 -> 26, of which waited for: 19 -> 14; matrix products, arithmetic and copies ran while one was open for 2% -> 0% of each run, Pallas kernels for 0% -> 0%
where the time goes in v1:
time: 140 us
  waiting for transfers between devices  62 us (44%)
  starting transfers between devices  58.1 us (42%)
  Pallas kernels  12.6 us (9%)
  between operations  4.93 us (4%)
  local copies, waits for them, and re-layouts  2.59 us (2%)
    ppermute x26, waiting for transfers between devices, swapped(): lax.ppermute(value, axis, [(i, i ^ bits) for i in range(lax.axis_size(axi...  62 us
    ppermute x26, starting transfers between devices, swapped(): lax.ppermute(value, axis, [(i, i ^ bits) for i in range(lax.axis_size(axi...  58.1 us
    pallas_call x1, Pallas kernels, shards(): pl.pallas_call(back_kernel, out_shape=([wide] + [sent] * (SLOTS - 1)) * 2...  8.02 us
  transfers between devices with their start and end apart: 26, of which 14 were waited for; matrix products, arithmetic and copies ran while one was open for 0% of the time, Pallas kernels for 0%

profile of v1, /device:TPU:1, one launch (start us, length us, event | category | flops | bytes accessed | tf_op | source)
XLA Modules:
  0.0 140.2 jit_solution(6410948223449552286)
XLA Ops:
  0.6 0.0 copy-start
  0.6 1.0 copy-done
  1.6 1.0 copy-done.2
  2.6 0.2 unit.1
  2.9 2.1 %collective-permute-start = (bf16[256,768]{1,0:T(8,128)(2,1)S(1)}, bf16[256,768]{1,0:T(8,128)(2,1)S(1)}, u32[]{:S(2)}, u32[]{:S(2)}) collective-permute-start(bf16[256,768]{1,0:T(8,128)(2,1)S(1)} %get-tuple-element.19.refs_0_), channel_id=1, source_target_pairs={{0,4},{1,5},{2,6},{3,7},{4,0},{5,1},{6,2},{7,3},{8,12},{9,13},{10,... | collective-permute-start | bytes 1179656 | tf_op jit(solution)/shard_map/ppermute | solution.py:19
  5.0 2.5 %collective-permute-start.1 = (bf16[256,768]{1,0:T(8,128)(2,1)S(1)}, bf16[256,768]{1,0:T(8,128)(2,1)S(1)}, u32[]{:S(2)}, u32[]{:S(2)}) collective-permute-start(bf16[256,768]{1,0:T(8,128)(2,1)S(1)} %get-tuple-element.19.refs_0_), channel_id=1, source_target_pairs={{0,8},{1,9},{2,10},{3,11},{4,12},{5,13},{6,14},{7,15},{8,0},{9,1},... | collective-permute-start | bytes 1179656 | tf_op jit(solution)/shard_map/ppermute | solution.py:19
  7.4 0.0 collective-permute-start.2
  7.5 3.4 %collective-permute-start.3 = (bf16[256,768]{1,0:T(8,128)(2,1)S(1)}, bf16[256,768]{1,0:T(8,128)(2,1)S(1)}, u32[]{:S(2)}, u32[]{:S(2)}) collective-permute-start(bf16[256,768]{1,0:T(8,128)(2,1)S(1)} %get-tuple-element.20.refs_4_), channel_id=1, source_target_pairs={{0,1},{1,0},{2,3},{3,2},{4,5},{5,4},{6,7},{7,6},{8,9},{9,8},{10,11... | collective-permute-start | bytes 1179656 | tf_op jit(solution)/shard_map/ppermute | solution.py:19
  10.9 1.2 collective-permute-start.4
  12.1 0.4 collective-permute-done.refs_1_
  12.5 6.8 %collective-permute-start.5 = (bf16[256,768]{1,0:T(8,128)(2,1)S(1)}, bf16[256,768]{1,0:T(8,128)(2,1)S(1)}, u32[]{:S(2)}, u32[]{:S(2)}) collective-permute-start(bf16[256,768]{1,0:T(8,128)(2,1)S(1)} %get-tuple-element.20.refs_4_), channel_id=1, source_target_pairs={{0,3},{1,2},{2,1},{3,0},{4,7},{5,6},{6,5},{7,4},{8,11},{9,10},{10,... | collective-permute-start | bytes 1179656 | tf_op jit(solution)/shard_map/ppermute | solution.py:19
  19.9 4.5 %collective-permute-done.1.refs_2_ = bf16[256,768]{1,0:T(8,128)(2,1)S(1)} collective-permute-done((bf16[256,768]{1,0:T(8,128)(2,1)S(1)}, bf16[256,768]{1,0:T(8,128)(2,1)S(1)}, u32[]{:S(2)}, u32[]{:S(2)}) %collective-permute-start.1) | collective-permute-done | bytes 393248 | tf_op jit(solution)/shard_map/ppermute | solution.py:19
  24.4 2.0 %collective-permute-done.2.refs_3_ = bf16[256,768]{1,0:T(8,128)(2,1)S(1)} collective-permute-done((bf16[256,768]{1,0:T(8,128)(2,1)S(1)}, bf16[256,768]{1,0:T(8,128)(2,1)S(1)}, u32[]{:S(2)}, u32[]{:S(2)}) %collective-permute-start.2) | collective-permute-done | bytes 393248 | tf_op jit(solution)/shard_map/ppermute | solution.py:19
  26.5 0.0 collective-permute-done.3.refs_5_
  26.5 0.0 collective-permute-done.4.refs_6_
  26.5 5.2 %collective-permute-done.5.refs_7_ = bf16[256,768]{1,0:T(8,128)(2,1)S(1)} collective-permute-done((bf16[256,768]{1,0:T(8,128)(2,1)S(1)}, bf16[256,768]{1,0:T(8,128)(2,1)S(1)}, u32[]{:S(2)}, u32[]{:S(2)}) %collective-permute-start.5) | collective-permute-done | bytes 393248 | tf_op jit(solution)/shard_map/ppermute | solution.py:19
  31.7 2.7 %stats.1 = (f32[4,256]{1,0:T(4,128)S(1)}, f32[4,256]{1,0:T(4,128)S(1)}) custom-call(f32[1]{0:T(128)S(6)} %copy.8.scale, bf16[256,768]{1,0:T(8,128)(2,1)S(1)} %get-tuple-element.19.refs_0_, bf16[256,768]{1,0:T(8,128)(2,1)S(1)} %collective-permute-done.refs_1_, bf16[256,768]{1,0:T(8,128)(2,1)S(1)} %collective-permute-done.1.refs_2_, ...), custom_call_target="tpu_custom_call" | custom-call | tf_op jit(solution)/shard_map/stats/pallas_call | solution.py:154
  34.4 1.3 collective-permute-start.10
  35.7 2.3 %collective-permute-start.11 = (f32[4,256]{1,0:T(4,128)S(1)}, f32[4,256]{1,0:T(4,128)S(1)}, u32[]{:S(2)}, u32[]{:S(2)}) collective-permute-start(f32[4,256]{1,0:T(4,128)S(1)} %get-tuple-element.22.refs_12_), channel_id=1, source_target_pairs={{0,3},{1,2},{2,1},{3,0},{4,7},{5,6},{6,5},{7,4},{8,11},{9,10},{10,... | collective-permute-start | bytes 12296 | tf_op jit(solution)/shard_map/ppermute | solution.py:19
  37.9 0.0 collective-permute-start.6
  37.9 1.9 %collective-permute-start.7 = (f32[4,256]{1,0:T(4,128)S(1)}, f32[4,256]{1,0:T(4,128)S(1)}, u32[]{:S(2)}, u32[]{:S(2)}) collective-permute-start(f32[4,256]{1,0:T(4,128)S(1)} %get-tuple-element.21.refs_8_), channel_id=1, source_target_pairs={{0,8},{1,9},{2,10},{3,11},{4,12},{5,13},{6,14},{7,15},{8,0},{9,1},... | collective-permute-start | bytes 12296 | tf_op jit(solution)/shard_map/ppermute | solution.py:19
  39.9 1.9 %collective-permute-start.8 = (f32[4,256]{1,0:T(4,128)S(1)}, f32[4,256]{1,0:T(4,128)S(1)}, u32[]{:S(2)}, u32[]{:S(2)}) collective-permute-start(f32[4,256]{1,0:T(4,128)S(1)} %get-tuple-element.21.refs_8_), channel_id=1, source_target_pairs={{0,12},{1,13},{2,14},{3,15},{4,8},{5,9},{6,10},{7,11},{8,4},{9,5},... | collective-permute-start | bytes 12296 | tf_op jit(solution)/shard_map/ppermute | solution.py:19
  41.8 0.0 collective-permute-done.10.refs_14_
  41.8 0.8 collective-permute-start.9
  42.6 0.0 collective-permute-done.11.refs_15_
  42.6 0.0 collective-permute-done.6.refs_9_
  42.6 0.0 collective-permute-done.7.refs_10_
  42.6 1.0 collective-permute-done.8.refs_11_
  43.5 0.0 collective-permute-done.9.refs_13_
  43.5 0.0 copy-done.4
  43.5 0.0 copy-start.3
  43.6 8.0 %back.1 = (f32[256,768]{1,0:T(8,128)S(1)}, f32[256,768]{1,0:T(8,128)S(1)}, f32[256,768]{1,0:T(8,128)S(1)}, f32[256,768]{1,0:T(8,128)S(1)}, f32[256,768]{1,0:T(8,...) custom-call(f32[1]{0:T(128)S(6)} %copy.8.scale, ...), custom_call_target="tpu_custom_call" | custom-call | tf_op jit(solution)/shard_map/back/pallas_call | solution.py:164
  51.6 0.1 collective-permute-start.20
  51.7 1.9 %collective-permute-start.12 = (f32[8,128]{1,0:T(8,128)S(1)}, f32[8,128]{1,0:T(8,128)S(1)}, u32[]{:S(2)}, u32[]{:S(2)}) collective-permute-start(f32[8,128]{1,0:T(8,128)S(1)} %get-tuple-element.23), channel_id=1, source_target_pairs={{0,1},{1,0},{2,3},{3,2},{4,5},{5,4},{6,7},{7,6},{8,9},{9,8},{10,11... | collective-permute-start | bytes 12296 | tf_op jit(solution)/shard_map/ppermute | solution.py:19
  53.5 0.8 collective-permute-done.12
  54.4 2.8 %collective-permute-start.13 = (f32[8,128]{1,0:T(8,128)S(1)}, f32[8,128]{1,0:T(8,128)S(1)}, u32[]{:S(2)}, u32[]{:S(2)}) collective-permute-start(f32[8,128]{1,0:T(8,128)S(1)} %add.24), channel_id=1, source_target_pairs={{0,2},{1,3},{2,0},{3,1},{4,6},{5,7},{6,4},{7,5},{8,10},{9,11},{10,... | collective-permute-start | bytes 12296 | tf_op jit(solution)/shard_map/ppermute | solution.py:19
  57.2 1.2 collective-permute-done.13
  58.3 1.6 %collective-permute-start.14 = (f32[8,128]{1,0:T(8,128)S(1)}, f32[8,128]{1,0:T(8,128)S(1)}, u32[]{:S(2)}, u32[]{:S(2)}) collective-permute-start(f32[8,128]{1,0:T(8,128)S(1)} %add.25), channel_id=1, source_target_pairs={{0,4},{1,5},{2,6},{3,7},{4,0},{5,1},{6,2},{7,3},{8,12},{9,13},{10,... | collective-permute-start | bytes 12296 | tf_op jit(solution)/shard_map/ppermute | solution.py:19
  60.0 9.0 %collective-permute-done.14 = f32[8,128]{1,0:T(8,128)S(1)} collective-permute-done((f32[8,128]{1,0:T(8,128)S(1)}, f32[8,128]{1,0:T(8,128)S(1)}, u32[]{:S(2)}, u32[]{:S(2)}) %collective-permute-start.14) | collective-permute-done | bytes 4128 | tf_op jit(solution)/shard_map/ppermute | solution.py:19
  69.0 2.1 %collective-permute-start.15 = (f32[8,128]{1,0:T(8,128)S(1)}, f32[8,128]{1,0:T(8,128)S(1)}, u32[]{:S(2)}, u32[]{:S(2)}) collective-permute-start(f32[8,128]{1,0:T(8,128)S(1)} %add.26), channel_id=1, source_target_pairs={{0,8},{1,9},{2,10},{3,11},{4,12},{5,13},{6,14},{7,15},{8,0},{9,1},... | collective-permute-start | bytes 12296 | tf_op jit(solution)/shard_map/ppermute | solution.py:19
  71.1 1.9 %collective-permute-done.15 = f32[8,128]{1,0:T(8,128)S(1)} collective-permute-done((f32[8,128]{1,0:T(8,128)S(1)}, f32[8,128]{1,0:T(8,128)S(1)}, u32[]{:S(2)}, u32[]{:S(2)}) %collective-permute-start.15) | collective-permute-done | bytes 4128 | tf_op jit(solution)/shard_map/ppermute | solution.py:19
  73.0 1.4 %collective-permute-start.16 = (f32[8,128]{1,0:T(8,128)S(1)}, f32[8,128]{1,0:T(8,128)S(1)}, u32[]{:S(2)}, u32[]{:S(2)}) collective-permute-start(f32[8,128]{1,0:T(8,128)S(1)} %add.27), channel_id=1, source_target_pairs={{0,16},{16,0},{32,48},{48,32},{64,80},{80,64},{96,112},{112,96},{1... | collective-permute-start | bytes 12296 | tf_op jit(solution)/shard_map/ppermute | solution.py:19
  74.4 1.3 collective-permute-done.16
  75.7 1.6 %collective-permute-start.17 = (f32[8,128]{1,0:T(8,128)S(1)}, f32[8,128]{1,0:T(8,128)S(1)}, u32[]{:S(2)}, u32[]{:S(2)}) collective-permute-start(f32[8,128]{1,0:T(8,128)S(1)} %add.28), channel_id=1, source_target_pairs={{0,32},{16,48},{32,0},{48,16},{64,96},{80,112},{96,64},{112,80},{1... | collective-permute-start | bytes 12296 | tf_op jit(solution)/shard_map/ppermute | solution.py:19
  77.4 1.0 collective-permute-done.17
  78.4 3.0 %collective-permute-start.18 = (f32[8,128]{1,0:T(8,128)S(1)}, f32[8,128]{1,0:T(8,128)S(1)}, u32[]{:S(2)}, u32[]{:S(2)}) collective-permute-start(f32[8,128]{1,0:T(8,128)S(1)} %add.29), channel_id=1, source_target_pairs={{0,64},{16,80},{32,96},{48,112},{64,0},{80,16},{96,32},{112,48},{1... | collective-permute-start | bytes 12296 | tf_op jit(solution)/shard_map/ppermute | solution.py:19
  81.4 1.0 collective-permute-done.18
  82.4 6.1 %collective-permute-start.19 = (f32[8,128]{1,0:T(8,128)S(1)}, f32[8,128]{1,0:T(8,128)S(1)}, u32[]{:S(2)}, u32[]{:S(2)}) collective-permute-start(f32[8,128]{1,0:T(8,128)S(1)} %add.30), channel_id=1, source_target_pairs={{0,128},{16,144},{32,160},{48,176},{64,192},{80,208},{96,224},{112... | collective-permute-start | bytes 12296 | tf_op jit(solution)/shard_map/ppermute | solution.py:19
  88.5 0.9 collective-permute-start.21
  89.3 1.8 %collective-permute-start.22 = (f32[256,768]{1,0:T(8,128)S(1)}, f32[256,768]{1,0:T(8,128)S(1)}, u32[]{:S(2)}, u32[]{:S(2)}) collective-permute-start(f32[256,768]{1,0:T(8,128)S(1)} %get-tuple-element.27), channel_id=1, source_target_pairs={{0,12},{1,13},{2,14},{3,15},{4,8},{5,9},{6,10},{7,11},{8,4},{9,5},... | collective-permute-start | bytes 2359304 | tf_op jit(solution)/shard_map/ppermute | solution.py:19
  91.1 7.6 %collective-permute-start.23 = (f32[256,768]{1,0:T(8,128)S(1)}, f32[256,768]{1,0:T(8,128)S(1)}, u32[]{:S(2)}, u32[]{:S(2)}) collective-permute-start(f32[256,768]{1,0:T(8,128)S(1)} %get-tuple-element.29), channel_id=1, source_target_pairs={{0,1},{1,0},{2,3},{3,2},{4,5},{5,4},{6,7},{7,6},{8,9},{9,8},{10,11... | collective-permute-start | bytes 2359304 | tf_op jit(solution)/shard_map/ppermute | solution.py:19
  98.7 0.0 collective-permute-done.19
  98.7 2.9 %collective-permute-start.24 = (f32[256,768]{1,0:T(8,128)S(1)}, f32[256,768]{1,0:T(8,128)S(1)}, u32[]{:S(2)}, u32[]{:S(2)}) collective-permute-start(f32[256,768]{1,0:T(8,128)S(1)} %get-tuple-element.30), channel_id=1, source_target_pairs={{0,2},{1,3},{2,0},{3,1},{4,6},{5,7},{6,4},{7,5},{8,10},{9,11},{10,... | collective-permute-start | bytes 2359304 | tf_op jit(solution)/shard_map/ppermute | solution.py:19
  101.6 0.0 collective-permute-done.20.refs_1_
  101.6 0.2 collective-permute-start.25
  101.9 0.6 fusion
  103.7 0.0 collective-permute-done.21.refs_2_
  103.8 22.5 %collective-permute-done.22.refs_3_ = f32[256,768]{1,0:T(8,128)S(1)} collective-permute-done((f32[256,768]{1,0:T(8,128)S(1)}, f32[256,768]{1,0:T(8,128)S(1)}, u32[]{:S(2)}, u32[]{:S(2)}) %collective-permute-start.22) | collective-permute-done | bytes 786464 | tf_op jit(solution)/shard_map/ppermute | solution.py:19
  126.3 0.0 collective-permute-done.23.refs_5_
  126.3 0.0 collective-permute-done.24.refs_6_
  126.3 10.0 %collective-permute-done.25.refs_7_ = f32[256,768]{1,0:T(8,128)S(1)} collective-permute-done((f32[256,768]{1,0:T(8,128)S(1)}, f32[256,768]{1,0:T(8,128)S(1)}, u32[]{:S(2)}, u32[]{:S(2)}) %collective-permute-start.25) | collective-permute-done | bytes 786464 | tf_op jit(solution)/shard_map/ppermute | solution.py:19
  136.3 0.0 copy-done.1
  136.3 0.0 copy-done.3
  136.3 1.6 %grad.1 = (bf16[256,768]{1,0:T(8,128)(2,1)}, bf16[256,768]{1,0:T(8,128)(2,1)}) custom-call(f32[1]{0:T(128)S(6)} %copy.8.scale, bf16[256,768]{1,0:T(8,128)(2,1)S(1)} %copy-done.1, bf16[256,768]{1,0:T(8,128)(2,1)S(1)} %copy-done.3, f32[256,768]{1,0:T(8,128)S(1)} %get-tuple-element.24.refs_0_, f32[256,768]{1,0:T(8,128)S(1)} %collective-permute-done.20.refs_1_, ...), custom_call_target="tpu_custom_call" | custom-call | tf_op jit(solution)/shard_map/grad/pallas_call | solution.py:182
  (11 shorter events, 0.0 us)
Async XLA Ops:
  0.6 1.0 copy-start
  1.6 1.0 copy-start.2
  2.9 9.6 %collective-permute-start = (bf16[256,768]{1,0:T(8,128)(2,1)S(1)}, bf16[256,768]{1,0:T(8,128)(2,1)S(1)}, u32[]{:S(2)}, u32[]{:S(2)}) collective-permute-start(bf16[256,768]{1,0:T(8,128)(2,1)S(1)} %get-tuple-element.19.refs_0_), channel_id=1, source_target_pairs={{0,4},{1,5},{2,6},{3,7},{4,0},{5,1},{6,2},{7,3},{8,12},{9,13},{10,... | collective-permute-start | bytes 1179656 | tf_op jit(solution)/shard_map/ppermute | solution.py:19
  5.0 19.4 %collective-permute-start.1 = (bf16[256,768]{1,0:T(8,128)(2,1)S(1)}, bf16[256,768]{1,0:T(8,128)(2,1)S(1)}, u32[]{:S(2)}, u32[]{:S(2)}) collective-permute-start(bf16[256,768]{1,0:T(8,128)(2,1)S(1)} %get-tuple-element.19.refs_0_), channel_id=1, source_target_pairs={{0,8},{1,9},{2,10},{3,11},{4,12},{5,13},{6,14},{7,15},{8,0},{9,1},... | collective-permute-start | bytes 1179656 | tf_op jit(solution)/shard_map/ppermute | solution.py:19
  7.4 19.0 %collective-permute-start.2 = (bf16[256,768]{1,0:T(8,128)(2,1)S(1)}, bf16[256,768]{1,0:T(8,128)(2,1)S(1)}, u32[]{:S(2)}, u32[]{:S(2)}) collective-permute-start(bf16[256,768]{1,0:T(8,128)(2,1)S(1)} %get-tuple-element.19.refs_0_), channel_id=1, source_target_pairs={{0,12},{1,13},{2,14},{3,15},{4,8},{5,9},{6,10},{7,11},{8,4},{9,5},... | collective-permute-start | bytes 1179656 | tf_op jit(solution)/shard_map/ppermute | solution.py:19
  7.5 19.0 %collective-permute-start.3 = (bf16[256,768]{1,0:T(8,128)(2,1)S(1)}, bf16[256,768]{1,0:T(8,128)(2,1)S(1)}, u32[]{:S(2)}, u32[]{:S(2)}) collective-permute-start(bf16[256,768]{1,0:T(8,128)(2,1)S(1)} %get-tuple-element.20.refs_4_), channel_id=1, source_target_pairs={{0,1},{1,0},{2,3},{3,2},{4,5},{5,4},{6,7},{7,6},{8,9},{9,8},{10,11... | collective-permute-start | bytes 1179656 | tf_op jit(solution)/shard_map/ppermute | solution.py:19
  10.9 15.6 %collective-permute-start.4 = (bf16[256,768]{1,0:T(8,128)(2,1)S(1)}, bf16[256,768]{1,0:T(8,128)(2,1)S(1)}, u32[]{:S(2)}, u32[]{:S(2)}) collective-permute-start(bf16[256,768]{1,0:T(8,128)(2,1)S(1)} %get-tuple-element.20.refs_4_), channel_id=1, source_target_pairs={{0,2},{1,3},{2,0},{3,1},{4,6},{5,7},{6,4},{7,5},{8,10},{9,11},{10,... | collective-permute-start | bytes 1179656 | tf_op jit(solution)/shard_map/ppermute | solution.py:19
  12.5 19.2 %collective-permute-start.5 = (bf16[256,768]{1,0:T(8,128)(2,1)S(1)}, bf16[256,768]{1,0:T(8,128)(2,1)S(1)}, u32[]{:S(2)}, u32[]{:S(2)}) collective-permute-start(bf16[256,768]{1,0:T(8,128)(2,1)S(1)} %get-tuple-element.20.refs_4_), channel_id=1, source_target_pairs={{0,3},{1,2},{2,1},{3,0},{4,7},{5,6},{6,5},{7,4},{8,11},{9,10},{10,... | collective-permute-start | bytes 1179656 | tf_op jit(solution)/shard_map/ppermute | solution.py:19
  34.4 7.4 %collective-permute-start.10 = (f32[4,256]{1,0:T(4,128)S(1)}, f32[4,256]{1,0:T(4,128)S(1)}, u32[]{:S(2)}, u32[]{:S(2)}) collective-permute-start(f32[4,256]{1,0:T(4,128)S(1)} %get-tuple-element.22.refs_12_), channel_id=1, source_target_pairs={{0,2},{1,3},{2,0},{3,1},{4,6},{5,7},{6,4},{7,5},{8,10},{9,11},{10,... | collective-permute-start | bytes 12296 | tf_op jit(solution)/shard_map/ppermute | solution.py:19
  35.7 6.9 %collective-permute-start.11 = (f32[4,256]{1,0:T(4,128)S(1)}, f32[4,256]{1,0:T(4,128)S(1)}, u32[]{:S(2)}, u32[]{:S(2)}) collective-permute-start(f32[4,256]{1,0:T(4,128)S(1)} %get-tuple-element.22.refs_12_), channel_id=1, source_target_pairs={{0,3},{1,2},{2,1},{3,0},{4,7},{5,6},{6,5},{7,4},{8,11},{9,10},{10,... | collective-permute-start | bytes 12296 | tf_op jit(solution)/shard_map/ppermute | solution.py:19
  37.9 5.6 %copy-start.4 = (s32[256]{0:T(256)S(1)}, s32[256]{0:T(256)}, u32[]{:S(2)}) copy-start(s32[256]{0:T(256)} %param.6) | copy-start | bytes 3076
  37.9 4.6 %collective-permute-start.6 = (f32[4,256]{1,0:T(4,128)S(1)}, f32[4,256]{1,0:T(4,128)S(1)}, u32[]{:S(2)}, u32[]{:S(2)}) collective-permute-start(f32[4,256]{1,0:T(4,128)S(1)} %get-tuple-element.21.refs_8_), channel_id=1, source_target_pairs={{0,4},{1,5},{2,6},{3,7},{4,0},{5,1},{6,2},{7,3},{8,12},{9,13},{10,... | collective-permute-start | bytes 12296 | tf_op jit(solution)/shard_map/ppermute | solution.py:19
  37.9 4.6 %collective-permute-start.7 = (f32[4,256]{1,0:T(4,128)S(1)}, f32[4,256]{1,0:T(4,128)S(1)}, u32[]{:S(2)}, u32[]{:S(2)}) collective-permute-start(f32[4,256]{1,0:T(4,128)S(1)} %get-tuple-element.21.refs_8_), channel_id=1, source_target_pairs={{0,8},{1,9},{2,10},{3,11},{4,12},{5,13},{6,14},{7,15},{8,0},{9,1},... | collective-permute-start | bytes 12296 | tf_op jit(solution)/shard_map/ppermute | solution.py:19
  39.9 3.7 %collective-permute-start.8 = (f32[4,256]{1,0:T(4,128)S(1)}, f32[4,256]{1,0:T(4,128)S(1)}, u32[]{:S(2)}, u32[]{:S(2)}) collective-permute-start(f32[4,256]{1,0:T(4,128)S(1)} %get-tuple-element.21.refs_8_), channel_id=1, source_target_pairs={{0,12},{1,13},{2,14},{3,15},{4,8},{5,9},{6,10},{7,11},{8,4},{9,5},... | collective-permute-start | bytes 12296 | tf_op jit(solution)/shard_map/ppermute | solution.py:19
  41.8 1.7 %collective-permute-start.9 = (f32[4,256]{1,0:T(4,128)S(1)}, f32[4,256]{1,0:T(4,128)S(1)}, u32[]{:S(2)}, u32[]{:S(2)}) collective-permute-start(f32[4,256]{1,0:T(4,128)S(1)} %get-tuple-element.22.refs_12_), channel_id=1, source_target_pairs={{0,1},{1,0},{2,3},{3,2},{4,5},{5,4},{6,7},{7,6},{8,9},{9,8},{10,11... | collective-permute-start | bytes 12296 | tf_op jit(solution)/shard_map/ppermute | solution.py:19
  43.5 92.8 %copy-start.1 = (bf16[256,768]{1,0:T(8,128)(2,1)S(1)}, bf16[256,768]{1,0:T(8,128)(2,1)}, u32[]{:S(2)}) copy-start(bf16[256,768]{1,0:T(8,128)(2,1)} %image.3) | copy-start | bytes 1179652
  43.5 92.8 %copy-start.3 = (bf16[256,768]{1,0:T(8,128)(2,1)S(1)}, bf16[256,768]{1,0:T(8,128)(2,1)}, u32[]{:S(2)}) copy-start(bf16[256,768]{1,0:T(8,128)(2,1)} %text.3) | copy-start | bytes 1179652
  51.6 50.0 %collective-permute-start.20 = (f32[256,768]{1,0:T(8,128)S(1)}, f32[256,768]{1,0:T(8,128)S(1)}, u32[]{:S(2)}, u32[]{:S(2)}) collective-permute-start(f32[256,768]{1,0:T(8,128)S(1)} %get-tuple-element.25), channel_id=1, source_target_pairs={{0,4},{1,5},{2,6},{3,7},{4,0},{5,1},{6,2},{7,3},{8,12},{9,13},{10,... | collective-permute-start | bytes 2359304 | tf_op jit(solution)/shard_map/ppermute | solution.py:19
  51.7 2.7 %collective-permute-start.12 = (f32[8,128]{1,0:T(8,128)S(1)}, f32[8,128]{1,0:T(8,128)S(1)}, u32[]{:S(2)}, u32[]{:S(2)}) collective-permute-start(f32[8,128]{1,0:T(8,128)S(1)} %get-tuple-element.23), channel_id=1, source_target_pairs={{0,1},{1,0},{2,3},{3,2},{4,5},{5,4},{6,7},{7,6},{8,9},{9,8},{10,11... | collective-permute-start | bytes 12296 | tf_op jit(solution)/shard_map/ppermute | solution.py:19
  54.4 4.0 %collective-permute-start.13 = (f32[8,128]{1,0:T(8,128)S(1)}, f32[8,128]{1,0:T(8,128)S(1)}, u32[]{:S(2)}, u32[]{:S(2)}) collective-permute-start(f32[8,128]{1,0:T(8,128)S(1)} %add.24), channel_id=1, source_target_pairs={{0,2},{1,3},{2,0},{3,1},{4,6},{5,7},{6,4},{7,5},{8,10},{9,11},{10,... | collective-permute-start | bytes 12296 | tf_op jit(solution)/shard_map/ppermute | solution.py:19
  58.3 10.7 %collective-permute-start.14 = (f32[8,128]{1,0:T(8,128)S(1)}, f32[8,128]{1,0:T(8,128)S(1)}, u32[]{:S(2)}, u32[]{:S(2)}) collective-permute-start(f32[8,128]{1,0:T(8,128)S(1)} %add.25), channel_id=1, source_target_pairs={{0,4},{1,5},{2,6},{3,7},{4,0},{5,1},{6,2},{7,3},{8,12},{9,13},{10,... | collective-permute-start | bytes 12296 | tf_op jit(solution)/shard_map/ppermute | solution.py:19
  69.0 4.0 %collective-permute-start.15 = (f32[8,128]{1,0:T(8,128)S(1)}, f32[8,128]{1,0:T(8,128)S(1)}, u32[]{:S(2)}, u32[]{:S(2)}) collective-permute-start(f32[8,128]{1,0:T(8,128)S(1)} %add.26), channel_id=1, source_target_pairs={{0,8},{1,9},{2,10},{3,11},{4,12},{5,13},{6,14},{7,15},{8,0},{9,1},... | collective-permute-start | bytes 12296 | tf_op jit(solution)/shard_map/ppermute | solution.py:19
  73.0 2.8 %collective-permute-start.16 = (f32[8,128]{1,0:T(8,128)S(1)}, f32[8,128]{1,0:T(8,128)S(1)}, u32[]{:S(2)}, u32[]{:S(2)}) collective-permute-start(f32[8,128]{1,0:T(8,128)S(1)} %add.27), channel_id=1, source_target_pairs={{0,16},{16,0},{32,48},{48,32},{64,80},{80,64},{96,112},{112,96},{1... | collective-permute-start | bytes 12296 | tf_op jit(solution)/shard_map/ppermute | solution.py:19
  75.7 2.6 %collective-permute-start.17 = (f32[8,128]{1,0:T(8,128)S(1)}, f32[8,128]{1,0:T(8,128)S(1)}, u32[]{:S(2)}, u32[]{:S(2)}) collective-permute-start(f32[8,128]{1,0:T(8,128)S(1)} %add.28), channel_id=1, source_target_pairs={{0,32},{16,48},{32,0},{48,16},{64,96},{80,112},{96,64},{112,80},{1... | collective-permute-start | bytes 12296 | tf_op jit(solution)/shard_map/ppermute | solution.py:19
  78.4 4.0 %collective-permute-start.18 = (f32[8,128]{1,0:T(8,128)S(1)}, f32[8,128]{1,0:T(8,128)S(1)}, u32[]{:S(2)}, u32[]{:S(2)}) collective-permute-start(f32[8,128]{1,0:T(8,128)S(1)} %add.29), channel_id=1, source_target_pairs={{0,64},{16,80},{32,96},{48,112},{64,0},{80,16},{96,32},{112,48},{1... | collective-permute-start | bytes 12296 | tf_op jit(solution)/shard_map/ppermute | solution.py:19
  82.4 16.3 %collective-permute-start.19 = (f32[8,128]{1,0:T(8,128)S(1)}, f32[8,128]{1,0:T(8,128)S(1)}, u32[]{:S(2)}, u32[]{:S(2)}) collective-permute-start(f32[8,128]{1,0:T(8,128)S(1)} %add.30), channel_id=1, source_target_pairs={{0,128},{16,144},{32,160},{48,176},{64,192},{80,208},{96,224},{112... | collective-permute-start | bytes 12296 | tf_op jit(solution)/shard_map/ppermute | solution.py:19
  88.5 15.3 %collective-permute-start.21 = (f32[256,768]{1,0:T(8,128)S(1)}, f32[256,768]{1,0:T(8,128)S(1)}, u32[]{:S(2)}, u32[]{:S(2)}) collective-permute-start(f32[256,768]{1,0:T(8,128)S(1)} %get-tuple-element.26), channel_id=1, source_target_pairs={{0,8},{1,9},{2,10},{3,11},{4,12},{5,13},{6,14},{7,15},{8,0},{9,1},... | collective-permute-start | bytes 2359304 | tf_op jit(solution)/shard_map/ppermute | solution.py:19
  89.3 37.0 %collective-permute-start.22 = (f32[256,768]{1,0:T(8,128)S(1)}, f32[256,768]{1,0:T(8,128)S(1)}, u32[]{:S(2)}, u32[]{:S(2)}) collective-permute-start(f32[256,768]{1,0:T(8,128)S(1)} %get-tuple-element.27), channel_id=1, source_target_pairs={{0,12},{1,13},{2,14},{3,15},{4,8},{5,9},{6,10},{7,11},{8,4},{9,5},... | collective-permute-start | bytes 2359304 | tf_op jit(solution)/shard_map/ppermute | solution.py:19
  91.1 35.1 %collective-permute-start.23 = (f32[256,768]{1,0:T(8,128)S(1)}, f32[256,768]{1,0:T(8,128)S(1)}, u32[]{:S(2)}, u32[]{:S(2)}) collective-permute-start(f32[256,768]{1,0:T(8,128)S(1)} %get-tuple-element.29), channel_id=1, source_target_pairs={{0,1},{1,0},{2,3},{3,2},{4,5},{5,4},{6,7},{7,6},{8,9},{9,8},{10,11... | collective-permute-start | bytes 2359304 | tf_op jit(solution)/shard_map/ppermute | solution.py:19
  98.7 27.6 %collective-permute-start.24 = (f32[256,768]{1,0:T(8,128)S(1)}, f32[256,768]{1,0:T(8,128)S(1)}, u32[]{:S(2)}, u32[]{:S(2)}) collective-permute-start(f32[256,768]{1,0:T(8,128)S(1)} %get-tuple-element.30), channel_id=1, source_target_pairs={{0,2},{1,3},{2,0},{3,1},{4,6},{5,7},{6,4},{7,5},{8,10},{9,11},{10,... | collective-permute-start | bytes 2359304 | tf_op jit(solution)/shard_map/ppermute | solution.py:19
  101.6 34.7 %collective-permute-start.25 = (f32[256,768]{1,0:T(8,128)S(1)}, f32[256,768]{1,0:T(8,128)S(1)}, u32[]{:S(2)}, u32[]{:S(2)}) collective-permute-start(f32[256,768]{1,0:T(8,128)S(1)} %get-tuple-element.31), channel_id=1, source_target_pairs={{0,3},{1,2},{2,1},{3,0},{4,7},{5,6},{6,5},{7,4},{8,11},{9,10},{10,... | collective-permute-start | bytes 2359304 | tf_op jit(solution)/shard_map/ppermute | solution.py:19

commit v2 on v0

v2 whole, which is shorter than its diff:
```python
import jax
import jax.numpy as jnp
from jax import lax
from jax.experimental import pallas as pl
from jax.experimental.pallas import tpu as pltpu
from jax.sharding import PartitionSpec as P

EPSILON = 1e-06
VMEM = pl.BlockSpec(memory_space=pltpu.VMEM)
SMEM = pl.BlockSpec(memory_space=pltpu.SMEM)
SLOTS = 4
LOW = -1e30
NEAR = (0, 1, 3)
X1, X2, X3, Y, CORE = 4, 8, 12, 2, 1


def swapped(value, bits, axis="blk"):
    return lax.ppermute(value, axis, [(i, i ^ bits) for i in range(lax.axis_size(axis))])


def call(kernel, name, outs, *args, scalar=False):
    specs = [SMEM] * scalar + [VMEM] * (len(args) - scalar)
    return pl.pallas_call(
        kernel, out_shape=[jax.ShapeDtypeStruct(s, d) for s, d in outs], in_specs=specs,
        out_specs=[VMEM] * len(outs), name=name,
        compiler_params=pltpu.CompilerParams(vmem_limit_bytes=24 * 1024 * 1024),
    )(*args)


def eye(n):
    return lax.broadcasted_iota(jnp.int32, (n, n), 0) == lax.broadcasted_iota(jnp.int32, (n, n), 1)


def to_row(column, diagonal):
    return jnp.sum(jnp.where(diagonal, column, 0.0), axis=0, keepdims=True)


def to_column(row, diagonal):
    return jnp.sum(jnp.where(diagonal, row, 0.0), axis=1, keepdims=True)


def unit_rows(values):
    wide = values.astype(jnp.float32)
    inverse = lax.rsqrt(jnp.sum(wide * wide, axis=-1, keepdims=True) + EPSILON)
    return wide * inverse, inverse


def hits(positive, diagonal):
    target = to_column(positive[...].astype(jnp.float32), diagonal).astype(jnp.int32)
    return lax.broadcasted_iota(jnp.int32, diagonal.shape, 1) == target


def merged(a, b):
    top = jnp.maximum(a[0], b[0])
    ea, eb = jnp.exp(a[0] - top), jnp.exp(b[0] - top)
    both = ea + eb
    return top + jnp.log(both), (a[1] * ea + b[1] * eb) / both


def into(part, span, value):
    part[0:1, span], part[1:2, span] = merged((part[0:1, span], part[1:2, span]), value)


def stats(scale, imgs, txts, logits, row_part, col_part):
    diagonal = eye(next(iter(txts.values())).shape[0])
    rows = diagonal.shape[0]
    slots, blocks = tuple(imgs), tuple(txts)
    at = lambda k: pl.ds(k * rows, rows)
    row_top, col_top = {}, {}
    for l in blocks:
        for k in slots:
            tile = scale * lax.dot_general(
                imgs[k][...], txts[l][...], (((1,), (1,)), ((), ())),
                preferred_element_type=jnp.float32,
            )
            logits[k, l][...] = tile
            right = jnp.max(tile, axis=1, keepdims=True)
            down = jnp.max(tile, axis=0, keepdims=True)
            row_top[k] = jnp.maximum(row_top[k], right) if k in row_top else right
            col_top[l] = jnp.maximum(col_top[l], down) if l in col_top else down
    none = jnp.zeros((1, rows), jnp.float32)
    col_sum, col_moment = {l: none for l in blocks}, {l: none for l in blocks}
    for k in slots:
        total = jnp.zeros((rows, 1), jnp.float32)
        moment = jnp.zeros((rows, 1), jnp.float32)
        for l in blocks:
            tile = logits[k, l][...]
            e = jnp.exp(tile - row_top[k])
            total += jnp.sum(e, axis=1, keepdims=True)
            moment += jnp.sum(e * tile, axis=1, keepdims=True)
            f = jnp.exp(tile - col_top[l])
            col_sum[l] += jnp.sum(f, axis=0, keepdims=True)
            col_moment[l] += jnp.sum(f * tile, axis=0, keepdims=True)
        total = to_row(total, diagonal)
        top = to_row(row_top[k], diagonal)
        into(row_part, at(k), (top + jnp.log(total), to_row(moment, diagonal) / total))
    for l in blocks:
        into(col_part, at(l), (col_top[l] + jnp.log(col_sum[l]), col_moment[l] / col_sum[l]))


def unit(values):
    return unit_rows(values[...])[0].astype(jnp.bfloat16)


def views(ref, slots, rows):
    return {k: ref.at[pl.ds(n * rows, rows), :] for n, k in enumerate(slots)}


def tiles(ref, slots, blocks, rows):
    return {
        (k, l): ref.at[pl.ds(n * rows, rows), pl.ds(m * rows, rows)]
        for n, k in enumerate(slots) for m, l in enumerate(blocks)
    }


def first_kernel(
    scale, i0, i1, i3, t0, t1, t2, positive, near, txts, logits, row_part, col_part
):
    rows = i0.shape[0]
    imgs, texts = views(near, NEAR, rows), views(txts, (0, 1, 2), rows)
    for k, raw in ((0, i0), (1, i1), (3, i3)):
        imgs[k][...] = unit(raw)
    for l, raw in ((0, t0), (1, t1), (2, t2)):
        texts[l][...] = unit(raw)
    for part in (row_part, col_part):
        part[0:1, :] = jnp.full((1, SLOTS * rows), LOW, jnp.float32)
        part[1:4, :] = jnp.zeros((3, SLOTS * rows), jnp.float32)
    scores = tiles(logits, NEAR, (0, 1, 2), rows)
    stats(scale[0], imgs, texts, scores, row_part, col_part)
    matched = jnp.where(hits(positive, eye(rows)), scores[0, 0][...], 0.0)
    row_part[2:3, pl.ds(0, rows)] = jnp.sum(matched, axis=0, keepdims=True)


def split_kernel(i1, i3, via1, via3):
    half = via1.shape[0]
    via1[...] = i3[pl.ds(0, half), :]
    via3[...] = i1[pl.ds(half, half), :]


def second_kernel(scale, t3, near, txts_in, row_in, col_in, txts, logits, row_part, col_part):
    rows = t3.shape[0]
    row_part[...] = row_in[...]
    col_part[...] = col_in[...]
    txts[pl.ds(0, 3 * rows), :] = txts_in[...]
    last = txts.at[pl.ds(3 * rows, rows), :]
    last[...] = unit(t3)
    scores = tiles(logits, NEAR, (3,), rows)
    stats(scale[0], views(near, NEAR, rows), {3: last}, scores, row_part, col_part)


def third_kernel(scale, i2a, i2b, txts, row_in, col_in, far, logits, row_part, col_part):
    half = i2a.shape[0]
    rows = 2 * half
    row_part[...] = row_in[...]
    col_part[...] = col_in[...]
    far[pl.ds(0, half), :] = unit(i2a)
    far[pl.ds(half, half), :] = unit(i2b)
    blocks = range(SLOTS)
    scores = tiles(logits, (2,), blocks, rows)
    stats(scale[0], {2: far}, views(txts, blocks, rows), scores, row_part, col_part)


def joined(mine, theirs, bit):
    rows = mine.shape[1] // SLOTS
    swap = lambda at: jnp.concatenate(
        [theirs[at : at + 1, (k ^ bit) * rows : ((k ^ bit) + 1) * rows] for k in range(SLOTS)], axis=1
    )
    value, mean = merged((mine[0:1, :], mine[1:2, :]), (swap(0), swap(1)))
    return value, mean, mine[2:3, :] + swap(2)


def join_kernel(row_a, row_b, col_a, col_b, row, col):
    for a, b, out in ((row_a, row_b, row), (col_a, col_b, col)):
        out[0:1, :], out[1:2, :], out[2:3, :] = joined(a, b, 1)
        out[3:4, :] = jnp.zeros((1, out.shape[1]), jnp.float32)


def lse_kernel(row_a, row_b, col_a, col_b, lse, row_sums, col_sums):
    lane = lax.broadcasted_iota(jnp.int32, row_sums.shape, 1)
    for at, (a, b, out) in enumerate(((row_a, row_b, row_sums), (col_a, col_b, col_sums))):
        value, mean, matched = joined(a, b, 2)
        lse[at : at + 1, :] = value
        add = lambda v: jnp.sum(v, axis=1, keepdims=True)
        loss, slope = add(0.5 * value - matched), add(0.5 * mean - matched)
        out[...] = jnp.where(lane == 0, loss, jnp.where(lane == 1, slope, 0.0))


def over(near_w, far_w, near, far, span):
    term = lambda weights, blocks: lax.dot_general(
        weights[:, span], blocks[...], (((0,), (0,)), ((), ())), preferred_element_type=jnp.float32
    )
    return term(near_w, near) + term(far_w, far)


def weight_kernel(first, second, third, lse, positive, near, far, near_w, far_w, core_part):
    rows = far.shape[0]
    diagonal = eye(rows)
    at = lambda k: pl.ds(k * rows, rows)
    blocks = range(SLOTS)
    scores = tiles(first, NEAR, (0, 1, 2), rows)
    scores.update(tiles(second, NEAR, (3,), rows))
    scores.update(tiles(third, (2,), blocks, rows))
    w = tiles(near_w, NEAR, blocks, rows)
    w.update(tiles(far_w, (2,), blocks, rows))
    for k in range(SLOTS):
        right = to_column(lse[0:1, at(k)], diagonal)
        for l in blocks:
            tile = scores[k, l][...]
            weight = 0.5 * (jnp.exp(tile - right) + jnp.exp(tile - lse[1:2, at(l)]))
            if k == 0 and l == 0:
                weight = weight - hits(positive, diagonal).astype(jnp.float32)
            w[k, l][...] = weight.astype(jnp.bfloat16)
    for n, l in enumerate((1, 3)):
        core_part[at(n), :] = over(near_w, far_w, near, far, at(l)).astype(core_part.dtype)


def home_kernel(
    near_w, far_w, near, far, txts, row_a, row_b, col_a, col_b,
    img_back, txt_back, txt_next, row, col,
):
    rows = img_back.shape[0]
    img_back[...] = jnp.dot(near_w[pl.ds(0, rows), :], txts[...], preferred_element_type=jnp.float32)
    for out, l in ((txt_back, 0), (txt_next, 2)):
        out[...] = over(near_w, far_w, near, far, pl.ds(l * rows, rows))
    row[...] = row_a[...] + row_b[...]
    col[...] = col_a[...] + col_b[...]


def away_kernel(
    near_w, far_w, txts, txt_next, core_part, row_a, row_b, col_a, col_b,
    part1, part2, part3, part_y, sums,
):
    rows = part1.shape[0]
    w = views(near_w, NEAR, rows)
    w[2] = far_w
    for k, out in ((1, part1), (2, part2), (3, part3)):
        back = jnp.dot(w[k][...], txts[...], preferred_element_type=jnp.float32)
        out[...] = back.astype(out.dtype)
    total = txt_next[...] + core_part[pl.ds(rows, rows), :].astype(jnp.float32)
    part_y[...] = total.astype(part_y.dtype)
    sums[...] = (row_a[...] + row_b[...]) + (col_a[...] + col_b[...])


def grad_kernel(scale, image, text, img_back, txt_back, core_part, p1, p2, p3, py, image_grad, text_grad):
    for values, parts, out in (
        (image, (img_back, p1, p2, p3), image_grad), (text, (txt_back, core_part, py), text_grad),
    ):
        direction, inverse = unit_rows(values[...])
        incoming = scale[0] * sum(
            part[pl.ds(0, direction.shape[0]), :].astype(jnp.float32) for part in parts
        )
        along = jnp.sum(direction * incoming, axis=-1, keepdims=True)
        out[...] = ((incoming - direction * along) * inverse).astype(out.dtype)


def shards(image, text, positive, logit_scale):
    rows, width = image.shape
    group = SLOTS * rows
    f32, bf16 = jnp.float32, jnp.bfloat16
    block, parts = ((rows, width), bf16), ((SLOTS, group), f32)
    positive = positive.reshape(1, rows)

    i1, i3 = swapped(image, X1), swapped(image, X3)
    t1, t2 = swapped(text, CORE), swapped(text, Y)
    half = ((rows // 2, width), bf16)
    via1, via3 = call(split_kernel, "split", [half] * 2, i1, i3)
    i2a, i2b = swapped(via1, X1), swapped(via3, X3)
    t3 = swapped(t2, CORE)
    three = group - rows
    near, txts, first, row_part, col_part = call(
        first_kernel, "first", [((three, width), bf16)] * 2 + [((three, three), f32), parts, parts],
        logit_scale, image, i1, i3, text, t1, t2, positive, scalar=True,
    )
    txts, second, row_part, col_part = call(
        second_kernel, "second", [((group, width), bf16), ((three, rows), f32), parts, parts],
        logit_scale, t3, near, txts, row_part, col_part, scalar=True,
    )
    far, third, row_part, col_part = call(
        third_kernel, "third", [block, ((rows, group), f32), parts, parts],
        logit_scale, i2a, i2b, txts, row_part, col_part, scalar=True,
    )
    row_half, col_half = call(
        join_kernel, "join", [parts] * 2,
        row_part, swapped(row_part, X1), col_part, swapped(col_part, CORE),
    )
    lse, row_sums, col_sums = call(
        lse_kernel, "lse", [((2, group), f32)] + [((8, 128), f32)] * 2,
        row_half, swapped(row_half, X2), col_half, swapped(col_half, Y),
    )
    near_w, far_w, core_part = call(
        weight_kernel, "weight",
        [((three, group), bf16), ((rows, group), bf16), ((2 * rows, width), bf16)],
        first, second, third, lse, positive, near, far,
    )
    core_part = swapped(core_part, CORE)
    wide, few = ((rows, width), f32), ((8, 128), f32)
    img_back, txt_back, txt_next, row_sums, col_sums = call(
        home_kernel, "home", [wide] * 3 + [few] * 2, near_w, far_w, near, far, txts,
        row_sums, swapped(row_sums, CORE), col_sums, swapped(col_sums, X1),
    )
    part1, part2, part3, part_y, sums = call(
        away_kernel, "away", [block] * 4 + [few], near_w, far_w, txts, txt_next, core_part,
        row_sums, swapped(row_sums, Y), col_sums, swapped(col_sums, X2),
    )
    part1, part2, part3 = swapped(part1, X1), swapped(part2, X2), swapped(part3, X3)
    part_y = swapped(part_y, Y)
    step = lax.axis_size("dp") // 2
    while step >= 1:
        sums = sums + swapped(sums, step, "dp")
        step //= 2
    image_grad, text_grad = call(
        grad_kernel, "grad", [block] * 2,
        logit_scale, image, text, img_back, txt_back, core_part, part1, part2, part3, part_y, scalar=True,
    )
    total_rows = rows * lax.axis_size("blk") * lax.axis_size("dp")
    loss = sums[0, :1] / total_rows
    scale_grad = sums[0, 1:2] / (total_rows * logit_scale)
    return (loss, scale_grad, image_grad, text_grad)


def solution(mesh):
    in_specs = (P(("dp", "blk"), None), P(("dp", "blk"), None), P(("dp", "blk")), P())
    out_specs = (P(), P(), P(("dp", "blk"), None), P(("dp", "blk"), None))
    return jax.shard_map(shards, mesh=mesh, in_specs=in_specs, out_specs=out_specs, check_vma=False)
```

time: 614 us -> 86.9 us (0.14)
  the two profiles are of different devices: /device:TPU:1 before, /device:TPU:16 now
where the time goes in v2:
time: 86.9 us; the launch traced here: 86.6 us
  starting transfers between devices  35.8 us (41%)
  waiting for transfers between devices  30.7 us (35%)
  Pallas kernels  11.8 us (14%)
  between operations  5.03 us (6%)
  local copies, waits for them, and re-layouts  3.26 us (4%)
    ppermute x24, starting transfers between devices, swapped(): lax.ppermute(value, axis, [(i, i ^ bits) for i in range(lax.axis_size(axi...  35.8 us
    ppermute x24, waiting for transfers between devices, swapped(): lax.ppermute(value, axis, [(i, i ^ bits) for i in range(lax.axis_size(axi...  30.7 us
    pallas_call x10, Pallas kernels, call(): pl.pallas_call(kernel, out_shape=[jax.ShapeDtypeStruct(s, d) for s, d in...  11.8 us
    unnamed x12, local copies, waits for them, and re-layouts  2.68 us
  transfers between devices with their start and end apart: 24, of which 13 were waited for; matrix products, arithmetic and copies ran while one was open for 1% of the time, Pallas kernels for 6%

profile of v2, /device:TPU:16, one launch (start us, length us, event | category | flops | bytes accessed | tf_op | source)
XLA Modules:
  0.0 86.6 jit_solution(13824531051737462507)
XLA Ops:
  0.6 2.2 %collective-permute-start.3 = (bf16[256,768]{1,0:T(8,128)(2,1)}, bf16[256,768]{1,0:T(8,128)(2,1)S(1)}, u32[]{:S(2)}, u32[]{:S(2)}) collective-permute-start(bf16[256,768]{1,0:T(8,128)(2,1)} %text.1), channel_id=1, source_target_pairs={{0,2},{1,3},{2,0},{3,1},{4,6},{5,7},{6,4},{7,5},{8,10},{9,11},{10,... | collective-permute-start | bytes 1179656 | tf_op jit(solution)/shard_map/ppermute | solution.py:18
  2.8 0.0 collective-permute-start
  2.8 1.8 %collective-permute-start.1 = (bf16[256,768]{1,0:T(8,128)(2,1)}, bf16[256,768]{1,0:T(8,128)(2,1)S(1)}, u32[]{:S(2)}, u32[]{:S(2)}) collective-permute-start(bf16[256,768]{1,0:T(8,128)(2,1)} %image.1), channel_id=1, source_target_pairs={{0,12},{1,13},{2,14},{3,15},{4,8},{5,9},{6,10},{7,11},{8,4},{9,5},... | collective-permute-start | bytes 1179656 | tf_op jit(solution)/shard_map/ppermute | solution.py:18
  4.6 0.0 collective-permute-start.2
  4.6 8.6 %collective-permute-done.3.t2 = bf16[256,768]{1,0:T(8,128)(2,1)S(1)} collective-permute-done((bf16[256,768]{1,0:T(8,128)(2,1)}, bf16[256,768]{1,0:T(8,128)(2,1)S(1)}, u32[]{:S(2)}, u32[]{:S(2)}) %collective-permute-start.3) | collective-permute-done | bytes 393248 | tf_op jit(solution)/shard_map/ppermute | solution.py:18
  13.3 0.0 collective-permute-start.4
  13.3 0.0 collective-permute-done.i1
  13.3 1.0 %collective-permute-done.1.i3 = bf16[256,768]{1,0:T(8,128)(2,1)S(1)} collective-permute-done((bf16[256,768]{1,0:T(8,128)(2,1)}, bf16[256,768]{1,0:T(8,128)(2,1)S(1)}, u32[]{:S(2)}, u32[]{:S(2)}) %collective-permute-start.1) | collective-permute-done | bytes 393248 | tf_op jit(solution)/shard_map/ppermute | solution.py:18
  14.3 0.6 collective-permute-start.5
  14.9 2.1 %collective-permute-start.6 = (bf16[128,768]{1,0:T(8,128)(2,1)S(1)}, bf16[128,768]{1,0:T(8,128)(2,1)S(1)}, u32[]{:S(2)}, u32[]{:S(2)}) collective-permute-start(bf16[128,768]{1,0:T(8,128)(2,1)S(1)} %get-tuple-element.46), channel_id=1, source_target_pairs={{0,12},{1,13},{2,14},{3,15},{4,8},{5,9},{6,10},{7,11},{8,4},{9,5},... | collective-permute-start | bytes 589832 | tf_op jit(solution)/shard_map/ppermute | solution.py:18
  17.7 0.0 collective-permute-done.2.t1
  17.7 0.0 copy-start
  17.7 1.0 %copy-done = bf16[256,768]{1,0:T(8,128)(2,1)S(1)} copy-done((bf16[256,768]{1,0:T(8,128)(2,1)S(1)}, bf16[256,768]{1,0:T(8,128)(2,1)}, u32[]{:S(2)}) %copy-start) | copy-done | bytes 393240
  18.7 1.0 %copy-done.2 = bf16[256,768]{1,0:T(8,128)(2,1)S(1)} copy-done((bf16[256,768]{1,0:T(8,128)(2,1)S(1)}, bf16[256,768]{1,0:T(8,128)(2,1)}, u32[]{:S(2)}) %copy-start.2) | copy-done | bytes 393240
  19.7 0.7 copy-done.4
  20.3 2.7 %first.1 = (bf16[768,768]{1,0:T(8,128)(2,1)S(1)}, bf16[768,768]{1,0:T(8,128)(2,1)S(1)}, f32[768,768]{1,0:T(8,128)S(1)}, f32[4,1024]{1,0:T(4,128)S(1)}, f32[4,1024]{1,0:T(4,128)S(1)}) custom-call(f32[1]{0:T(128)S(6)} %copy.8.scale, bf16[256,768]{1,0:T(8,128)(2,1)S(1)} %copy-done, bf16[256,768]{1,0:T(8,128)(2,1)S(1)} %collective-permute-done.i1, ...), custom_call_target="tpu_custom_call" | custom-call | tf_op jit(solution)/shard_map/first/pallas_call | solution.py:23
  23.1 0.0 collective-permute-done.4.t3
  23.1 1.1 %second.1 = (bf16[1024,768]{1,0:T(8,128)(2,1)S(1)}, f32[768,256]{1,0:T(8,128)S(1)}, f32[4,1024]{1,0:T(4,128)S(1)}, f32[4,1024]{1,0:T(4,128)S(1)}) custom-call(f32[1]{0:T(128)S(6)} %copy.8.scale, bf16[256,768]{1,0:T(8,128)(2,1)S(1)} %collective-permute-done.4.t3, bf16[768,768]{1,0:T(8,128)(2,1)S(1)} %get-tuple-element.40.near, ...), custom_call_target="tpu_custom_call" | custom-call | tf_op jit(solution)/shard_map/second/pallas_call | solution.py:23
  24.2 0.0 copy-start.5
  24.2 0.0 collective-permute-done.5.i2a
  24.2 0.0 collective-permute-done.6.i2b
  24.2 1.1 %third.1 = (bf16[256,768]{1,0:T(8,128)(2,1)S(1)}, f32[256,1024]{1,0:T(8,128)S(1)}, f32[4,1024]{1,0:T(4,128)S(1)}, f32[4,1024]{1,0:T(4,128)S(1)}) custom-call(f32[1]{0:T(128)S(6)} %copy.8.scale, bf16[128,768]{1,0:T(8,128)(2,1)S(1)} %collective-permute-done.5.i2a, bf16[128,768]{1,0:T(8,128)(2,1)S(1)} %collective-permute-done.6.i2b, ...), custom_call_target="tpu_custom_call" | custom-call | tf_op jit(solution)/shard_map/third/pallas_call | solution.py:23
  25.3 1.0 %collective-permute-start.7 = (f32[4,1024]{1,0:T(4,128)S(1)}, f32[4,1024]{1,0:T(4,128)S(1)}, u32[]{:S(2)}, u32[]{:S(2)}) collective-permute-start(f32[4,1024]{1,0:T(4,128)S(1)} %get-tuple-element.51.row_a), channel_id=1, source_target_pairs={{0,4},{1,5},{2,6},{3,7},{4,0},{5,1},{6,2},{7,3},{8,12},{9,13},{10,... | collective-permute-start | bytes 49160 | tf_op jit(solution)/shard_map/ppermute | solution.py:18
  26.4 0.0 collective-permute-start.8
  26.4 2.8 %collective-permute-done.7.row_b = f32[4,1024]{1,0:T(4,128)S(1)} collective-permute-done((f32[4,1024]{1,0:T(4,128)S(1)}, f32[4,1024]{1,0:T(4,128)S(1)}, u32[]{:S(2)}, u32[]{:S(2)}) %collective-permute-start.7) | collective-permute-done | bytes 16416 | tf_op jit(solution)/shard_map/ppermute | solution.py:18
  29.2 0.0 collective-permute-done.8.col_b
  29.2 2.8 %collective-permute-start.10 = (f32[4,1024]{1,0:T(4,128)S(1)}, f32[4,1024]{1,0:T(4,128)S(1)}, u32[]{:S(2)}, u32[]{:S(2)}) collective-permute-start(f32[4,1024]{1,0:T(4,128)S(1)} %get-tuple-element.54.col_a), channel_id=1, source_target_pairs={{0,2},{1,3},{2,0},{3,1},{4,6},{5,7},{6,4},{7,5},{8,10},{9,11},{10,... | collective-permute-start | bytes 49160 | tf_op jit(solution)/shard_map/ppermute | solution.py:18
  32.1 1.9 %collective-permute-start.9 = (f32[4,1024]{1,0:T(4,128)S(1)}, f32[4,1024]{1,0:T(4,128)S(1)}, u32[]{:S(2)}, u32[]{:S(2)}) collective-permute-start(f32[4,1024]{1,0:T(4,128)S(1)} %get-tuple-element.53.row_a), channel_id=1, source_target_pairs={{0,8},{1,9},{2,10},{3,11},{4,12},{5,13},{6,14},{7,15},{8,0},{9,1},... | collective-permute-start | bytes 49160 | tf_op jit(solution)/shard_map/ppermute | solution.py:18
  34.0 0.6 collective-permute-done.10.col_b
  34.5 2.8 %collective-permute-done.9.row_b = f32[4,1024]{1,0:T(4,128)S(1)} collective-permute-done((f32[4,1024]{1,0:T(4,128)S(1)}, f32[4,1024]{1,0:T(4,128)S(1)}, u32[]{:S(2)}, u32[]{:S(2)}) %collective-permute-start.9) | collective-permute-done | bytes 16416 | tf_op jit(solution)/shard_map/ppermute | solution.py:18
  37.3 0.1 lse.1
  37.4 0.0 copy-done.5
  37.4 2.1 %weight.1 = (bf16[768,1024]{1,0:T(8,128)(2,1)S(1)}, bf16[256,1024]{1,0:T(8,128)(2,1)S(1)}, bf16[512,768]{1,0:T(8,128)(2,1)S(1)}) custom-call(f32[768,768]{1,0:T(8,128)S(1)} %get-tuple-element.39.first, f32[768,256]{1,0:T(8,128)S(1)} %get-tuple-element.44.second, f32[256,1024]{1,0:T(8,128)S(1)} %get-tuple-element.50.third, ...), custom_call_target="tpu_custom_call" | custom-call | tf_op jit(solution)/shard_map/weight/pallas_call | solution.py:23
  39.6 0.1 collective-permute-start.13
  39.7 0.5 collective-permute-start.11
  40.2 1.3 %collective-permute-start.12 = (f32[8,128]{1,0:T(8,128)S(1)}, f32[8,128]{1,0:T(8,128)S(1)}, u32[]{:S(2)}, u32[]{:S(2)}) collective-permute-start(f32[8,128]{1,0:T(8,128)S(1)} %get-tuple-element.60.col_a), channel_id=1, source_target_pairs={{0,4},{1,5},{2,6},{3,7},{4,0},{5,1},{6,2},{7,3},{8,12},{9,13},{10,... | collective-permute-start | bytes 12296 | tf_op jit(solution)/shard_map/ppermute | solution.py:18
  41.5 0.5 collective-permute-done.11.row_b
  42.0 1.8 %collective-permute-done.12.col_b = f32[8,128]{1,0:T(8,128)S(1)} collective-permute-done((f32[8,128]{1,0:T(8,128)S(1)}, f32[8,128]{1,0:T(8,128)S(1)}, u32[]{:S(2)}, u32[]{:S(2)}) %collective-permute-start.12) | collective-permute-done | bytes 4128 | tf_op jit(solution)/shard_map/ppermute | solution.py:18
  43.8 1.4 %home.1 = (f32[256,768]{1,0:T(8,128)S(1)}, f32[256,768]{1,0:T(8,128)S(1)}, f32[256,768]{1,0:T(8,128)S(1)}, f32[8,128]{1,0:T(8,128)S(1)}, f32[8,128]{1,0:T(8,128)S(1)}) custom-call(bf16[768,1024]{1,0:T(8,128)(2,1)S(1)} %get-tuple-element.57.near_w, bf16[256,1024]{1,0:T(8,128)(2,1)S(1)} %get-tuple-element.58.far_w, ...), custom_call_target="tpu_custom_call" | custom-call | tf_op jit(solution)/shard_map/home/pallas_call | solution.py:23
  45.2 0.9 collective-permute-start.14
  46.1 1.5 %collective-permute-start.15 = (f32[8,128]{1,0:T(8,128)S(1)}, f32[8,128]{1,0:T(8,128)S(1)}, u32[]{:S(2)}, u32[]{:S(2)}) collective-permute-start(f32[8,128]{1,0:T(8,128)S(1)} %get-tuple-element.64.col_a), channel_id=1, source_target_pairs={{0,8},{1,9},{2,10},{3,11},{4,12},{5,13},{6,14},{7,15},{8,0},{9,1},... | collective-permute-start | bytes 12296 | tf_op jit(solution)/shard_map/ppermute | solution.py:18
  47.6 2.8 %collective-permute-done.14.row_b = f32[8,128]{1,0:T(8,128)S(1)} collective-permute-done((f32[8,128]{1,0:T(8,128)S(1)}, f32[8,128]{1,0:T(8,128)S(1)}, u32[]{:S(2)}, u32[]{:S(2)}) %collective-permute-start.14) | collective-permute-done | bytes 4128 | tf_op jit(solution)/shard_map/ppermute | solution.py:18
  50.4 0.8 collective-permute-done.15.col_b
  51.2 0.0 collective-permute-done.13.core_part
  51.2 1.5 %away.1 = (bf16[256,768]{1,0:T(8,128)(2,1)S(1)}, bf16[256,768]{1,0:T(8,128)(2,1)S(1)}, bf16[256,768]{1,0:T(8,128)(2,1)S(1)}, bf16[256,768]{1,0:T(8,128)(2,1)S(1)}, f32[8,128]{1,0:T(8,128)S(1)}) custom-call(bf16[768,1024]{1,0:T(8,128)(2,1)S(1)} %get-tuple-element.57.near_w, bf16[256,1024]{1,0:T(8,128)(2,1)S(1)} %get-tuple-element.58.far_w, ...), custom_call_target="tpu_custom_call" | custom-call | tf_op jit(solution)/shard_map/away/pallas_call | solution.py:23
  52.7 1.0 %collective-permute-start.20 = (bf16[256,768]{1,0:T(8,128)(2,1)S(1)}, bf16[256,768]{1,0:T(8,128)(2,1)S(1)}, u32[]{:S(2)}, u32[]{:S(2)}) collective-permute-start(bf16[256,768]{1,0:T(8,128)(2,1)S(1)} %get-tuple-element.68), channel_id=1, source_target_pairs={{0,4},{1,5},{2,6},{3,7},{4,0},{5,1},{6,2},{7,3},{8,12},{9,13},{10,... | collective-permute-start | bytes 1179656 | tf_op jit(solution)/shard_map/ppermute | solution.py:18
  53.7 1.7 %collective-permute-start.21 = (bf16[256,768]{1,0:T(8,128)(2,1)S(1)}, bf16[256,768]{1,0:T(8,128)(2,1)S(1)}, u32[]{:S(2)}, u32[]{:S(2)}) collective-permute-start(bf16[256,768]{1,0:T(8,128)(2,1)S(1)} %get-tuple-element.69), channel_id=1, source_target_pairs={{0,8},{1,9},{2,10},{3,11},{4,12},{5,13},{6,14},{7,15},{8,0},{9,1},... | collective-permute-start | bytes 1179656 | tf_op jit(solution)/shard_map/ppermute | solution.py:18
  55.4 2.1 %collective-permute-start.22 = (bf16[256,768]{1,0:T(8,128)(2,1)S(1)}, bf16[256,768]{1,0:T(8,128)(2,1)S(1)}, u32[]{:S(2)}, u32[]{:S(2)}) collective-permute-start(bf16[256,768]{1,0:T(8,128)(2,1)S(1)} %get-tuple-element.70), channel_id=1, source_target_pairs={{0,12},{1,13},{2,14},{3,15},{4,8},{5,9},{6,10},{7,11},{8,4},{9,5},... | collective-permute-start | bytes 1179656 | tf_op jit(solution)/shard_map/ppermute | solution.py:18
  57.5 2.8 %collective-permute-start.23 = (bf16[256,768]{1,0:T(8,128)(2,1)S(1)}, bf16[256,768]{1,0:T(8,128)(2,1)S(1)}, u32[]{:S(2)}, u32[]{:S(2)}) collective-permute-start(bf16[256,768]{1,0:T(8,128)(2,1)S(1)} %get-tuple-element.71), channel_id=1, source_target_pairs={{0,2},{1,3},{2,0},{3,1},{4,6},{5,7},{6,4},{7,5},{8,10},{9,11},{10,... | collective-permute-start | bytes 1179656 | tf_op jit(solution)/shard_map/ppermute | solution.py:18
  60.3 7.2 %collective-permute-start.16 = (f32[8,128]{1,0:T(8,128)S(1)}, f32[8,128]{1,0:T(8,128)S(1)}, u32[]{:S(2)}, u32[]{:S(2)}) collective-permute-start(f32[8,128]{1,0:T(8,128)S(1)} %get-tuple-element.65), channel_id=1, source_target_pairs={{0,128},{16,144},{32,160},{48,176},{64,192},{80,208},{96,224},{112... | collective-permute-start | bytes 12296 | tf_op jit(solution)/shard_map/ppermute | solution.py:18
  67.5 1.6 %collective-permute-done.16 = f32[8,128]{1,0:T(8,128)S(1)} collective-permute-done((f32[8,128]{1,0:T(8,128)S(1)}, f32[8,128]{1,0:T(8,128)S(1)}, u32[]{:S(2)}, u32[]{:S(2)}) %collective-permute-start.16) | collective-permute-done | bytes 4128 | tf_op jit(solution)/shard_map/ppermute | solution.py:18
  69.0 2.0 %collective-permute-start.17 = (f32[8,128]{1,0:T(8,128)S(1)}, f32[8,128]{1,0:T(8,128)S(1)}, u32[]{:S(2)}, u32[]{:S(2)}) collective-permute-start(f32[8,128]{1,0:T(8,128)S(1)} %add.12), channel_id=1, source_target_pairs={{0,64},{16,80},{32,96},{48,112},{64,0},{80,16},{96,32},{112,48},{1... | collective-permute-start | bytes 12296 | tf_op jit(solution)/shard_map/ppermute | solution.py:18
  71.0 2.5 %collective-permute-done.17 = f32[8,128]{1,0:T(8,128)S(1)} collective-permute-done((f32[8,128]{1,0:T(8,128)S(1)}, f32[8,128]{1,0:T(8,128)S(1)}, u32[]{:S(2)}, u32[]{:S(2)}) %collective-permute-start.17) | collective-permute-done | bytes 4128 | tf_op jit(solution)/shard_map/ppermute | solution.py:18
  73.6 1.0 %collective-permute-start.18 = (f32[8,128]{1,0:T(8,128)S(1)}, f32[8,128]{1,0:T(8,128)S(1)}, u32[]{:S(2)}, u32[]{:S(2)}) collective-permute-start(f32[8,128]{1,0:T(8,128)S(1)} %add.13), channel_id=1, source_target_pairs={{0,32},{16,48},{32,0},{48,16},{64,96},{80,112},{96,64},{112,80},{1... | collective-permute-start | bytes 12296 | tf_op jit(solution)/shard_map/ppermute | solution.py:18
  74.6 2.6 %collective-permute-done.18 = f32[8,128]{1,0:T(8,128)S(1)} collective-permute-done((f32[8,128]{1,0:T(8,128)S(1)}, f32[8,128]{1,0:T(8,128)S(1)}, u32[]{:S(2)}, u32[]{:S(2)}) %collective-permute-start.18) | collective-permute-done | bytes 4128 | tf_op jit(solution)/shard_map/ppermute | solution.py:18
  77.2 1.3 %collective-permute-start.19 = (f32[8,128]{1,0:T(8,128)S(1)}, f32[8,128]{1,0:T(8,128)S(1)}, u32[]{:S(2)}, u32[]{:S(2)}) collective-permute-start(f32[8,128]{1,0:T(8,128)S(1)} %add.14), channel_id=1, source_target_pairs={{0,16},{16,0},{32,48},{48,32},{64,80},{80,64},{96,112},{112,96},{1... | collective-permute-start | bytes 12296 | tf_op jit(solution)/shard_map/ppermute | solution.py:18
  78.4 2.3 %collective-permute-done.19 = f32[8,128]{1,0:T(8,128)S(1)} collective-permute-done((f32[8,128]{1,0:T(8,128)S(1)}, f32[8,128]{1,0:T(8,128)S(1)}, u32[]{:S(2)}, u32[]{:S(2)}) %collective-permute-start.19) | collective-permute-done | bytes 4128 | tf_op jit(solution)/shard_map/ppermute | solution.py:18
  80.8 0.6 fusion
  82.7 0.0 collective-permute-done.20.p1
  82.7 0.0 collective-permute-done.21.p2
  82.7 0.0 collective-permute-done.22.p3
  82.7 0.0 collective-permute-done.23.py
  82.7 0.0 copy-done.1
  82.7 1.6 %grad.1 = (bf16[256,768]{1,0:T(8,128)(2,1)}, bf16[256,768]{1,0:T(8,128)(2,1)}) custom-call(f32[1]{0:T(128)S(6)} %copy.8.scale, bf16[256,768]{1,0:T(8,128)(2,1)S(1)} %copy-done.1, bf16[256,768]{1,0:T(8,128)(2,1)S(1)} %copy-done.3, f32[256,768]{1,0:T(8,128)S(1)} %get-tuple-element.66.img_back, f32[256,768]{1,0:T(8,128)S(1)} %get-tuple-element.67.txt_back, ...), custom_call_target="tpu_custom_call" | custom-call | tf_op jit(solution)/shard_map/grad/pallas_call | solution.py:23
  (11 shorter events, 0.1 us)
Async XLA Ops:
  0.6 12.7 %collective-permute-start.3 = (bf16[256,768]{1,0:T(8,128)(2,1)}, bf16[256,768]{1,0:T(8,128)(2,1)S(1)}, u32[]{:S(2)}, u32[]{:S(2)}) collective-permute-start(bf16[256,768]{1,0:T(8,128)(2,1)} %text.1), channel_id=1, source_target_pairs={{0,2},{1,3},{2,0},{3,1},{4,6},{5,7},{6,4},{7,5},{8,10},{9,11},{10,... | collective-permute-start | bytes 1179656 | tf_op jit(solution)/shard_map/ppermute | solution.py:18
  2.8 10.5 %collective-permute-start = (bf16[256,768]{1,0:T(8,128)(2,1)}, bf16[256,768]{1,0:T(8,128)(2,1)S(1)}, u32[]{:S(2)}, u32[]{:S(2)}) collective-permute-start(bf16[256,768]{1,0:T(8,128)(2,1)} %image.1), channel_id=1, source_target_pairs={{0,4},{1,5},{2,6},{3,7},{4,0},{5,1},{6,2},{7,3},{8,12},{9,13},{10,... | collective-permute-start | bytes 1179656 | tf_op jit(solution)/shard_map/ppermute | solution.py:18
  2.8 11.5 %collective-permute-start.1 = (bf16[256,768]{1,0:T(8,128)(2,1)}, bf16[256,768]{1,0:T(8,128)(2,1)S(1)}, u32[]{:S(2)}, u32[]{:S(2)}) collective-permute-start(bf16[256,768]{1,0:T(8,128)(2,1)} %image.1), channel_id=1, source_target_pairs={{0,12},{1,13},{2,14},{3,15},{4,8},{5,9},{6,10},{7,11},{8,4},{9,5},... | collective-permute-start | bytes 1179656 | tf_op jit(solution)/shard_map/ppermute | solution.py:18
  4.6 13.0 %collective-permute-start.2 = (bf16[256,768]{1,0:T(8,128)(2,1)}, bf16[256,768]{1,0:T(8,128)(2,1)S(1)}, u32[]{:S(2)}, u32[]{:S(2)}) collective-permute-start(bf16[256,768]{1,0:T(8,128)(2,1)} %text.1), channel_id=1, source_target_pairs={{0,1},{1,0},{2,3},{3,2},{4,5},{5,4},{6,7},{7,6},{8,9},{9,8},{10,11... | collective-permute-start | bytes 1179656 | tf_op jit(solution)/shard_map/ppermute | solution.py:18
  13.3 9.8 %collective-permute-start.4 = (bf16[256,768]{1,0:T(8,128)(2,1)S(1)}, bf16[256,768]{1,0:T(8,128)(2,1)S(1)}, u32[]{:S(2)}, u32[]{:S(2)}) collective-permute-start(bf16[256,768]{1,0:T(8,128)(2,1)S(1)} %collective-permute-done.3.t2), channel_id=1, source_target_pairs={{0,1},{1,0},{2,3},{3,2},{4,5},{5,4},{6,7},{7,6},{8,9},{9,8},{10,11... | collective-permute-start | bytes 1179656 | tf_op jit(solution)/shard_map/ppermute | solution.py:18
  14.3 9.8 %collective-permute-start.5 = (bf16[128,768]{1,0:T(8,128)(2,1)S(1)}, bf16[128,768]{1,0:T(8,128)(2,1)S(1)}, u32[]{:S(2)}, u32[]{:S(2)}) collective-permute-start(bf16[128,768]{1,0:T(8,128)(2,1)S(1)} %get-tuple-element.45), channel_id=1, source_target_pairs={{0,4},{1,5},{2,6},{3,7},{4,0},{5,1},{6,2},{7,3},{8,12},{9,13},{10,... | collective-permute-start | bytes 589832 | tf_op jit(solution)/shard_map/ppermute | solution.py:18
  14.9 9.3 %collective-permute-start.6 = (bf16[128,768]{1,0:T(8,128)(2,1)S(1)}, bf16[128,768]{1,0:T(8,128)(2,1)S(1)}, u32[]{:S(2)}, u32[]{:S(2)}) collective-permute-start(bf16[128,768]{1,0:T(8,128)(2,1)S(1)} %get-tuple-element.46), channel_id=1, source_target_pairs={{0,12},{1,13},{2,14},{3,15},{4,8},{5,9},{6,10},{7,11},{8,4},{9,5},... | collective-permute-start | bytes 589832 | tf_op jit(solution)/shard_map/ppermute | solution.py:18
  17.7 1.0 %copy-start = (bf16[256,768]{1,0:T(8,128)(2,1)S(1)}, bf16[256,768]{1,0:T(8,128)(2,1)}, u32[]{:S(2)}) copy-start(bf16[256,768]{1,0:T(8,128)(2,1)} %image.1) | copy-start | bytes 1179652
  18.7 1.0 %copy-start.2 = (bf16[256,768]{1,0:T(8,128)(2,1)S(1)}, bf16[256,768]{1,0:T(8,128)(2,1)}, u32[]{:S(2)}) copy-start(bf16[256,768]{1,0:T(8,128)(2,1)} %text.1) | copy-start | bytes 1179652
  19.7 0.7 copy-start.4
  24.2 13.3 %copy-start.5 = (s32[256]{0:T(256)S(1)}, s32[256]{0:T(256)}, u32[]{:S(2)}) copy-start(s32[256]{0:T(256)} %param.6) | copy-start | bytes 3076
  25.3 3.8 %collective-permute-start.7 = (f32[4,1024]{1,0:T(4,128)S(1)}, f32[4,1024]{1,0:T(4,128)S(1)}, u32[]{:S(2)}, u32[]{:S(2)}) collective-permute-start(f32[4,1024]{1,0:T(4,128)S(1)} %get-tuple-element.51.row_a), channel_id=1, source_target_pairs={{0,4},{1,5},{2,6},{3,7},{4,0},{5,1},{6,2},{7,3},{8,12},{9,13},{10,... | collective-permute-start | bytes 49160 | tf_op jit(solution)/shard_map/ppermute | solution.py:18
  26.4 2.8 %collective-permute-start.8 = (f32[4,1024]{1,0:T(4,128)S(1)}, f32[4,1024]{1,0:T(4,128)S(1)}, u32[]{:S(2)}, u32[]{:S(2)}) collective-permute-start(f32[4,1024]{1,0:T(4,128)S(1)} %get-tuple-element.52.col_a), channel_id=1, source_target_pairs={{0,1},{1,0},{2,3},{3,2},{4,5},{5,4},{6,7},{7,6},{8,9},{9,8},{10,11... | collective-permute-start | bytes 49160 | tf_op jit(solution)/shard_map/ppermute | solution.py:18
  29.2 5.3 %collective-permute-start.10 = (f32[4,1024]{1,0:T(4,128)S(1)}, f32[4,1024]{1,0:T(4,128)S(1)}, u32[]{:S(2)}, u32[]{:S(2)}) collective-permute-start(f32[4,1024]{1,0:T(4,128)S(1)} %get-tuple-element.54.col_a), channel_id=1, source_target_pairs={{0,2},{1,3},{2,0},{3,1},{4,6},{5,7},{6,4},{7,5},{8,10},{9,11},{10,... | collective-permute-start | bytes 49160 | tf_op jit(solution)/shard_map/ppermute | solution.py:18
  32.1 5.2 %collective-permute-start.9 = (f32[4,1024]{1,0:T(4,128)S(1)}, f32[4,1024]{1,0:T(4,128)S(1)}, u32[]{:S(2)}, u32[]{:S(2)}) collective-permute-start(f32[4,1024]{1,0:T(4,128)S(1)} %get-tuple-element.53.row_a), channel_id=1, source_target_pairs={{0,8},{1,9},{2,10},{3,11},{4,12},{5,13},{6,14},{7,15},{8,0},{9,1},... | collective-permute-start | bytes 49160 | tf_op jit(solution)/shard_map/ppermute | solution.py:18
  39.6 11.6 %collective-permute-start.13 = (bf16[512,768]{1,0:T(8,128)(2,1)S(1)}, bf16[512,768]{1,0:T(8,128)(2,1)S(1)}, u32[]{:S(2)}, u32[]{:S(2)}) collective-permute-start(bf16[512,768]{1,0:T(8,128)(2,1)S(1)} %get-tuple-element.62), channel_id=1, source_target_pairs={{0,1},{1,0},{2,3},{3,2},{4,5},{5,4},{6,7},{7,6},{8,9},{9,8},{10,11... | collective-permute-start | bytes 2359304 | tf_op jit(solution)/shard_map/ppermute | solution.py:18
  39.7 2.3 %collective-permute-start.11 = (f32[8,128]{1,0:T(8,128)S(1)}, f32[8,128]{1,0:T(8,128)S(1)}, u32[]{:S(2)}, u32[]{:S(2)}) collective-permute-start(f32[8,128]{1,0:T(8,128)S(1)} %get-tuple-element.59.row_a), channel_id=1, source_target_pairs={{0,1},{1,0},{2,3},{3,2},{4,5},{5,4},{6,7},{7,6},{8,9},{9,8},{10,11... | collective-permute-start | bytes 12296 | tf_op jit(solution)/shard_map/ppermute | solution.py:18
  40.2 3.6 %collective-permute-start.12 = (f32[8,128]{1,0:T(8,128)S(1)}, f32[8,128]{1,0:T(8,128)S(1)}, u32[]{:S(2)}, u32[]{:S(2)}) collective-permute-start(f32[8,128]{1,0:T(8,128)S(1)} %get-tuple-element.60.col_a), channel_id=1, source_target_pairs={{0,4},{1,5},{2,6},{3,7},{4,0},{5,1},{6,2},{7,3},{8,12},{9,13},{10,... | collective-permute-start | bytes 12296 | tf_op jit(solution)/shard_map/ppermute | solution.py:18
  45.2 5.2 %collective-permute-start.14 = (f32[8,128]{1,0:T(8,128)S(1)}, f32[8,128]{1,0:T(8,128)S(1)}, u32[]{:S(2)}, u32[]{:S(2)}) collective-permute-start(f32[8,128]{1,0:T(8,128)S(1)} %get-tuple-element.63.row_a), channel_id=1, source_target_pairs={{0,2},{1,3},{2,0},{3,1},{4,6},{5,7},{6,4},{7,5},{8,10},{9,11},{10,... | collective-permute-start | bytes 12296 | tf_op jit(solution)/shard_map/ppermute | solution.py:18
  46.1 5.1 %collective-permute-start.15 = (f32[8,128]{1,0:T(8,128)S(1)}, f32[8,128]{1,0:T(8,128)S(1)}, u32[]{:S(2)}, u32[]{:S(2)}) collective-permute-start(f32[8,128]{1,0:T(8,128)S(1)} %get-tuple-element.64.col_a), channel_id=1, source_target_pairs={{0,8},{1,9},{2,10},{3,11},{4,12},{5,13},{6,14},{7,15},{8,0},{9,1},... | collective-permute-start | bytes 12296 | tf_op jit(solution)/shard_map/ppermute | solution.py:18
  51.2 31.5 %copy-start.1 = (bf16[256,768]{1,0:T(8,128)(2,1)S(1)}, bf16[256,768]{1,0:T(8,128)(2,1)}, u32[]{:S(2)}) copy-start(bf16[256,768]{1,0:T(8,128)(2,1)} %image.1) | copy-start | bytes 1179652
  51.2 31.5 %copy-start.3 = (bf16[256,768]{1,0:T(8,128)(2,1)S(1)}, bf16[256,768]{1,0:T(8,128)(2,1)}, u32[]{:S(2)}) copy-start(bf16[256,768]{1,0:T(8,128)(2,1)} %text.1) | copy-start | bytes 1179652
  52.7 30.0 %collective-permute-start.20 = (bf16[256,768]{1,0:T(8,128)(2,1)S(1)}, bf16[256,768]{1,0:T(8,128)(2,1)S(1)}, u32[]{:S(2)}, u32[]{:S(2)}) collective-permute-start(bf16[256,768]{1,0:T(8,128)(2,1)S(1)} %get-tuple-element.68), channel_id=1, source_target_pairs={{0,4},{1,5},{2,6},{3,7},{4,0},{5,1},{6,2},{7,3},{8,12},{9,13},{10,... | collective-permute-start | bytes 1179656 | tf_op jit(solution)/shard_map/ppermute | solution.py:18
  53.7 29.0 %collective-permute-start.21 = (bf16[256,768]{1,0:T(8,128)(2,1)S(1)}, bf16[256,768]{1,0:T(8,128)(2,1)S(1)}, u32[]{:S(2)}, u32[]{:S(2)}) collective-permute-start(bf16[256,768]{1,0:T(8,128)(2,1)S(1)} %get-tuple-element.69), channel_id=1, source_target_pairs={{0,8},{1,9},{2,10},{3,11},{4,12},{5,13},{6,14},{7,15},{8,0},{9,1},... | collective-permute-start | bytes 1179656 | tf_op jit(solution)/shard_map/ppermute | solution.py:18
  55.4 27.3 %collective-permute-start.22 = (bf16[256,768]{1,0:T(8,128)(2,1)S(1)}, bf16[256,768]{1,0:T(8,128)(2,1)S(1)}, u32[]{:S(2)}, u32[]{:S(2)}) collective-permute-start(bf16[256,768]{1,0:T(8,128)(2,1)S(1)} %get-tuple-element.70), channel_id=1, source_target_pairs={{0,12},{1,13},{2,14},{3,15},{4,8},{5,9},{6,10},{7,11},{8,4},{9,5},... | collective-permute-start | bytes 1179656 | tf_op jit(solution)/shard_map/ppermute | solution.py:18
  57.5 25.2 %collective-permute-start.23 = (bf16[256,768]{1,0:T(8,128)(2,1)S(1)}, bf16[256,768]{1,0:T(8,128)(2,1)S(1)}, u32[]{:S(2)}, u32[]{:S(2)}) collective-permute-start(bf16[256,768]{1,0:T(8,128)(2,1)S(1)} %get-tuple-element.71), channel_id=1, source_target_pairs={{0,2},{1,3},{2,0},{3,1},{4,6},{5,7},{6,4},{7,5},{8,10},{9,11},{10,... | collective-permute-start | bytes 1179656 | tf_op jit(solution)/shard_map/ppermute | solution.py:18
  60.3 8.8 %collective-permute-start.16 = (f32[8,128]{1,0:T(8,128)S(1)}, f32[8,128]{1,0:T(8,128)S(1)}, u32[]{:S(2)}, u32[]{:S(2)}) collective-permute-start(f32[8,128]{1,0:T(8,128)S(1)} %get-tuple-element.65), channel_id=1, source_target_pairs={{0,128},{16,144},{32,160},{48,176},{64,192},{80,208},{96,224},{112... | collective-permute-start | bytes 12296 | tf_op jit(solution)/shard_map/ppermute | solution.py:18
  69.0 4.5 %collective-permute-start.17 = (f32[8,128]{1,0:T(8,128)S(1)}, f32[8,128]{1,0:T(8,128)S(1)}, u32[]{:S(2)}, u32[]{:S(2)}) collective-permute-start(f32[8,128]{1,0:T(8,128)S(1)} %add.12), channel_id=1, source_target_pairs={{0,64},{16,80},{32,96},{48,112},{64,0},{80,16},{96,32},{112,48},{1... | collective-permute-start | bytes 12296 | tf_op jit(solution)/shard_map/ppermute | solution.py:18
  73.6 3.6 %collective-permute-start.18 = (f32[8,128]{1,0:T(8,128)S(1)}, f32[8,128]{1,0:T(8,128)S(1)}, u32[]{:S(2)}, u32[]{:S(2)}) collective-permute-start(f32[8,128]{1,0:T(8,128)S(1)} %add.13), channel_id=1, source_target_pairs={{0,32},{16,48},{32,0},{48,16},{64,96},{80,112},{96,64},{112,80},{1... | collective-permute-start | bytes 12296 | tf_op jit(solution)/shard_map/ppermute | solution.py:18
  77.2 3.6 %collective-permute-start.19 = (f32[8,128]{1,0:T(8,128)S(1)}, f32[8,128]{1,0:T(8,128)S(1)}, u32[]{:S(2)}, u32[]{:S(2)}) collective-permute-start(f32[8,128]{1,0:T(8,128)S(1)} %add.14), channel_id=1, source_target_pairs={{0,16},{16,0},{32,48},{48,32},{64,80},{80,64},{96,112},{112,96},{1... | collective-permute-start | bytes 12296 | tf_op jit(solution)/shard_map/ppermute | solution.py:18

commit v3 on v2

v3 whole, which is shorter than its diff:
```python
import functools
import itertools
import math

import jax
import jax.numpy as jnp
from jax import lax
from jax.experimental import pallas as pl
from jax.experimental.pallas import tpu as pltpu
from jax.sharding import PartitionSpec as P

EPSILON = 1e-06
VMEM = pl.BlockSpec(memory_space=pltpu.VMEM)
SMEM = pl.BlockSpec(memory_space=pltpu.SMEM)
PARAMS = pltpu.CompilerParams(vmem_limit_bytes=24 * 1024 * 1024)
SLOTS = 4
LOW = -1e30
COST = {
    "pick": 5.0,
    "own": 0.25, "first": 2.4, "second": 1.05, "third": 1.15, "lse": 0.15, "weight": 1.3,
    "image": 1.1, "text": 1.1, "early": 1.4, "away": 0.3, "grad": 1.6,
}
NEAR = (0, 1, 3)
X1, X2, X3, Y, CORE = 4, 8, 12, 2, 1


def swapped(value, bits, axis="blk"):
    return lax.ppermute(value, axis, [(i, i ^ bits) for i in range(lax.axis_size(axis))])


def moved(value, step):
    places = itertools.product(range(8), range(2), range(4), range(2), range(2))
    flat = lambda z, lo, x, hi, core: (z % 8 * 2 + lo) * 16 + x * 4 + hi * 2 + core
    pairs = [(flat(*p), flat(*step(*p))) for p in places]
    return lax.ppermute(value, ("dp", "blk"), pairs)


def by_sides(z, lo, x, hi, core):
    return (z, 1 - lo, x, 1 - hi, core) if core == 0 else (z, lo, 3 - x, hi, core)


def relay(z, lo, x, hi, core):
    return (z, lo, x ^ 1 if core == 0 else 3 - x, hi, core)


def by_planes(z, lo, x, hi, core):
    return (z + (1 if (z + core) % 2 == 0 else -1), lo, x, hi, core)


def by_far_planes(z, lo, x, hi, core):
    return (z + (-3 if core == 0 else 3), lo, x, hi, core)


def call(kernel, name, outs, *args, scalar=False):
    specs = [SMEM] * scalar + [VMEM] * (len(args) - scalar)
    moved = sum(a.size * a.dtype.itemsize for a in args)
    moved += sum(math.prod(s) * jnp.dtype(d).itemsize for s, d in outs)
    return pl.pallas_call(
        kernel, out_shape=[jax.ShapeDtypeStruct(s, d) for s, d in outs], in_specs=specs,
        out_specs=[VMEM] * len(outs), name=name,
        cost_estimate=pl.CostEstimate(
            flops=int(COST.get(name, 0.05) * 1.1e9), bytes_accessed=moved, transcendentals=0
        ),
        compiler_params=PARAMS,
    )(*args)


def eye(n):
    return lax.broadcasted_iota(jnp.int32, (n, n), 0) == lax.broadcasted_iota(jnp.int32, (n, n), 1)


def to_row(column, diagonal):
    return jnp.sum(jnp.where(diagonal, column, 0.0), axis=0, keepdims=True)


def to_column(row, diagonal):
    return jnp.sum(jnp.where(diagonal, row, 0.0), axis=1, keepdims=True)


def unit_rows(values):
    wide = values.astype(jnp.float32)
    inverse = lax.rsqrt(jnp.sum(wide * wide, axis=-1, keepdims=True) + EPSILON)
    return wide * inverse, inverse


def hits(positive, diagonal):
    target = to_column(positive[...].astype(jnp.float32), diagonal).astype(jnp.int32)
    return lax.broadcasted_iota(jnp.int32, diagonal.shape, 1) == target


def merged(a, b):
    top = jnp.maximum(a[0], b[0])
    ea, eb = jnp.exp(a[0] - top), jnp.exp(b[0] - top)
    both = ea + eb
    return top + jnp.log(both), (a[1] * ea + b[1] * eb) / both


def into(part, span, value):
    part[0:1, span], part[1:2, span] = merged((part[0:1, span], part[1:2, span]), value)


def stats(scale, imgs, txts, logits, row_part, col_part):
    diagonal = eye(next(iter(txts.values())).shape[0])
    rows = diagonal.shape[0]
    slots, blocks = tuple(imgs), tuple(txts)
    at = lambda k: pl.ds(k * rows, rows)
    row_top, col_top = {}, {}
    for l in blocks:
        for k in slots:
            tile = scale * lax.dot_general(
                imgs[k][...], txts[l][...], (((1,), (1,)), ((), ())),
                preferred_element_type=jnp.float32,
            )
            logits[k, l][...] = tile
            right = jnp.max(tile, axis=1, keepdims=True)
            down = jnp.max(tile, axis=0, keepdims=True)
            row_top[k] = jnp.maximum(row_top[k], right) if k in row_top else right
            col_top[l] = jnp.maximum(col_top[l], down) if l in col_top else down
    none = jnp.zeros((1, rows), jnp.float32)
    col_sum, col_moment = {l: none for l in blocks}, {l: none for l in blocks}
    for k in slots:
        total = jnp.zeros((rows, 1), jnp.float32)
        moment = jnp.zeros((rows, 1), jnp.float32)
        for l in blocks:
            tile = logits[k, l][...]
            e = jnp.exp(tile - row_top[k])
            total += jnp.sum(e, axis=1, keepdims=True)
            moment += jnp.sum(e * tile, axis=1, keepdims=True)
            f = jnp.exp(tile - col_top[l])
            col_sum[l] += jnp.sum(f, axis=0, keepdims=True)
            col_moment[l] += jnp.sum(f * tile, axis=0, keepdims=True)
        total = to_row(total, diagonal)
        top = to_row(row_top[k], diagonal)
        into(row_part, at(k), (top + jnp.log(total), to_row(moment, diagonal) / total))
    for l in blocks:
        into(col_part, at(l), (col_top[l] + jnp.log(col_sum[l]), col_moment[l] / col_sum[l]))


def unit(values):
    return unit_rows(values[...])[0].astype(jnp.bfloat16)


def views(ref, slots, rows):
    return {k: ref.at[pl.ds(n * rows, rows), :] for n, k in enumerate(slots)}


def tiles(ref, slots, blocks, rows):
    return {
        (k, l): ref.at[pl.ds(n * rows, rows), pl.ds(m * rows, rows)]
        for n, k in enumerate(slots) for m, l in enumerate(blocks)
    }


def own_kernel(image, text, img_unit, txt_unit):
    img_unit[...] = unit(image)
    txt_unit[...] = unit(text)


def first_kernel(
    scale, i0, t0, i1, i3, t1, t2, positive, near, txts, logits, row_part, col_part
):
    rows = i0.shape[0]
    imgs, texts = views(near, NEAR, rows), views(txts, (0, 1, 2), rows)
    imgs[0][...] = i0[...]
    texts[0][...] = t0[...]
    imgs[1][...], imgs[3][...] = unit(i1), unit(i3)
    texts[1][...], texts[2][...] = unit(t1), unit(t2)
    for part in (row_part, col_part):
        part[0:1, :] = jnp.full((1, SLOTS * rows), LOW, jnp.float32)
        part[1:4, :] = jnp.zeros((3, SLOTS * rows), jnp.float32)
    scores = tiles(logits, NEAR, (0, 1, 2), rows)
    stats(scale[0], imgs, texts, scores, row_part, col_part)
    matched = jnp.where(hits(positive, eye(rows)), scores[0, 0][...], 0.0)
    row_part[2:3, pl.ds(0, rows)] = jnp.sum(matched, axis=0, keepdims=True)


def core_index():
    return lax.axis_index("blk") % 2


def pick_kernel(i1, i3, before, out):
    core = core_index()

    @pl.when(core == 0)
    def _():
        out[...] = i3[...]

    @pl.when(core != 0)
    def _():
        out[...] = i1[...]


def second_kernel(scale, t3, near, txts_in, row_in, col_in, txts, logits, row_part, col_part):
    rows = t3.shape[0]
    row_part[...] = row_in[...]
    col_part[...] = col_in[...]
    txts[pl.ds(0, 3 * rows), :] = txts_in[...]
    last = txts.at[pl.ds(3 * rows, rows), :]
    last[...] = unit(t3)
    scores = tiles(logits, NEAR, (3,), rows)
    stats(scale[0], views(near, NEAR, rows), {3: last}, scores, row_part, col_part)


def third_kernel(scale, i2, txts, row_in, col_in, far, logits, row_part, col_part):
    rows = i2.shape[0]
    row_part[...] = row_in[...]
    col_part[...] = col_in[...]
    far[...] = unit(i2)
    blocks = range(SLOTS)
    scores = tiles(logits, (2,), blocks, rows)
    stats(scale[0], {2: far}, views(txts, blocks, rows), scores, row_part, col_part)


def joined(mine, other, bits):
    rows = mine.shape[1] // SLOTS
    swap = lambda at: jnp.concatenate(
        [other[at : at + 1, (k ^ bits) * rows : ((k ^ bits) + 1) * rows] for k in range(SLOTS)],
        axis=1,
    )
    value, mean = merged((mine[0:1, :], mine[1:2, :]), (swap(0), swap(1)))
    return value, mean, mine[2:3, :] + swap(2)


def join_kernel(mine, other, before, out):
    out[0:1, :], out[1:2, :], out[2:3, :] = joined(mine, other, 1)
    out[3:4, :] = jnp.zeros((1, out.shape[1]), jnp.float32)


def slot_sum(v):
    rows = v.shape[1] // SLOTS
    at = [jnp.sum(v[:, k * rows : (k + 1) * rows], axis=1, keepdims=True) for k in range(SLOTS)]
    return (at[0] + at[1]) + (at[2] + at[3])


def lse_kernel(row, row3, col, col2, lse, row_sums, col_sums):
    lane = lax.broadcasted_iota(jnp.int32, row_sums.shape, 1)
    sides = ((joined(row, row3, 3), row_sums), (joined(col, col2, 2), col_sums))
    for at, ((value, mean, matched), out) in enumerate(sides):
        lse[at : at + 1, :] = value
        loss, slope = slot_sum(0.5 * value - matched), slot_sum(0.5 * mean - matched)
        out[...] = jnp.where(lane == 0, loss, jnp.where(lane == 1, slope, 0.0))


def weigh(scores, lse, slots, w, hit=None):
    rows = lse.shape[1] // SLOTS
    diagonal = eye(rows)
    at = lambda k: pl.ds(k * rows, rows)
    for k in slots:
        right = to_column(lse[0:1, at(k)], diagonal)
        for l in range(SLOTS):
            tile = scores[k, l][...]
            weight = 0.5 * (jnp.exp(tile - right) + jnp.exp(tile - lse[1:2, at(l)]))
            if k == 0 and l == 0:
                weight = weight - hit.astype(jnp.float32)
            w[k, l][...] = weight.astype(jnp.bfloat16)


def over(w01, w23, near, far, l):
    rows = far.shape[0]
    span = pl.ds(l * rows, rows)
    term = lambda weights, blocks: lax.dot_general(
        weights, blocks, (((0,), (0,)), ((), ())), preferred_element_type=jnp.float32
    )
    one, two = pl.ds(0, rows), pl.ds(rows, rows)
    return (
        term(w01[:, span], near[pl.ds(0, 2 * rows), :])
        + term(w23[one, span], far[...])
        + term(w23[two, span], near[pl.ds(2 * rows, rows), :])
    )


def weight_kernel(first, second, third, lse, positive, w01, w23):
    rows = w01.shape[0] // 2
    scores = tiles(first, NEAR, (0, 1, 2), rows)
    scores.update(tiles(second, NEAR, (3,), rows))
    scores.update(tiles(third, (2,), range(SLOTS), rows))
    hit = hits(positive, eye(rows))
    weigh(scores, lse, (2, 3), tiles(w23, (2, 3), range(SLOTS), rows))
    weigh(scores, lse, (0, 1), tiles(w01, (0, 1), range(SLOTS), rows), hit)


def early_kernel(w01, w23, near, far, txts, before, core_part, part2):
    rows = far.shape[0]
    back = jnp.dot(w23[pl.ds(0, rows), :], txts[...], preferred_element_type=jnp.float32)
    part2[...] = back.astype(part2.dtype)
    for n, l in enumerate((1, 3)):
        core_part[pl.ds(n * rows, rows), :] = over(w01, w23, near, far, l).astype(core_part.dtype)


def image_kernel(w01, w23, txts, img_back, part1, part3, token):
    rows = img_back.shape[0]
    token[...] = jnp.zeros(token.shape, jnp.float32)
    for w, n, out in ((w01, 1, part1), (w23, 1, part3), (w01, 0, img_back)):
        out[...] = jnp.dot(w[pl.ds(n * rows, rows), :], txts[...], preferred_element_type=jnp.float32)


def text_kernel(w01, w23, near, far, before, txt_back, txt_next, token):
    token[...] = jnp.zeros(token.shape, jnp.float32)
    for out, l in ((txt_back, 0), (txt_next, 2)):
        out[...] = over(w01, w23, near, far, l)


def away_kernel(wide1, wide3, txt_next, relayed, core_part, before, part1, part3, part_y):
    rows = part1.shape[0]
    passed = relayed[...].astype(jnp.float32)
    zero = core_index() == 0
    part3[...] = (wide3[...] + jnp.where(zero, passed, 0.0)).astype(part3.dtype)
    part1[...] = (wide1[...] + jnp.where(zero, 0.0, passed)).astype(part1.dtype)
    total = txt_next[...] + core_part[pl.ds(rows, rows), :].astype(jnp.float32)
    part_y[...] = total.astype(part_y.dtype)


def half_kernel(row, row_core, col, col1, before, out):
    out[...] = jnp.where(core_index() == 0, row[...] + row_core[...], col[...] + col1[...])


def side_kernel(a, b, before, out):
    out[...] = a[...] + b[...]


def add_kernel(a, b, out):
    out[...] = a[...] + b[...]


def lane_from_z(shape):
    lane = lax.broadcasted_iota(jnp.int32, shape, 1)
    return (lane - lax.axis_index("dp") // 2 + 8) % 8, lane < 8


def total_kernel(mine, other, held):
    sums = mine[0:1, :] + other[0:1, :]
    line = lax.broadcasted_iota(jnp.int32, held.shape, 0)
    value = jnp.where(line == 0, sums[:, 0:1], jnp.where(line == 1, sums[:, 1:2], 0.0))
    ahead, inside = lane_from_z(held.shape)
    held[...] = jnp.where(inside & (ahead == 0), value, 0.0)


def union(held, other, both):
    ahead, _ = lane_from_z(held.shape)
    twice = functools.reduce(jnp.logical_or, [ahead == n for n in both])
    return jnp.where(twice, held[...], held[...] + other[...])


def planes_kernel(held, other, out):
    out[...] = union(held, other, (0,))


def scalar_kernel(total_rows, scale, held, other, before, loss, scale_grad):
    sums = jnp.sum(union(held, other, (0, 1, 4, 7)), axis=1, keepdims=True)
    loss[0] = sums[0, 0] / total_rows
    scale_grad[0] = sums[1, 0] / (total_rows * scale[0])


def grad_kernel(scale, image, text, img_back, txt_back, core_part, p1, p3, py, image_grad, text_grad, token):
    token[...] = jnp.zeros(token.shape, jnp.float32)
    for values, parts, out in (
        (image, (img_back, p1, p3), image_grad), (text, (txt_back, core_part, py), text_grad),
    ):
        direction, inverse = unit_rows(values[...])
        incoming = scale[0] * sum(
            part[pl.ds(0, direction.shape[0]), :].astype(jnp.float32) for part in parts
        )
        along = jnp.sum(direction * incoming, axis=-1, keepdims=True)
        out[...] = ((incoming - direction * along) * inverse).astype(out.dtype)


def shards(image, text, positive, logit_scale):
    rows, width = image.shape
    group = SLOTS * rows
    f32, bf16 = jnp.float32, jnp.bfloat16
    block, parts = ((rows, width), bf16), ((SLOTS, group), f32)
    positive = positive.reshape(1, rows)

    i1, i3 = swapped(image, X1), swapped(image, X3)
    t1, t2 = swapped(text, CORE), swapped(text, Y)
    own_img, own_txt = call(own_kernel, "own", [block] * 2, image, text)
    (on,) = call(pick_kernel, "pick", [block], i1, i3, own_img)
    i2 = moved(on, relay)
    t3 = swapped(t2, CORE)
    three = group - rows
    near, txts, first, row_part, col_part = call(
        first_kernel, "first", [((three, width), bf16)] * 2 + [((three, three), f32), parts, parts],
        logit_scale, own_img, own_txt, i1, i3, t1, t2, positive, scalar=True,
    )
    txts, second, row_part, col_part = call(
        second_kernel, "second", [((group, width), bf16), ((three, rows), f32), parts, parts],
        logit_scale, t3, near, txts, row_part, col_part, scalar=True,
    )
    few = ((8, 128), f32)
    far, third, row_part, col_part = call(
        third_kernel, "third", [block, ((rows, group), f32), parts, parts],
        logit_scale, i2, txts, row_part, col_part, scalar=True,
    )
    (col_part,) = call(join_kernel, "join", [parts], col_part, swapped(col_part, CORE), col_part)
    col_y = swapped(col_part, Y)
    (row_part,) = call(join_kernel, "join", [parts], row_part, swapped(row_part, X1), col_y)
    lse, row_sums, col_sums = call(
        lse_kernel, "lse", [((2, group), f32), few, few],
        row_part, swapped(row_part, X3), col_part, col_y,
    )
    row_core, col1 = swapped(row_sums, CORE), swapped(col_sums, X1)
    heavy = ((2 * rows, group), bf16)
    w01, w23 = call(
        weight_kernel, "weight", [heavy, heavy], first, second, third, lse, positive
    )
    wide = ((rows, width), f32)
    img_back, part1, part3, token = call(image_kernel, "image", [wide] * 3 + [few], w01, w23, txts)
    (sums,) = call(half_kernel, "half", [few], row_sums, row_core, col_sums, col1, token)
    core_part, part2 = call(
        early_kernel, "early", [((2 * rows, width), bf16), block], w01, w23, near, far, txts, sums
    )
    core_part, relayed = swapped(core_part, CORE), moved(part2, relay)
    txt_back, txt_next, token = call(
        text_kernel, "text", [wide] * 2 + [few], w01, w23, near, far, sums
    )
    (sums,) = call(side_kernel, "side", [few], sums, swapped(sums, 1, "dp"), token)
    (sums,) = call(add_kernel, "add", [few], sums, moved(sums, by_sides))
    (held,) = call(total_kernel, "total", [few], sums, swapped(sums, CORE))
    part1, part3, part_y = call(
        away_kernel, "away", [block] * 3, part1, part3, txt_next, relayed, core_part, held
    )
    part1, part3, part_y = swapped(part1, X1), swapped(part3, X3), swapped(part_y, Y)
    (held,) = call(add_kernel, "add", [few], held, moved(held, by_planes))
    (held,) = call(planes_kernel, "planes", [few], held, swapped(held, CORE))
    (held,) = call(add_kernel, "add", [few], held, moved(held, by_far_planes))
    image_grad, text_grad, token = call(
        grad_kernel, "grad", [block] * 2 + [few],
        logit_scale, image, text, img_back, txt_back, core_part, part1, part3, part_y, scalar=True,
    )
    total_rows = rows * lax.axis_size("blk") * lax.axis_size("dp")
    loss, scale_grad = pl.pallas_call(
        functools.partial(scalar_kernel, total_rows), name="scalar",
        out_shape=[jax.ShapeDtypeStruct((1,), f32)] * 2,
        in_specs=[SMEM, VMEM, VMEM, VMEM], out_specs=[SMEM] * 2,
        compiler_params=PARAMS,
    )(logit_scale, held, swapped(held, CORE), token)
    return (loss, scale_grad, image_grad, text_grad)


def solution(mesh):
    in_specs = (P(("dp", "blk"), None), P(("dp", "blk"), None), P(("dp", "blk")), P())
    out_specs = (P(), P(), P(("dp", "blk"), None), P(("dp", "blk"), None))
    return jax.shard_map(shards, mesh=mesh, in_specs=in_specs, out_specs=out_specs, check_vma=False)
```

time: 86.9 us -> 74.4 us (0.86)
  the two profiles are of different devices: /device:TPU:16 before, /device:TPU:1 now
where the time goes in v3:
time: 74.4 us; the launch traced here: 74.3 us
  starting transfers between devices  33.6 us (45%)
  waiting for transfers between devices  24.1 us (32%)
  Pallas kernels  13 us (17%)
  local copies, waits for them, and re-layouts  2.01 us (3%)
  between operations  1.64 us (2%)
    ppermute x19, starting transfers between devices, swapped(): lax.ppermute(value, axis, [(i, i ^ bits) for i in range(lax.axis_size(axi...  22 us
    ppermute x19, waiting for transfers between devices, swapped(): lax.ppermute(value, axis, [(i, i ^ bits) for i in range(lax.axis_size(axi...  14.4 us
    pallas_call x21, Pallas kernels, call(): pl.pallas_call(kernel, out_shape=[jax.ShapeDtypeStruct(s, d) for s, d in...  12.3 us
    ppermute x5, starting transfers between devices, moved(): return lax.ppermute(value, ('dp', 'blk'), pairs)  11.6 us
    ppermute x5, waiting for transfers between devices, moved(): return lax.ppermute(value, ('dp', 'blk'), pairs)  9.67 us
    unnamed x10, local copies, waits for them, and re-layouts  2.01 us
  transfers between devices with their start and end apart: 24, of which 14 were waited for; matrix products, arithmetic and copies ran while one was open for 0% of the time, Pallas kernels for 12%

profile of v3, /device:TPU:1, one launch (start us, length us, event | category | flops | bytes accessed | tf_op | source)
XLA Modules:
  0.0 74.3 jit_solution(15943037845237433728)
XLA Ops:
  0.6 3.8 %collective-permute-start.3 = (bf16[256,768]{1,0:T(8,128)(2,1)}, bf16[256,768]{1,0:T(8,128)(2,1)S(1)}, u32[]{:S(2)}, u32[]{:S(2)}) collective-permute-start(bf16[256,768]{1,0:T(8,128)(2,1)} %text.5), channel_id=1, source_target_pairs={{0,2},{1,3},{2,0},{3,1},{4,6},{5,7},{6,4},{7,5},{8,10},{9,11},{10,... | collective-permute-start | bytes 1179656 | tf_op jit(solution)/shard_map/ppermute | solution.py:28
  4.5 2.5 %collective-permute-start.1 = (bf16[256,768]{1,0:T(8,128)(2,1)}, bf16[256,768]{1,0:T(8,128)(2,1)S(1)}, u32[]{:S(2)}, u32[]{:S(2)}) collective-permute-start(bf16[256,768]{1,0:T(8,128)(2,1)} %image.5), channel_id=1, source_target_pairs={{0,12},{1,13},{2,14},{3,15},{4,8},{5,9},{6,10},{7,11},{8,4},{9,5},... | collective-permute-start | bytes 1179656 | tf_op jit(solution)/shard_map/ppermute | solution.py:28
  6.9 0.0 collective-permute-start
  6.9 1.5 %collective-permute-start.5 = (bf16[256,768]{1,0:T(8,128)(2,1)}, bf16[256,768]{1,0:T(8,128)(2,1)S(1)}, u32[]{:S(2)}, u32[]{:S(2)}) collective-permute-start(bf16[256,768]{1,0:T(8,128)(2,1)} %text.5), channel_id=1, source_target_pairs={{0,1},{1,0},{2,3},{3,2},{4,5},{5,4},{6,7},{7,6},{8,9},{9,8},{10,11... | collective-permute-start | bytes 1179656 | tf_op jit(solution)/shard_map/ppermute | solution.py:28
  8.4 1.0 %copy-done = bf16[256,768]{1,0:T(8,128)(2,1)S(1)} copy-done((bf16[256,768]{1,0:T(8,128)(2,1)S(1)}, bf16[256,768]{1,0:T(8,128)(2,1)}, u32[]{:S(2)}) %copy-start) | copy-done | bytes 393240
  9.4 1.0 %copy-done.2 = bf16[256,768]{1,0:T(8,128)(2,1)S(1)} copy-done((bf16[256,768]{1,0:T(8,128)(2,1)S(1)}, bf16[256,768]{1,0:T(8,128)(2,1)}, u32[]{:S(2)}) %copy-start.2) | copy-done | bytes 393240
  10.4 0.2 own.1
  10.6 1.9 %collective-permute-done.3.t2 = bf16[256,768]{1,0:T(8,128)(2,1)S(1)} collective-permute-done((bf16[256,768]{1,0:T(8,128)(2,1)}, bf16[256,768]{1,0:T(8,128)(2,1)S(1)}, u32[]{:S(2)}, u32[]{:S(2)}) %collective-permute-start.3) | collective-permute-done | bytes 393248 | tf_op jit(solution)/shard_map/ppermute | solution.py:28
  12.6 2.2 %collective-permute-start.4 = (bf16[256,768]{1,0:T(8,128)(2,1)S(1)}, bf16[256,768]{1,0:T(8,128)(2,1)S(1)}, u32[]{:S(2)}, u32[]{:S(2)}) collective-permute-start(bf16[256,768]{1,0:T(8,128)(2,1)S(1)} %collective-permute-done.3.t2), channel_id=1, source_target_pairs={{0,1},{1,0},{2,3},{3,2},{4,5},{5,4},{6,7},{7,6},{8,9},{9,8},{10,11... | collective-permute-start | bytes 1179656 | tf_op jit(solution)/shard_map/ppermute | solution.py:28
  14.7 0.8 %collective-permute-done.1.i3 = bf16[256,768]{1,0:T(8,128)(2,1)S(1)} collective-permute-done((bf16[256,768]{1,0:T(8,128)(2,1)}, bf16[256,768]{1,0:T(8,128)(2,1)S(1)}, u32[]{:S(2)}, u32[]{:S(2)}) %collective-permute-start.1) | collective-permute-done | bytes 393248 | tf_op jit(solution)/shard_map/ppermute | solution.py:28
  15.5 1.0 %collective-permute-done.i1 = bf16[256,768]{1,0:T(8,128)(2,1)S(1)} collective-permute-done((bf16[256,768]{1,0:T(8,128)(2,1)}, bf16[256,768]{1,0:T(8,128)(2,1)S(1)}, u32[]{:S(2)}, u32[]{:S(2)}) %collective-permute-start) | collective-permute-done | bytes 393248 | tf_op jit(solution)/shard_map/ppermute | solution.py:28
  16.6 1.6 %collective-permute-start.2 = (bf16[256,768]{1,0:T(8,128)(2,1)S(1)}, bf16[256,768]{1,0:T(8,128)(2,1)S(1)}, u32[]{:S(2)}, u32[]{:S(2)}) collective-permute-start(bf16[256,768]{1,0:T(8,128)(2,1)S(1)} %pick.1), channel_id=1, source_target_pairs={{0,4},{1,13},{2,6},{3,15},{4,0},{5,9},{6,2},{7,11},{8,12},{9,5},{1... | collective-permute-start | bytes 1179656 | tf_op jit(solution)/shard_map/ppermute | solution.py:35
  18.8 0.0 collective-permute-done.5.t1
  18.8 2.5 %first.1 = (bf16[768,768]{1,0:T(8,128)(2,1)S(1)}, bf16[768,768]{1,0:T(8,128)(2,1)S(1)}, f32[768,768]{1,0:T(8,128)S(1)}, f32[4,1024]{1,0:T(4,128)S(1)}, f32[4,1024]{1,0:T(4,128)S(1)}) custom-call(f32[1]{0:T(128)S(6)} %copy.8.scale, bf16[256,768]{1,0:T(8,128)(2,1)S(1)} %get-tuple-element.41.before.i0, bf16[256,768]{1,0:T(8,128)(2,1)S(1)} %get-tuple-element.42.t0, ...), custom_call_target="tpu_custom_call" | custom-call | flops 2640000000 | bytes 7111684 | tf_op jit(solution)/shard_map/first/pallas_call | solution.py:58
  21.3 0.0 collective-permute-done.4.t3
  21.3 1.1 %second.1 = (bf16[1024,768]{1,0:T(8,128)(2,1)S(1)}, f32[768,256]{1,0:T(8,128)S(1)}, f32[4,1024]{1,0:T(4,128)S(1)}, f32[4,1024]{1,0:T(4,128)S(1)}) custom-call(f32[1]{0:T(128)S(6)} %copy.8.scale, bf16[256,768]{1,0:T(8,128)(2,1)S(1)} %collective-permute-done.4.t3, bf16[768,768]{1,0:T(8,128)(2,1)S(1)} %get-tuple-element.43.near, ...), custom_call_target="tpu_custom_call" | custom-call | flops 1155000064 | bytes 5177348 | tf_op jit(solution)/shard_map/second/pallas_call | solution.py:58
  22.4 2.1 %collective-permute-done.2.i2 = bf16[256,768]{1,0:T(8,128)(2,1)S(1)} collective-permute-done((bf16[256,768]{1,0:T(8,128)(2,1)S(1)}, bf16[256,768]{1,0:T(8,128)(2,1)S(1)}, u32[]{:S(2)}, u32[]{:S(2)}) %collective-permute-start.2) | collective-permute-done | bytes 393248 | tf_op jit(solution)/shard_map/ppermute | solution.py:35
  24.5 1.2 %third.1 = (bf16[256,768]{1,0:T(8,128)(2,1)S(1)}, f32[256,1024]{1,0:T(8,128)S(1)}, f32[4,1024]{1,0:T(4,128)S(1)}, f32[4,1024]{1,0:T(4,128)S(1)}) custom-call(f32[1]{0:T(128)S(6)} %copy.8.scale, bf16[256,768]{1,0:T(8,128)(2,1)S(1)} %collective-permute-done.2.i2, bf16[1024,768]{1,0:T(8,128)(2,1)S(1)} %get-tuple-element.47.txts, ...), custom_call_target="tpu_custom_call" | custom-call | flops 1264999936 | bytes 3473412 | tf_op jit(solution)/shard_map/third/pallas_call | solution.py:58
  25.6 2.2 %collective-permute-start.7 = (f32[4,1024]{1,0:T(4,128)S(1)}, f32[4,1024]{1,0:T(4,128)S(1)}, u32[]{:S(2)}, u32[]{:S(2)}) collective-permute-start(f32[4,1024]{1,0:T(4,128)S(1)} %get-tuple-element.51.mine.before), channel_id=1, source_target_pairs={{0,1},{1,0},{2,3},{3,2},{4,5},{5,4},{6,7},{7,6},{8,9},{9,8},{10,11... | collective-permute-start | bytes 49160 | tf_op jit(solution)/shard_map/ppermute | solution.py:28
  27.8 0.1 collective-permute-start.6
  27.9 0.8 %collective-permute-done.7.other = f32[4,1024]{1,0:T(4,128)S(1)} collective-permute-done((f32[4,1024]{1,0:T(4,128)S(1)}, f32[4,1024]{1,0:T(4,128)S(1)}, u32[]{:S(2)}, u32[]{:S(2)}) %collective-permute-start.7) | collective-permute-done | bytes 16416 | tf_op jit(solution)/shard_map/ppermute | solution.py:28
  28.7 0.2 collective-permute-start.8
  28.9 1.5 %collective-permute-done.6.other = f32[4,1024]{1,0:T(4,128)S(1)} collective-permute-done((f32[4,1024]{1,0:T(4,128)S(1)}, f32[4,1024]{1,0:T(4,128)S(1)}, u32[]{:S(2)}, u32[]{:S(2)}) %collective-permute-start.6) | collective-permute-done | bytes 16416 | tf_op jit(solution)/shard_map/ppermute | solution.py:28
  30.4 2.4 %collective-permute-done.8.before.col2 = f32[4,1024]{1,0:T(4,128)S(1)} collective-permute-done((f32[4,1024]{1,0:T(4,128)S(1)}, f32[4,1024]{1,0:T(4,128)S(1)}, u32[]{:S(2)}, u32[]{:S(2)}) %collective-permute-start.8) | collective-permute-done | bytes 16416 | tf_op jit(solution)/shard_map/ppermute | solution.py:28
  32.9 1.3 %collective-permute-start.9 = (f32[4,1024]{1,0:T(4,128)S(1)}, f32[4,1024]{1,0:T(4,128)S(1)}, u32[]{:S(2)}, u32[]{:S(2)}) collective-permute-start(f32[4,1024]{1,0:T(4,128)S(1)} %join.3.row), channel_id=1, source_target_pairs={{0,12},{1,13},{2,14},{3,15},{4,8},{5,9},{6,10},{7,11},{8,4},{9,5},... | collective-permute-start | bytes 49160 | tf_op jit(solution)/shard_map/ppermute | solution.py:28
  34.2 2.6 %collective-permute-done.9.row3 = f32[4,1024]{1,0:T(4,128)S(1)} collective-permute-done((f32[4,1024]{1,0:T(4,128)S(1)}, f32[4,1024]{1,0:T(4,128)S(1)}, u32[]{:S(2)}, u32[]{:S(2)}) %collective-permute-start.9) | collective-permute-done | bytes 16416 | tf_op jit(solution)/shard_map/ppermute | solution.py:28
  36.8 0.1 lse.1
  37.0 2.7 %collective-permute-start.10 = (f32[8,128]{1,0:T(8,128)S(1)}, f32[8,128]{1,0:T(8,128)S(1)}, u32[]{:S(2)}, u32[]{:S(2)}) collective-permute-start(f32[8,128]{1,0:T(8,128)S(1)} %get-tuple-element.52.row), channel_id=1, source_target_pairs={{0,1},{1,0},{2,3},{3,2},{4,5},{5,4},{6,7},{7,6},{8,9},{9,8},{10,11... | collective-permute-start | bytes 12296 | tf_op jit(solution)/shard_map/ppermute | solution.py:28
  39.7 0.0 collective-permute-start.11
  39.7 1.3 %weight.1 = (bf16[512,1024]{1,0:T(8,128)(2,1)S(1)}, bf16[512,1024]{1,0:T(8,128)(2,1)S(1)}) custom-call(f32[768,768]{1,0:T(8,128)S(1)} %get-tuple-element.54.first, f32[768,256]{1,0:T(8,128)S(1)} %get-tuple-element.55.second, f32[256,1024]{1,0:T(8,128)S(1)} %get-tuple-element.56.third, f32[2,1024]{1,0:T(2,128)S(1)} %get-tuple-element.57.lse, s32[1,256]{1,0:T(1,128)S(1)} %bitcast.2), custom_call_target="tpu_custom_call" | custom-call | flops 1430000000 | bytes 6300672 | tf_op jit(solution)/shard_map/weight/pallas_call | solution.py:58
  41.0 1.4 %image.4 = (f32[256,768]{1,0:T(8,128)S(1)}, f32[256,768]{1,0:T(8,128)S(1)}, f32[256,768]{1,0:T(8,128)S(1)}, f32[8,128]{1,0:T(8,128)S(1)}) custom-call(bf16[512,1024]{1,0:T(8,128)(2,1)S(1)} %get-tuple-element.58.w01, bf16[512,1024]{1,0:T(8,128)(2,1)S(1)} %get-tuple-element.59.w23, bf16[1024,768]{1,0:T(8,128)(2,1)S(1)} %get-tuple-element.47.txts), custom_call_target="tpu_custom_call" | custom-call | flops 1210000000 | bytes 6033408 | tf_op jit(solution)/shard_map/image/pallas_call | solution.py:58
  42.4 0.0 collective-permute-done.10.row_core
  42.4 0.0 collective-permute-done.11.col1
  42.4 1.4 %early.1 = (bf16[512,768]{1,0:T(8,128)(2,1)S(1)}, bf16[256,768]{1,0:T(8,128)(2,1)S(1)}) custom-call(bf16[512,1024]{1,0:T(8,128)(2,1)S(1)} %get-tuple-element.58.w01, bf16[512,1024]{1,0:T(8,128)(2,1)S(1)} %get-tuple-element.59.w23, bf16[768,768]{1,0:T(8,128)(2,1)S(1)} %get-tuple-element.43.near, bf16[256,768]{1,0:T(8,128)(2,1)S(1)} %get-tuple-element.61.far, ...), custom_call_target="tpu_custom_call" | custom-call | flops 1540000000 | bytes 6426624 | tf_op jit(solution)/shard_map/early/pallas_call | solution.py:58
  43.9 1.2 %collective-permute-start.19 = (bf16[512,768]{1,0:T(8,128)(2,1)S(1)}, bf16[512,768]{1,0:T(8,128)(2,1)S(1)}, u32[]{:S(2)}, u32[]{:S(2)}) collective-permute-start(bf16[512,768]{1,0:T(8,128)(2,1)S(1)} %get-tuple-element.65), channel_id=1, source_target_pairs={{0,1},{1,0},{2,3},{3,2},{4,5},{5,4},{6,7},{7,6},{8,9},{9,8},{10,11... | collective-permute-start | bytes 2359304 | tf_op jit(solution)/shard_map/ppermute | solution.py:28
  45.1 1.2 %collective-permute-start.20 = (bf16[256,768]{1,0:T(8,128)(2,1)S(1)}, bf16[256,768]{1,0:T(8,128)(2,1)S(1)}, u32[]{:S(2)}, u32[]{:S(2)}) collective-permute-start(bf16[256,768]{1,0:T(8,128)(2,1)S(1)} %get-tuple-element.69), channel_id=1, source_target_pairs={{0,4},{1,13},{2,6},{3,15},{4,0},{5,9},{6,2},{7,11},{8,12},{9,5},{1... | collective-permute-start | bytes 1179656 | tf_op jit(solution)/shard_map/ppermute | solution.py:35
  46.3 0.4 collective-permute-start.12
  46.7 1.0 %text.4 = (f32[256,768]{1,0:T(8,128)S(1)}, f32[256,768]{1,0:T(8,128)S(1)}, f32[8,128]{1,0:T(8,128)S(1)}) custom-call(bf16[512,1024]{1,0:T(8,128)(2,1)S(1)} %get-tuple-element.58.w01, bf16[512,1024]{1,0:T(8,128)(2,1)S(1)} %get-tuple-element.59.w23, bf16[768,768]{1,0:T(8,128)(2,1)S(1)} %get-tuple-element.43.near, bf16[256,768]{1,0:T(8,128)(2,1)S(1)} %get-tuple-element.61.far, ...), custom_call_target="tpu_custom_call" | custom-call | flops 1210000000 | bytes 5251072 | tf_op jit(solution)/shard_map/text/pallas_call | solution.py:58
  47.7 1.3 %collective-permute-done.12.b = f32[8,128]{1,0:T(8,128)S(1)} collective-permute-done((f32[8,128]{1,0:T(8,128)S(1)}, f32[8,128]{1,0:T(8,128)S(1)}, u32[]{:S(2)}, u32[]{:S(2)}) %collective-permute-start.12) | collective-permute-done | bytes 4128 | tf_op jit(solution)/shard_map/ppermute | solution.py:28
  49.1 1.5 %collective-permute-start.13 = (f32[8,128]{1,0:T(8,128)S(1)}, f32[8,128]{1,0:T(8,128)S(1)}, u32[]{:S(2)}, u32[]{:S(2)}) collective-permute-start(f32[8,128]{1,0:T(8,128)S(1)} %side.1.a), channel_id=1, source_target_pairs={{0,18},{1,13},{2,16},{3,15},{4,22},{5,9},{6,20},{7,11},{8,26},{9,5... | collective-permute-start | bytes 12296 | tf_op jit(solution)/shard_map/ppermute | solution.py:35
  50.5 2.4 %collective-permute-done.13.b = f32[8,128]{1,0:T(8,128)S(1)} collective-permute-done((f32[8,128]{1,0:T(8,128)S(1)}, f32[8,128]{1,0:T(8,128)S(1)}, u32[]{:S(2)}, u32[]{:S(2)}) %collective-permute-start.13) | collective-permute-done | bytes 4128 | tf_op jit(solution)/shard_map/ppermute | solution.py:35
  53.0 1.8 %collective-permute-start.14 = (f32[8,128]{1,0:T(8,128)S(1)}, f32[8,128]{1,0:T(8,128)S(1)}, u32[]{:S(2)}, u32[]{:S(2)}) collective-permute-start(f32[8,128]{1,0:T(8,128)S(1)} %add.3.mine), channel_id=1, source_target_pairs={{0,1},{1,0},{2,3},{3,2},{4,5},{5,4},{6,7},{7,6},{8,9},{9,8},{10,11... | collective-permute-start | bytes 12296 | tf_op jit(solution)/shard_map/ppermute | solution.py:28
  54.8 0.8 %collective-permute-done.14.other = f32[8,128]{1,0:T(8,128)S(1)} collective-permute-done((f32[8,128]{1,0:T(8,128)S(1)}, f32[8,128]{1,0:T(8,128)S(1)}, u32[]{:S(2)}, u32[]{:S(2)}) %collective-permute-start.14) | collective-permute-done | bytes 4128 | tf_op jit(solution)/shard_map/ppermute | solution.py:28
  55.6 0.1 total.1.a.before
  55.7 0.0 collective-permute-done.19.core_part
  55.7 0.0 copy-start.1
  55.7 0.0 copy-start.3
  55.8 0.3 away.1
  56.1 0.7 collective-permute-start.21
  56.8 1.2 %collective-permute-start.22 = (bf16[256,768]{1,0:T(8,128)(2,1)S(1)}, bf16[256,768]{1,0:T(8,128)(2,1)S(1)}, u32[]{:S(2)}, u32[]{:S(2)}) collective-permute-start(bf16[256,768]{1,0:T(8,128)(2,1)S(1)} %get-tuple-element.71), channel_id=1, source_target_pairs={{0,12},{1,13},{2,14},{3,15},{4,8},{5,9},{6,10},{7,11},{8,4},{9,5},... | collective-permute-start | bytes 1179656 | tf_op jit(solution)/shard_map/ppermute | solution.py:28
  58.0 0.0 collective-permute-start.23
  58.0 5.6 %collective-permute-start.15 = (f32[8,128]{1,0:T(8,128)S(1)}, f32[8,128]{1,0:T(8,128)S(1)}, u32[]{:S(2)}, u32[]{:S(2)}) collective-permute-start(f32[8,128]{1,0:T(8,128)S(1)} %total.1.a.before), channel_id=1, source_target_pairs={{0,32},{1,225},{2,34},{3,227},{4,36},{5,229},{6,38},{7,231},{8,40}... | collective-permute-start | bytes 12296 | tf_op jit(solution)/shard_map/ppermute | solution.py:35
  63.5 1.3 %collective-permute-done.15.b = f32[8,128]{1,0:T(8,128)S(1)} collective-permute-done((f32[8,128]{1,0:T(8,128)S(1)}, f32[8,128]{1,0:T(8,128)S(1)}, u32[]{:S(2)}, u32[]{:S(2)}) %collective-permute-start.15) | collective-permute-done | bytes 4128 | tf_op jit(solution)/shard_map/ppermute | solution.py:35
  64.8 0.0 collective-permute-start.16
  64.8 1.2 %collective-permute-done.16.other = f32[8,128]{1,0:T(8,128)S(1)} collective-permute-done((f32[8,128]{1,0:T(8,128)S(1)}, f32[8,128]{1,0:T(8,128)S(1)}, u32[]{:S(2)}, u32[]{:S(2)}) %collective-permute-start.16) | collective-permute-done | bytes 4128 | tf_op jit(solution)/shard_map/ppermute | solution.py:28
  66.0 1.7 %collective-permute-start.17 = (f32[8,128]{1,0:T(8,128)S(1)}, f32[8,128]{1,0:T(8,128)S(1)}, u32[]{:S(2)}, u32[]{:S(2)}) collective-permute-start(f32[8,128]{1,0:T(8,128)S(1)} %planes.1.a), channel_id=1, source_target_pairs={{0,160},{1,97},{2,162},{3,99},{4,164},{5,101},{6,166},{7,103},{8,1... | collective-permute-start | bytes 12296 | tf_op jit(solution)/shard_map/ppermute | solution.py:35
  67.7 3.8 %collective-permute-done.17.b = f32[8,128]{1,0:T(8,128)S(1)} collective-permute-done((f32[8,128]{1,0:T(8,128)S(1)}, f32[8,128]{1,0:T(8,128)S(1)}, u32[]{:S(2)}, u32[]{:S(2)}) %collective-permute-start.17) | collective-permute-done | bytes 4128 | tf_op jit(solution)/shard_map/ppermute | solution.py:35
  71.6 0.3 collective-permute-start.18
  71.8 0.0 collective-permute-done.21.p1
  71.8 0.0 collective-permute-done.22.p3
  71.8 0.0 collective-permute-done.23.py
  71.9 1.6 %grad.1 = (bf16[256,768]{1,0:T(8,128)(2,1)}, bf16[256,768]{1,0:T(8,128)(2,1)}, f32[8,128]{1,0:T(8,128)S(1)}) custom-call(f32[1]{0:T(128)S(6)} %copy.8.scale, bf16[256,768]{1,0:T(8,128)(2,1)S(1)} %copy-done.1, bf16[256,768]{1,0:T(8,128)(2,1)S(1)} %copy-done.3, f32[256,768]{1,0:T(8,128)S(1)} %get-tuple-element.63.img_back, ...), custom_call_target="tpu_custom_call" | custom-call | flops 1760000000 | bytes 5115908 | tf_op jit(solution)/shard_map/grad/pallas_call | solution.py:58
  73.4 0.0 collective-permute-done.18.other
  73.4 0.7 scalar.1
  (16 shorter events, 0.1 us)
Async XLA Ops:
  0.6 11.9 %collective-permute-start.3 = (bf16[256,768]{1,0:T(8,128)(2,1)}, bf16[256,768]{1,0:T(8,128)(2,1)S(1)}, u32[]{:S(2)}, u32[]{:S(2)}) collective-permute-start(bf16[256,768]{1,0:T(8,128)(2,1)} %text.5), channel_id=1, source_target_pairs={{0,2},{1,3},{2,0},{3,1},{4,6},{5,7},{6,4},{7,5},{8,10},{9,11},{10,... | collective-permute-start | bytes 1179656 | tf_op jit(solution)/shard_map/ppermute | solution.py:28
  4.5 11.1 %collective-permute-start.1 = (bf16[256,768]{1,0:T(8,128)(2,1)}, bf16[256,768]{1,0:T(8,128)(2,1)S(1)}, u32[]{:S(2)}, u32[]{:S(2)}) collective-permute-start(bf16[256,768]{1,0:T(8,128)(2,1)} %image.5), channel_id=1, source_target_pairs={{0,12},{1,13},{2,14},{3,15},{4,8},{5,9},{6,10},{7,11},{8,4},{9,5},... | collective-permute-start | bytes 1179656 | tf_op jit(solution)/shard_map/ppermute | solution.py:28
  6.9 9.6 %collective-permute-start = (bf16[256,768]{1,0:T(8,128)(2,1)}, bf16[256,768]{1,0:T(8,128)(2,1)S(1)}, u32[]{:S(2)}, u32[]{:S(2)}) collective-permute-start(bf16[256,768]{1,0:T(8,128)(2,1)} %image.5), channel_id=1, source_target_pairs={{0,4},{1,5},{2,6},{3,7},{4,0},{5,1},{6,2},{7,3},{8,12},{9,13},{10,... | collective-permute-start | bytes 1179656 | tf_op jit(solution)/shard_map/ppermute | solution.py:28
  6.9 11.9 %collective-permute-start.5 = (bf16[256,768]{1,0:T(8,128)(2,1)}, bf16[256,768]{1,0:T(8,128)(2,1)S(1)}, u32[]{:S(2)}, u32[]{:S(2)}) collective-permute-start(bf16[256,768]{1,0:T(8,128)(2,1)} %text.5), channel_id=1, source_target_pairs={{0,1},{1,0},{2,3},{3,2},{4,5},{5,4},{6,7},{7,6},{8,9},{9,8},{10,11... | collective-permute-start | bytes 1179656 | tf_op jit(solution)/shard_map/ppermute | solution.py:28
  8.4 1.0 %copy-start = (bf16[256,768]{1,0:T(8,128)(2,1)S(1)}, bf16[256,768]{1,0:T(8,128)(2,1)}, u32[]{:S(2)}) copy-start(bf16[256,768]{1,0:T(8,128)(2,1)} %image.5) | copy-start | bytes 1179652
  9.4 1.0 %copy-start.2 = (bf16[256,768]{1,0:T(8,128)(2,1)S(1)}, bf16[256,768]{1,0:T(8,128)(2,1)}, u32[]{:S(2)}) copy-start(bf16[256,768]{1,0:T(8,128)(2,1)} %text.5) | copy-start | bytes 1179652
  12.6 8.7 %collective-permute-start.4 = (bf16[256,768]{1,0:T(8,128)(2,1)S(1)}, bf16[256,768]{1,0:T(8,128)(2,1)S(1)}, u32[]{:S(2)}, u32[]{:S(2)}) collective-permute-start(bf16[256,768]{1,0:T(8,128)(2,1)S(1)} %collective-permute-done.3.t2), channel_id=1, source_target_pairs={{0,1},{1,0},{2,3},{3,2},{4,5},{5,4},{6,7},{7,6},{8,9},{9,8},{10,11... | collective-permute-start | bytes 1179656 | tf_op jit(solution)/shard_map/ppermute | solution.py:28
  16.5 2.3 %copy-start.4 = (s32[256]{0:T(256)S(1)}, s32[256]{0:T(256)}, u32[]{:S(2)}) copy-start(s32[256]{0:T(256)} %param.6) | copy-start | bytes 3076
  16.6 7.9 %collective-permute-start.2 = (bf16[256,768]{1,0:T(8,128)(2,1)S(1)}, bf16[256,768]{1,0:T(8,128)(2,1)S(1)}, u32[]{:S(2)}, u32[]{:S(2)}) collective-permute-start(bf16[256,768]{1,0:T(8,128)(2,1)S(1)} %pick.1), channel_id=1, source_target_pairs={{0,4},{1,13},{2,6},{3,15},{4,0},{5,9},{6,2},{7,11},{8,12},{9,5},{1... | collective-permute-start | bytes 1179656 | tf_op jit(solution)/shard_map/ppermute | solution.py:35
  25.6 3.0 %collective-permute-start.7 = (f32[4,1024]{1,0:T(4,128)S(1)}, f32[4,1024]{1,0:T(4,128)S(1)}, u32[]{:S(2)}, u32[]{:S(2)}) collective-permute-start(f32[4,1024]{1,0:T(4,128)S(1)} %get-tuple-element.51.mine.before), channel_id=1, source_target_pairs={{0,1},{1,0},{2,3},{3,2},{4,5},{5,4},{6,7},{7,6},{8,9},{9,8},{10,11... | collective-permute-start | bytes 49160 | tf_op jit(solution)/shard_map/ppermute | solution.py:28
  27.8 2.6 %collective-permute-start.6 = (f32[4,1024]{1,0:T(4,128)S(1)}, f32[4,1024]{1,0:T(4,128)S(1)}, u32[]{:S(2)}, u32[]{:S(2)}) collective-permute-start(f32[4,1024]{1,0:T(4,128)S(1)} %get-tuple-element.50.mine), channel_id=1, source_target_pairs={{0,4},{1,5},{2,6},{3,7},{4,0},{5,1},{6,2},{7,3},{8,12},{9,13},{10,... | collective-permute-start | bytes 49160 | tf_op jit(solution)/shard_map/ppermute | solution.py:28
  28.7 4.2 %collective-permute-start.8 = (f32[4,1024]{1,0:T(4,128)S(1)}, f32[4,1024]{1,0:T(4,128)S(1)}, u32[]{:S(2)}, u32[]{:S(2)}) collective-permute-start(f32[4,1024]{1,0:T(4,128)S(1)} %join.2.col), channel_id=1, source_target_pairs={{0,2},{1,3},{2,0},{3,1},{4,6},{5,7},{6,4},{7,5},{8,10},{9,11},{10,... | collective-permute-start | bytes 49160 | tf_op jit(solution)/shard_map/ppermute | solution.py:28
  32.9 3.9 %collective-permute-start.9 = (f32[4,1024]{1,0:T(4,128)S(1)}, f32[4,1024]{1,0:T(4,128)S(1)}, u32[]{:S(2)}, u32[]{:S(2)}) collective-permute-start(f32[4,1024]{1,0:T(4,128)S(1)} %join.3.row), channel_id=1, source_target_pairs={{0,12},{1,13},{2,14},{3,15},{4,8},{5,9},{6,10},{7,11},{8,4},{9,5},... | collective-permute-start | bytes 49160 | tf_op jit(solution)/shard_map/ppermute | solution.py:28
  37.0 5.4 %collective-permute-start.10 = (f32[8,128]{1,0:T(8,128)S(1)}, f32[8,128]{1,0:T(8,128)S(1)}, u32[]{:S(2)}, u32[]{:S(2)}) collective-permute-start(f32[8,128]{1,0:T(8,128)S(1)} %get-tuple-element.52.row), channel_id=1, source_target_pairs={{0,1},{1,0},{2,3},{3,2},{4,5},{5,4},{6,7},{7,6},{8,9},{9,8},{10,11... | collective-permute-start | bytes 12296 | tf_op jit(solution)/shard_map/ppermute | solution.py:28
  39.7 2.7 %collective-permute-start.11 = (f32[8,128]{1,0:T(8,128)S(1)}, f32[8,128]{1,0:T(8,128)S(1)}, u32[]{:S(2)}, u32[]{:S(2)}) collective-permute-start(f32[8,128]{1,0:T(8,128)S(1)} %get-tuple-element.53.col), channel_id=1, source_target_pairs={{0,4},{1,5},{2,6},{3,7},{4,0},{5,1},{6,2},{7,3},{8,12},{9,13},{10,... | collective-permute-start | bytes 12296 | tf_op jit(solution)/shard_map/ppermute | solution.py:28
  43.9 11.9 %collective-permute-start.19 = (bf16[512,768]{1,0:T(8,128)(2,1)S(1)}, bf16[512,768]{1,0:T(8,128)(2,1)S(1)}, u32[]{:S(2)}, u32[]{:S(2)}) collective-permute-start(bf16[512,768]{1,0:T(8,128)(2,1)S(1)} %get-tuple-element.65), channel_id=1, source_target_pairs={{0,1},{1,0},{2,3},{3,2},{4,5},{5,4},{6,7},{7,6},{8,9},{9,8},{10,11... | collective-permute-start | bytes 2359304 | tf_op jit(solution)/shard_map/ppermute | solution.py:28
  45.1 10.6 %collective-permute-start.20 = (bf16[256,768]{1,0:T(8,128)(2,1)S(1)}, bf16[256,768]{1,0:T(8,128)(2,1)S(1)}, u32[]{:S(2)}, u32[]{:S(2)}) collective-permute-start(bf16[256,768]{1,0:T(8,128)(2,1)S(1)} %get-tuple-element.69), channel_id=1, source_target_pairs={{0,4},{1,13},{2,6},{3,15},{4,0},{5,9},{6,2},{7,11},{8,12},{9,5},{1... | collective-permute-start | bytes 1179656 | tf_op jit(solution)/shard_map/ppermute | solution.py:35
  46.3 2.8 %collective-permute-start.12 = (f32[8,128]{1,0:T(8,128)S(1)}, f32[8,128]{1,0:T(8,128)S(1)}, u32[]{:S(2)}, u32[]{:S(2)}) collective-permute-start(f32[8,128]{1,0:T(8,128)S(1)} %half.1.before.a), channel_id=1, source_target_pairs={{0,16},{16,0},{32,48},{48,32},{64,80},{80,64},{96,112},{112,96},{1... | collective-permute-start | bytes 12296 | tf_op jit(solution)/shard_map/ppermute | solution.py:28
  49.1 3.9 %collective-permute-start.13 = (f32[8,128]{1,0:T(8,128)S(1)}, f32[8,128]{1,0:T(8,128)S(1)}, u32[]{:S(2)}, u32[]{:S(2)}) collective-permute-start(f32[8,128]{1,0:T(8,128)S(1)} %side.1.a), channel_id=1, source_target_pairs={{0,18},{1,13},{2,16},{3,15},{4,22},{5,9},{6,20},{7,11},{8,26},{9,5... | collective-permute-start | bytes 12296 | tf_op jit(solution)/shard_map/ppermute | solution.py:35
  53.0 2.6 %collective-permute-start.14 = (f32[8,128]{1,0:T(8,128)S(1)}, f32[8,128]{1,0:T(8,128)S(1)}, u32[]{:S(2)}, u32[]{:S(2)}) collective-permute-start(f32[8,128]{1,0:T(8,128)S(1)} %add.3.mine), channel_id=1, source_target_pairs={{0,1},{1,0},{2,3},{3,2},{4,5},{5,4},{6,7},{7,6},{8,9},{9,8},{10,11... | collective-permute-start | bytes 12296 | tf_op jit(solution)/shard_map/ppermute | solution.py:28
  55.7 16.1 %copy-start.1 = (bf16[256,768]{1,0:T(8,128)(2,1)S(1)}, bf16[256,768]{1,0:T(8,128)(2,1)}, u32[]{:S(2)}) copy-start(bf16[256,768]{1,0:T(8,128)(2,1)} %image.5) | copy-start | bytes 1179652
  55.7 16.1 %copy-start.3 = (bf16[256,768]{1,0:T(8,128)(2,1)S(1)}, bf16[256,768]{1,0:T(8,128)(2,1)}, u32[]{:S(2)}) copy-start(bf16[256,768]{1,0:T(8,128)(2,1)} %text.5) | copy-start | bytes 1179652
  56.1 15.7 %collective-permute-start.21 = (bf16[256,768]{1,0:T(8,128)(2,1)S(1)}, bf16[256,768]{1,0:T(8,128)(2,1)S(1)}, u32[]{:S(2)}, u32[]{:S(2)}) collective-permute-start(bf16[256,768]{1,0:T(8,128)(2,1)S(1)} %get-tuple-element.70), channel_id=1, source_target_pairs={{0,4},{1,5},{2,6},{3,7},{4,0},{5,1},{6,2},{7,3},{8,12},{9,13},{10,... | collective-permute-start | bytes 1179656 | tf_op jit(solution)/shard_map/ppermute | solution.py:28
  56.8 15.1 %collective-permute-start.22 = (bf16[256,768]{1,0:T(8,128)(2,1)S(1)}, bf16[256,768]{1,0:T(8,128)(2,1)S(1)}, u32[]{:S(2)}, u32[]{:S(2)}) collective-permute-start(bf16[256,768]{1,0:T(8,128)(2,1)S(1)} %get-tuple-element.71), channel_id=1, source_target_pairs={{0,12},{1,13},{2,14},{3,15},{4,8},{5,9},{6,10},{7,11},{8,4},{9,5},... | collective-permute-start | bytes 1179656 | tf_op jit(solution)/shard_map/ppermute | solution.py:28
  58.0 13.9 %collective-permute-start.23 = (bf16[256,768]{1,0:T(8,128)(2,1)S(1)}, bf16[256,768]{1,0:T(8,128)(2,1)S(1)}, u32[]{:S(2)}, u32[]{:S(2)}) collective-permute-start(bf16[256,768]{1,0:T(8,128)(2,1)S(1)} %get-tuple-element.72), channel_id=1, source_target_pairs={{0,2},{1,3},{2,0},{3,1},{4,6},{5,7},{6,4},{7,5},{8,10},{9,11},{10,... | collective-permute-start | bytes 1179656 | tf_op jit(solution)/shard_map/ppermute | solution.py:28
  58.0 6.9 %collective-permute-start.15 = (f32[8,128]{1,0:T(8,128)S(1)}, f32[8,128]{1,0:T(8,128)S(1)}, u32[]{:S(2)}, u32[]{:S(2)}) collective-permute-start(f32[8,128]{1,0:T(8,128)S(1)} %total.1.a.before), channel_id=1, source_target_pairs={{0,32},{1,225},{2,34},{3,227},{4,36},{5,229},{6,38},{7,231},{8,40}... | collective-permute-start | bytes 12296 | tf_op jit(solution)/shard_map/ppermute | solution.py:35
  64.8 1.2 %collective-permute-start.16 = (f32[8,128]{1,0:T(8,128)S(1)}, f32[8,128]{1,0:T(8,128)S(1)}, u32[]{:S(2)}, u32[]{:S(2)}) collective-permute-start(f32[8,128]{1,0:T(8,128)S(1)} %add.4.held), channel_id=1, source_target_pairs={{0,1},{1,0},{2,3},{3,2},{4,5},{5,4},{6,7},{7,6},{8,9},{9,8},{10,11... | collective-permute-start | bytes 12296 | tf_op jit(solution)/shard_map/ppermute | solution.py:28
  66.0 5.5 %collective-permute-start.17 = (f32[8,128]{1,0:T(8,128)S(1)}, f32[8,128]{1,0:T(8,128)S(1)}, u32[]{:S(2)}, u32[]{:S(2)}) collective-permute-start(f32[8,128]{1,0:T(8,128)S(1)} %planes.1.a), channel_id=1, source_target_pairs={{0,160},{1,97},{2,162},{3,99},{4,164},{5,101},{6,166},{7,103},{8,1... | collective-permute-start | bytes 12296 | tf_op jit(solution)/shard_map/ppermute | solution.py:35
  71.6 1.9 %collective-permute-start.18 = (f32[8,128]{1,0:T(8,128)S(1)}, f32[8,128]{1,0:T(8,128)S(1)}, u32[]{:S(2)}, u32[]{:S(2)}) collective-permute-start(f32[8,128]{1,0:T(8,128)S(1)} %add.5.held), channel_id=1, source_target_pairs={{0,1},{1,0},{2,3},{3,2},{4,5},{5,4},{6,7},{7,6},{8,9},{9,8},{10,11... | collective-permute-start | bytes 12296 | tf_op jit(solution)/shard_map/ppermute | solution.py:28

commit v4 on v3

--- a/solution.py
+++ b/solution.py
@@ -16,9 +16,10 @@
 SLOTS = 4
 LOW = -1e30
 COST = {
+    "total": 30,
     "pick": 5.0,
-    "own": 0.25, "first": 2.4, "second": 1.05, "third": 1.15, "lse": 0.15, "weight": 1.3,
-    "image": 1.1, "text": 1.1, "early": 1.4, "away": 0.3, "grad": 1.6,
+    "own": 0.25, "first": 12, "second": 8, "third": 1.15, "lse": 0.15, "weight": 1.3,
+    "image": 1.1, "text": 1.1, "early": 1.4, "half": 0.3, "across": 0.2, "late": 0.2, "grad": 1.6,
 }
 NEAR = (0, 1, 3)
 X1, X2, X3, Y, CORE = 4, 8, 12, 2, 1
@@ -41,6 +42,10 @@
 
 def relay(z, lo, x, hi, core):
     return (z, lo, x ^ 1 if core == 0 else 3 - x, hi, core)
+
+
+def other_way(z, lo, x, hi, core):
+    return (z, lo, 3 - x if core == 0 else x ^ 1, hi, core)
 
 
 def by_planes(z, lo, x, hi, core):
@@ -221,9 +226,9 @@
     return value, mean, mine[2:3, :] + swap(2)
 
 
-def join_kernel(mine, other, before, out):
+def join_kernel(mine, other, out):
     out[0:1, :], out[1:2, :], out[2:3, :] = joined(mine, other, 1)
-    out[3:4, :] = jnp.zeros((1, out.shape[1]), jnp.float32)
+    out[3:, :] = jnp.zeros((out.shape[0] - 3, out.shape[1]), jnp.float32)
 
 
 def slot_sum(v):
@@ -279,7 +284,7 @@
     weigh(scores, lse, (0, 1), tiles(w01, (0, 1), range(SLOTS), rows), hit)
 
 
-def early_kernel(w01, w23, near, far, txts, before, core_part, part2):
+def early_kernel(w01, w23, near, far, txts, core_part, part2):
     rows = far.shape[0]
     back = jnp.dot(w23[pl.ds(0, rows), :], txts[...], preferred_element_type=jnp.float32)
     part2[...] = back.astype(part2.dtype)
@@ -287,11 +292,22 @@
         core_part[pl.ds(n * rows, rows), :] = over(w01, w23, near, far, l).astype(core_part.dtype)
 
 
-def image_kernel(w01, w23, txts, img_back, part1, part3, token):
+def image_kernel(w01, w23, txts, before, img_back, first, late):
     rows = img_back.shape[0]
-    token[...] = jnp.zeros(token.shape, jnp.float32)
-    for w, n, out in ((w01, 1, part1), (w23, 1, part3), (w01, 0, img_back)):
-        out[...] = jnp.dot(w[pl.ds(n * rows, rows), :], txts[...], preferred_element_type=jnp.float32)
+    back = lambda w, n: jnp.dot(
+        w[pl.ds(n * rows, rows), :], txts[...], preferred_element_type=jnp.float32
+    )
+    zero = core_index() == 0
+    one, three = back(w01, 1), back(w23, 1)
+    first[...] = jnp.where(zero, one, three).astype(first.dtype)
+    late[...] = jnp.where(zero, three, one)
+    img_back[...] = back(w01, 0)
+
+
+def half_kernel(row, row_core, col, col1, core_in, part2_in, before, sums, core_part, part2):
+    sums[...] = jnp.where(core_index() == 0, row[...] + row_core[...], col[...] + col1[...])
+    core_part[...] = core_in[...]
+    part2[...] = part2_in[...]
 
 
 def text_kernel(w01, w23, near, far, before, txt_back, txt_next, token):
@@ -300,21 +316,18 @@
         out[...] = over(w01, w23, near, far, l)
 
 
-def away_kernel(wide1, wide3, txt_next, relayed, core_part, before, part1, part3, part_y):
-    rows = part1.shape[0]
-    passed = relayed[...].astype(jnp.float32)
-    zero = core_index() == 0
-    part3[...] = (wide3[...] + jnp.where(zero, passed, 0.0)).astype(part3.dtype)
-    part1[...] = (wide1[...] + jnp.where(zero, 0.0, passed)).astype(part1.dtype)
+def across_kernel(txt_next, core_part, first_in, before, part_y, first):
+    rows = part_y.shape[0]
+    first[...] = first_in[...]
     total = txt_next[...] + core_part[pl.ds(rows, rows), :].astype(jnp.float32)
     part_y[...] = total.astype(part_y.dtype)
 
 
-def half_kernel(row, row_core, col, col1, before, out):
-    out[...] = jnp.where(core_index() == 0, row[...] + row_core[...], col[...] + col1[...])
-
-
-def side_kernel(a, b, before, out):
+def late_kernel(late, relayed, out):
+    out[...] = (late[...] + relayed[...].astype(jnp.float32)).astype(out.dtype)
+
+
+def side_kernel(a, b, before, before_too, out):
     out[...] = a[...] + b[...]
 
 
@@ -345,16 +358,16 @@
     out[...] = union(held, other, (0,))
 
 
-def scalar_kernel(total_rows, scale, held, other, before, loss, scale_grad):
+def scalar_kernel(total_rows, scale, held, other, loss, scale_grad):
     sums = jnp.sum(union(held, other, (0, 1, 4, 7)), axis=1, keepdims=True)
     loss[0] = sums[0, 0] / total_rows
     scale_grad[0] = sums[1, 0] / (total_rows * scale[0])
 
 
-def grad_kernel(scale, image, text, img_back, txt_back, core_part, p1, p3, py, image_grad, text_grad, token):
+def grad_kernel(scale, image, text, img_back, txt_back, core_part, first, late, py, image_grad, text_grad, token):
     token[...] = jnp.zeros(token.shape, jnp.float32)
     for values, parts, out in (
-        (image, (img_back, p1, p3), image_grad), (text, (txt_back, core_part, py), text_grad),
+        (image, (img_back, first, late), image_grad), (text, (txt_back, core_part, py), text_grad),
     ):
         direction, inverse = unit_rows(values[...])
         incoming = scale[0] * sum(
@@ -391,9 +404,9 @@
         third_kernel, "third", [block, ((rows, group), f32), parts, parts],
         logit_scale, i2, txts, row_part, col_part, scalar=True,
     )
-    (col_part,) = call(join_kernel, "join", [parts], col_part, swapped(col_part, CORE), col_part)
+    (col_part,) = call(join_kernel, "join", [((2 * SLOTS, group), f32)], col_part, swapped(col_part, CORE))
     col_y = swapped(col_part, Y)
-    (row_part,) = call(join_kernel, "join", [parts], row_part, swapped(row_part, X1), col_y)
+    (row_part,) = call(join_kernel, "join", [parts], row_part, swapped(row_part, X1))
     lse, row_sums, col_sums = call(
         lse_kernel, "lse", [((2, group), f32), few, few],
         row_part, swapped(row_part, X3), col_part, col_y,
@@ -404,36 +417,44 @@
         weight_kernel, "weight", [heavy, heavy], first, second, third, lse, positive
     )
     wide = ((rows, width), f32)
-    img_back, part1, part3, token = call(image_kernel, "image", [wide] * 3 + [few], w01, w23, txts)
-    (sums,) = call(half_kernel, "half", [few], row_sums, row_core, col_sums, col1, token)
-    core_part, part2 = call(
-        early_kernel, "early", [((2 * rows, width), bf16), block], w01, w23, near, far, txts, sums
+    pair = ((2 * rows, width), bf16)
+    core_part, part2 = call(early_kernel, "early", [pair, block], w01, w23, near, far, txts)
+    sums, core_part, part2 = call(
+        half_kernel, "half", [few, pair, block],
+        row_sums, row_core, col_sums, col1, core_part, part2, part2,
     )
     core_part, relayed = swapped(core_part, CORE), moved(part2, relay)
     txt_back, txt_next, token = call(
-        text_kernel, "text", [wide] * 2 + [few], w01, w23, near, far, sums
-    )
-    (sums,) = call(side_kernel, "side", [few], sums, swapped(sums, 1, "dp"), token)
-    (sums,) = call(add_kernel, "add", [few], sums, moved(sums, by_sides))
+        text_kernel, "text", [wide, wide, few], w01, w23, near, far, sums
+    )
+    (sums,) = call(side_kernel, "side", [few], sums, swapped(sums, 1, "dp"), token, token)
+    sums_got = moved(sums, by_sides)
+    img_back, first, late = call(
+        image_kernel, "image", [wide, block, wide], w01, w23, txts, sums
+    )
+    part_y, first = call(
+        across_kernel, "across", [block] * 2, txt_next, core_part, first, sums
+    )
+    (late,) = call(late_kernel, "late", [block], late, relayed)
+    (sums,) = call(side_kernel, "side", [few], sums, sums_got, part_y, late)
+    part_y, first, late = swapped(part_y, Y), moved(first, relay), moved(late, other_way)
     (held,) = call(total_kernel, "total", [few], sums, swapped(sums, CORE))
-    part1, part3, part_y = call(
-        away_kernel, "away", [block] * 3, part1, part3, txt_next, relayed, core_part, held
-    )
-    part1, part3, part_y = swapped(part1, X1), swapped(part3, X3), swapped(part_y, Y)
     (held,) = call(add_kernel, "add", [few], held, moved(held, by_planes))
     (held,) = call(planes_kernel, "planes", [few], held, swapped(held, CORE))
-    (held,) = call(add_kernel, "add", [few], held, moved(held, by_far_planes))
     image_grad, text_grad, token = call(
         grad_kernel, "grad", [block] * 2 + [few],
-        logit_scale, image, text, img_back, txt_back, core_part, part1, part3, part_y, scalar=True,
+        logit_scale, image, text, img_back, txt_back, core_part, first, late, part_y, scalar=True,
+    )
+    (held,) = call(
+        side_kernel, "side", [few], held, moved(held, by_far_planes), token, token
     )
     total_rows = rows * lax.axis_size("blk") * lax.axis_size("dp")
     loss, scale_grad = pl.pallas_call(
         functools.partial(scalar_kernel, total_rows), name="scalar",
         out_shape=[jax.ShapeDtypeStruct((1,), f32)] * 2,
-        in_specs=[SMEM, VMEM, VMEM, VMEM], out_specs=[SMEM] * 2,
+        in_specs=[SMEM, VMEM, VMEM], out_specs=[SMEM] * 2,
         compiler_params=PARAMS,
-    )(logit_scale, held, swapped(held, CORE), token)
+    )(logit_scale, held, swapped(held, CORE))
     return (loss, scale_grad, image_grad, text_grad)
 
 

time: 74.4 us -> 67.3 us (0.905)
  waiting for transfers between devices: 24.1 us -> 14.7 us
  starting transfers between devices: 33.6 us -> 35.8 us
    ppermute x19 -> x17, waiting for transfers between devices: 14.4 us -> 9.31 us  [swapped(): lax.ppermute(value, axis, [(i, i ^ bits) for i in range(lax.axis_size(axi...]
    ppermute x5 -> x7, waiting for transfers between devices: 9.67 us -> 5.42 us  [moved(): return lax.ppermute(value, ('dp', 'blk'), pairs)]
    ppermute x5 -> x7, starting transfers between devices: 11.6 us -> 13.5 us  [moved(): return lax.ppermute(value, ('dp', 'blk'), pairs)]
    ppermute x19 -> x17, starting transfers between devices: 22 us -> 22.2 us  [swapped(): lax.ppermute(value, axis, [(i, i ^ bits) for i in range(lax.axis_size(axi...]
    pallas_call x21 -> x22, Pallas kernels: 12.3 us -> 12.4 us  [call(): pl.pallas_call(kernel, out_shape=[jax.ShapeDtypeStruct(s, d) for s, d in...]
  transfers between devices with their start and end apart: 24 -> 24, of which waited for: 14 -> 11; matrix products, arithmetic and copies ran while one was open for 0% -> 0% of each run, Pallas kernels for 12% -> 16%
where the time goes in v4:
time: 67.3 us; the launch traced here: 67.1 us
  starting transfers between devices  35.8 us (53%)
  waiting for transfers between devices  14.7 us (22%)
  Pallas kernels  13 us (19%)
  local copies, waits for them, and re-layouts  2 us (3%)
  between operations  1.63 us (2%)
    ppermute x17, starting transfers between devices, swapped(): lax.ppermute(value, axis, [(i, i ^ bits) for i in range(lax.axis_size(axi...  22.2 us
    ppermute x7, starting transfers between devices, moved(): return lax.ppermute(value, ('dp', 'blk'), pairs)  13.5 us
    pallas_call x22, Pallas kernels, call(): pl.pallas_call(kernel, out_shape=[jax.ShapeDtypeStruct(s, d) for s, d in...  12.4 us
    ppermute x17, waiting for transfers between devices, swapped(): lax.ppermute(value, axis, [(i, i ^ bits) for i in range(lax.axis_size(axi...  9.31 us
    ppermute x7, waiting for transfers between devices, moved(): return lax.ppermute(value, ('dp', 'blk'), pairs)  5.42 us
    unnamed x10, local copies, waits for them, and re-layouts  2 us
  transfers between devices with their start and end apart: 24, of which 11 were waited for; matrix products, arithmetic and copies ran while one was open for 0% of the time, Pallas kernels for 16%

profile of v4, /device:TPU:1, one launch (start us, length us, event | category | flops | bytes accessed | tf_op | source)
XLA Modules:
  0.0 67.1 jit_solution(17781587668216704763)
XLA Ops:
  0.6 3.4 %collective-permute-start.1 = (bf16[256,768]{1,0:T(8,128)(2,1)}, bf16[256,768]{1,0:T(8,128)(2,1)S(1)}, u32[]{:S(2)}, u32[]{:S(2)}) collective-permute-start(bf16[256,768]{1,0:T(8,128)(2,1)} %image.5), channel_id=1, source_target_pairs={{0,12},{1,13},{2,14},{3,15},{4,8},{5,9},{6,10},{7,11},{8,4},{9,5},... | collective-permute-start | bytes 1179656 | tf_op jit(solution)/shard_map/ppermute | solution.py:29
  4.0 0.0 collective-permute-start
  4.0 2.9 %collective-permute-start.3 = (bf16[256,768]{1,0:T(8,128)(2,1)}, bf16[256,768]{1,0:T(8,128)(2,1)S(1)}, u32[]{:S(2)}, u32[]{:S(2)}) collective-permute-start(bf16[256,768]{1,0:T(8,128)(2,1)} %text.5), channel_id=1, source_target_pairs={{0,2},{1,3},{2,0},{3,1},{4,6},{5,7},{6,4},{7,5},{8,10},{9,11},{10,... | collective-permute-start | bytes 1179656 | tf_op jit(solution)/shard_map/ppermute | solution.py:29
  6.9 1.5 %collective-permute-start.5 = (bf16[256,768]{1,0:T(8,128)(2,1)}, bf16[256,768]{1,0:T(8,128)(2,1)S(1)}, u32[]{:S(2)}, u32[]{:S(2)}) collective-permute-start(bf16[256,768]{1,0:T(8,128)(2,1)} %text.5), channel_id=1, source_target_pairs={{0,1},{1,0},{2,3},{3,2},{4,5},{5,4},{6,7},{7,6},{8,9},{9,8},{10,11... | collective-permute-start | bytes 1179656 | tf_op jit(solution)/shard_map/ppermute | solution.py:29
  9.1 0.0 copy-start
  9.1 1.0 %copy-done = bf16[256,768]{1,0:T(8,128)(2,1)S(1)} copy-done((bf16[256,768]{1,0:T(8,128)(2,1)S(1)}, bf16[256,768]{1,0:T(8,128)(2,1)}, u32[]{:S(2)}) %copy-start) | copy-done | bytes 393240
  10.1 1.0 %copy-done.2 = bf16[256,768]{1,0:T(8,128)(2,1)S(1)} copy-done((bf16[256,768]{1,0:T(8,128)(2,1)S(1)}, bf16[256,768]{1,0:T(8,128)(2,1)}, u32[]{:S(2)}) %copy-start.2) | copy-done | bytes 393240
  11.0 0.2 own.1
  11.3 0.8 %collective-permute-done.1.i3 = bf16[256,768]{1,0:T(8,128)(2,1)S(1)} collective-permute-done((bf16[256,768]{1,0:T(8,128)(2,1)}, bf16[256,768]{1,0:T(8,128)(2,1)S(1)}, u32[]{:S(2)}, u32[]{:S(2)}) %collective-permute-start.1) | collective-permute-done | bytes 393248 | tf_op jit(solution)/shard_map/ppermute | solution.py:29
  12.1 1.8 %collective-permute-done.i1 = bf16[256,768]{1,0:T(8,128)(2,1)S(1)} collective-permute-done((bf16[256,768]{1,0:T(8,128)(2,1)}, bf16[256,768]{1,0:T(8,128)(2,1)S(1)}, u32[]{:S(2)}, u32[]{:S(2)}) %collective-permute-start) | collective-permute-done | bytes 393248 | tf_op jit(solution)/shard_map/ppermute | solution.py:29
  13.9 1.6 %collective-permute-start.2 = (bf16[256,768]{1,0:T(8,128)(2,1)S(1)}, bf16[256,768]{1,0:T(8,128)(2,1)S(1)}, u32[]{:S(2)}, u32[]{:S(2)}) collective-permute-start(bf16[256,768]{1,0:T(8,128)(2,1)S(1)} %pick.1), channel_id=1, source_target_pairs={{0,4},{1,13},{2,6},{3,15},{4,0},{5,9},{6,2},{7,11},{8,12},{9,5},{1... | collective-permute-start | bytes 1179656 | tf_op jit(solution)/shard_map/ppermute | solution.py:36
  15.6 0.0 collective-permute-done.3.t2
  15.6 1.7 %collective-permute-start.4 = (bf16[256,768]{1,0:T(8,128)(2,1)S(1)}, bf16[256,768]{1,0:T(8,128)(2,1)S(1)}, u32[]{:S(2)}, u32[]{:S(2)}) collective-permute-start(bf16[256,768]{1,0:T(8,128)(2,1)S(1)} %collective-permute-done.3.t2), channel_id=1, source_target_pairs={{0,1},{1,0},{2,3},{3,2},{4,5},{5,4},{6,7},{7,6},{8,9},{9,8},{10,11... | collective-permute-start | bytes 1179656 | tf_op jit(solution)/shard_map/ppermute | solution.py:29
  17.3 0.0 collective-permute-done.5.t1
  17.3 2.5 %first.1 = (bf16[768,768]{1,0:T(8,128)(2,1)S(1)}, bf16[768,768]{1,0:T(8,128)(2,1)S(1)}, f32[768,768]{1,0:T(8,128)S(1)}, f32[4,1024]{1,0:T(4,128)S(1)}, f32[4,1024]{1,0:T(4,128)S(1)}) custom-call(f32[1]{0:T(128)S(6)} %copy.8.scale, bf16[256,768]{1,0:T(8,128)(2,1)S(1)} %get-tuple-element.42.before.i0, bf16[256,768]{1,0:T(8,128)(2,1)S(1)} %get-tuple-element.43.t0, ...), custom_call_target="tpu_custom_call" | custom-call | flops 13200000000 | bytes 7111684 | tf_op jit(solution)/shard_map/first/pallas_call | solution.py:63
  19.8 0.0 collective-permute-done.4.t3
  19.8 1.1 %second.1 = (bf16[1024,768]{1,0:T(8,128)(2,1)S(1)}, f32[768,256]{1,0:T(8,128)S(1)}, f32[4,1024]{1,0:T(4,128)S(1)}, f32[4,1024]{1,0:T(4,128)S(1)}) custom-call(f32[1]{0:T(128)S(6)} %copy.8.scale, bf16[256,768]{1,0:T(8,128)(2,1)S(1)} %collective-permute-done.4.t3, bf16[768,768]{1,0:T(8,128)(2,1)S(1)} %get-tuple-element.44.near, ...), custom_call_target="tpu_custom_call" | custom-call | flops 8800000000 | bytes 5177348 | tf_op jit(solution)/shard_map/second/pallas_call | solution.py:63
  20.9 0.9 %collective-permute-done.2.i2 = bf16[256,768]{1,0:T(8,128)(2,1)S(1)} collective-permute-done((bf16[256,768]{1,0:T(8,128)(2,1)S(1)}, bf16[256,768]{1,0:T(8,128)(2,1)S(1)}, u32[]{:S(2)}, u32[]{:S(2)}) %collective-permute-start.2) | collective-permute-done | bytes 393248 | tf_op jit(solution)/shard_map/ppermute | solution.py:36
  21.9 1.2 %third.1 = (bf16[256,768]{1,0:T(8,128)(2,1)S(1)}, f32[256,1024]{1,0:T(8,128)S(1)}, f32[4,1024]{1,0:T(4,128)S(1)}, f32[4,1024]{1,0:T(4,128)S(1)}) custom-call(f32[1]{0:T(128)S(6)} %copy.8.scale, bf16[256,768]{1,0:T(8,128)(2,1)S(1)} %collective-permute-done.2.i2, bf16[1024,768]{1,0:T(8,128)(2,1)S(1)} %get-tuple-element.48.txts, ...), custom_call_target="tpu_custom_call" | custom-call | flops 1264999936 | bytes 3473412 | tf_op jit(solution)/shard_map/third/pallas_call | solution.py:63
  23.0 1.9 %collective-permute-start.8 = (f32[4,1024]{1,0:T(4,128)S(1)}, f32[4,1024]{1,0:T(4,128)S(1)}, u32[]{:S(2)}, u32[]{:S(2)}) collective-permute-start(f32[4,1024]{1,0:T(4,128)S(1)} %get-tuple-element.52.mine), channel_id=1, source_target_pairs={{0,1},{1,0},{2,3},{3,2},{4,5},{5,4},{6,7},{7,6},{8,9},{9,8},{10,11... | collective-permute-start | bytes 49160 | tf_op jit(solution)/shard_map/ppermute | solution.py:29
  24.9 0.0 collective-permute-start.6
  25.0 0.8 %collective-permute-done.8.other = f32[4,1024]{1,0:T(4,128)S(1)} collective-permute-done((f32[4,1024]{1,0:T(4,128)S(1)}, f32[4,1024]{1,0:T(4,128)S(1)}, u32[]{:S(2)}, u32[]{:S(2)}) %collective-permute-start.8) | collective-permute-done | bytes 16416 | tf_op jit(solution)/shard_map/ppermute | solution.py:29
  25.8 3.0 %collective-permute-start.9 = (f32[8,1024]{1,0:T(8,128)S(1)}, f32[8,1024]{1,0:T(8,128)S(1)}, u32[]{:S(2)}, u32[]{:S(2)}) collective-permute-start(f32[8,1024]{1,0:T(8,128)S(1)} %join.3.col), channel_id=1, source_target_pairs={{0,2},{1,3},{2,0},{3,1},{4,6},{5,7},{6,4},{7,5},{8,10},{9,11},{10,... | collective-permute-start | bytes 98312 | tf_op jit(solution)/shard_map/ppermute | solution.py:29
  28.8 0.0 collective-permute-done.6.other
  28.8 1.3 %collective-permute-start.7 = (f32[4,1024]{1,0:T(4,128)S(1)}, f32[4,1024]{1,0:T(4,128)S(1)}, u32[]{:S(2)}, u32[]{:S(2)}) collective-permute-start(f32[4,1024]{1,0:T(4,128)S(1)} %join.2.row), channel_id=1, source_target_pairs={{0,12},{1,13},{2,14},{3,15},{4,8},{5,9},{6,10},{7,11},{8,4},{9,5},... | collective-permute-start | bytes 49160 | tf_op jit(solution)/shard_map/ppermute | solution.py:29
  30.1 2.6 %collective-permute-done.7.row3 = f32[4,1024]{1,0:T(4,128)S(1)} collective-permute-done((f32[4,1024]{1,0:T(4,128)S(1)}, f32[4,1024]{1,0:T(4,128)S(1)}, u32[]{:S(2)}, u32[]{:S(2)}) %collective-permute-start.7) | collective-permute-done | bytes 16416 | tf_op jit(solution)/shard_map/ppermute | solution.py:29
  32.7 0.0 collective-permute-done.9.col2
  32.7 0.1 lse.1
  32.9 1.9 %collective-permute-start.10 = (f32[8,128]{1,0:T(8,128)S(1)}, f32[8,128]{1,0:T(8,128)S(1)}, u32[]{:S(2)}, u32[]{:S(2)}) collective-permute-start(f32[8,128]{1,0:T(8,128)S(1)} %get-tuple-element.53.row), channel_id=1, source_target_pairs={{0,1},{1,0},{2,3},{3,2},{4,5},{5,4},{6,7},{7,6},{8,9},{9,8},{10,11... | collective-permute-start | bytes 12296 | tf_op jit(solution)/shard_map/ppermute | solution.py:29
  34.7 0.0 collective-permute-start.11
  34.7 1.3 %weight.1 = (bf16[512,1024]{1,0:T(8,128)(2,1)S(1)}, bf16[512,1024]{1,0:T(8,128)(2,1)S(1)}) custom-call(f32[768,768]{1,0:T(8,128)S(1)} %get-tuple-element.55.first, f32[768,256]{1,0:T(8,128)S(1)} %get-tuple-element.56.second, f32[256,1024]{1,0:T(8,128)S(1)} %get-tuple-element.57.third, f32[2,1024]{1,0:T(2,128)S(1)} %get-tuple-element.58.lse, s32[1,256]{1,0:T(1,128)S(1)} %bitcast.2), custom_call_target="tpu_custom_call" | custom-call | flops 1430000000 | bytes 6300672 | tf_op jit(solution)/shard_map/weight/pallas_call | solution.py:63
  36.0 1.4 %early.1 = (bf16[512,768]{1,0:T(8,128)(2,1)S(1)}, bf16[256,768]{1,0:T(8,128)(2,1)S(1)}) custom-call(bf16[512,1024]{1,0:T(8,128)(2,1)S(1)} %get-tuple-element.59.w01, bf16[512,1024]{1,0:T(8,128)(2,1)S(1)} %get-tuple-element.60.w23, bf16[768,768]{1,0:T(8,128)(2,1)S(1)} %get-tuple-element.44.near, bf16[256,768]{1,0:T(8,128)(2,1)S(1)} %get-tuple-element.61.far, ...), custom_call_target="tpu_custom_call" | custom-call | flops 1540000000 | bytes 6422528 | tf_op jit(solution)/shard_map/early/pallas_call | solution.py:63
  37.4 0.0 collective-permute-done.10.row_core
  37.4 0.0 collective-permute-done.11.col1
  37.4 0.1 half.1
  37.5 1.2 %collective-permute-start.14 = (bf16[512,768]{1,0:T(8,128)(2,1)S(1)}, bf16[512,768]{1,0:T(8,128)(2,1)S(1)}, u32[]{:S(2)}, u32[]{:S(2)}) collective-permute-start(bf16[512,768]{1,0:T(8,128)(2,1)S(1)} %get-tuple-element.67), channel_id=1, source_target_pairs={{0,1},{1,0},{2,3},{3,2},{4,5},{5,4},{6,7},{7,6},{8,9},{9,8},{10,11... | collective-permute-start | bytes 2359304 | tf_op jit(solution)/shard_map/ppermute | solution.py:29
  38.8 1.2 %collective-permute-start.15 = (bf16[256,768]{1,0:T(8,128)(2,1)S(1)}, bf16[256,768]{1,0:T(8,128)(2,1)S(1)}, u32[]{:S(2)}, u32[]{:S(2)}) collective-permute-start(bf16[256,768]{1,0:T(8,128)(2,1)S(1)} %get-tuple-element.71), channel_id=1, source_target_pairs={{0,4},{1,13},{2,6},{3,15},{4,0},{5,9},{6,2},{7,11},{8,12},{9,5},{1... | collective-permute-start | bytes 1179656 | tf_op jit(solution)/shard_map/ppermute | solution.py:36
  40.0 0.6 collective-permute-start.12
  40.6 1.0 %text.4 = (f32[256,768]{1,0:T(8,128)S(1)}, f32[256,768]{1,0:T(8,128)S(1)}, f32[8,128]{1,0:T(8,128)S(1)}) custom-call(bf16[512,1024]{1,0:T(8,128)(2,1)S(1)} %get-tuple-element.59.w01, bf16[512,1024]{1,0:T(8,128)(2,1)S(1)} %get-tuple-element.60.w23, bf16[768,768]{1,0:T(8,128)(2,1)S(1)} %get-tuple-element.44.near, bf16[256,768]{1,0:T(8,128)(2,1)S(1)} %get-tuple-element.61.far, ...), custom_call_target="tpu_custom_call" | custom-call | flops 1210000000 | bytes 5251072 | tf_op jit(solution)/shard_map/text/pallas_call | solution.py:63
  41.7 1.1 %collective-permute-done.12.b = f32[8,128]{1,0:T(8,128)S(1)} collective-permute-done((f32[8,128]{1,0:T(8,128)S(1)}, f32[8,128]{1,0:T(8,128)S(1)}, u32[]{:S(2)}, u32[]{:S(2)}) %collective-permute-start.12) | collective-permute-done | bytes 4128 | tf_op jit(solution)/shard_map/ppermute | solution.py:29
  42.8 1.5 %collective-permute-start.13 = (f32[8,128]{1,0:T(8,128)S(1)}, f32[8,128]{1,0:T(8,128)S(1)}, u32[]{:S(2)}, u32[]{:S(2)}) collective-permute-start(f32[8,128]{1,0:T(8,128)S(1)} %side.3.before.a), channel_id=1, source_target_pairs={{0,18},{1,13},{2,16},{3,15},{4,22},{5,9},{6,20},{7,11},{8,26},{9,5... | collective-permute-start | bytes 12296 | tf_op jit(solution)/shard_map/ppermute | solution.py:36
  44.2 1.4 %image.4 = (f32[256,768]{1,0:T(8,128)S(1)}, bf16[256,768]{1,0:T(8,128)(2,1)S(1)}, f32[256,768]{1,0:T(8,128)S(1)}) custom-call(bf16[512,1024]{1,0:T(8,128)(2,1)S(1)} %get-tuple-element.59.w01, bf16[512,1024]{1,0:T(8,128)(2,1)S(1)} %get-tuple-element.60.w23, bf16[1024,768]{1,0:T(8,128)(2,1)S(1)} %get-tuple-element.48.txts, f32[8,128]{1,0:T(8,128)S(1)} %side.3.before.a), custom_call_target="tpu_custom_call" | custom-call | flops 1210000000 | bytes 5640192 | tf_op jit(solution)/shard_map/image/pallas_call | solution.py:63
  45.6 1.0 %collective-permute-done.15.relayed = bf16[256,768]{1,0:T(8,128)(2,1)S(1)} collective-permute-done((bf16[256,768]{1,0:T(8,128)(2,1)S(1)}, bf16[256,768]{1,0:T(8,128)(2,1)S(1)}, u32[]{:S(2)}, u32[]{:S(2)}) %collective-permute-start.15) | collective-permute-done | bytes 393248 | tf_op jit(solution)/shard_map/ppermute | solution.py:36
  46.6 0.1 late.1.before_too
  46.7 0.0 collective-permute-done.14.core_part
  46.7 0.1 across.1
  46.8 0.0 collective-permute-done.13.b
  46.8 1.6 %collective-permute-start.16 = (f32[8,128]{1,0:T(8,128)S(1)}, f32[8,128]{1,0:T(8,128)S(1)}, u32[]{:S(2)}, u32[]{:S(2)}) collective-permute-start(f32[8,128]{1,0:T(8,128)S(1)} %side.4.mine), channel_id=1, source_target_pairs={{0,1},{1,0},{2,3},{3,2},{4,5},{5,4},{6,7},{7,6},{8,9},{9,8},{10,11... | collective-permute-start | bytes 12296 | tf_op jit(solution)/shard_map/ppermute | solution.py:29
  48.5 0.6 collective-permute-start.21
  49.1 1.0 %collective-permute-start.22 = (bf16[256,768]{1,0:T(8,128)(2,1)S(1)}, bf16[256,768]{1,0:T(8,128)(2,1)S(1)}, u32[]{:S(2)}, u32[]{:S(2)}) collective-permute-start(bf16[256,768]{1,0:T(8,128)(2,1)S(1)} %get-tuple-element.69.before), channel_id=1, source_target_pairs={{0,2},{1,3},{2,0},{3,1},{4,6},{5,7},{6,4},{7,5},{8,10},{9,11},{10,... | collective-permute-start | bytes 1179656 | tf_op jit(solution)/shard_map/ppermute | solution.py:29
  50.1 1.2 %collective-permute-start.20 = (bf16[256,768]{1,0:T(8,128)(2,1)S(1)}, bf16[256,768]{1,0:T(8,128)(2,1)S(1)}, u32[]{:S(2)}, u32[]{:S(2)}) collective-permute-start(bf16[256,768]{1,0:T(8,128)(2,1)S(1)} %get-tuple-element.74), channel_id=1, source_target_pairs={{0,4},{1,13},{2,6},{3,15},{4,0},{5,9},{6,2},{7,11},{8,12},{9,5},{1... | collective-permute-start | bytes 1179656 | tf_op jit(solution)/shard_map/ppermute | solution.py:36
  51.3 0.0 collective-permute-done.16.other
  51.3 0.1 total.1.a
  51.5 5.7 %collective-permute-start.17 = (f32[8,128]{1,0:T(8,128)S(1)}, f32[8,128]{1,0:T(8,128)S(1)}, u32[]{:S(2)}, u32[]{:S(2)}) collective-permute-start(f32[8,128]{1,0:T(8,128)S(1)} %total.1.a), channel_id=1, source_target_pairs={{0,32},{1,225},{2,34},{3,227},{4,36},{5,229},{6,38},{7,231},{8,40}... | collective-permute-start | bytes 12296 | tf_op jit(solution)/shard_map/ppermute | solution.py:36
  57.1 1.3 %collective-permute-done.17.b = f32[8,128]{1,0:T(8,128)S(1)} collective-permute-done((f32[8,128]{1,0:T(8,128)S(1)}, f32[8,128]{1,0:T(8,128)S(1)}, u32[]{:S(2)}, u32[]{:S(2)}) %collective-permute-start.17) | collective-permute-done | bytes 4128 | tf_op jit(solution)/shard_map/ppermute | solution.py:36
  58.4 0.0 collective-permute-start.18
  58.4 1.2 %collective-permute-done.18.other = f32[8,128]{1,0:T(8,128)S(1)} collective-permute-done((f32[8,128]{1,0:T(8,128)S(1)}, f32[8,128]{1,0:T(8,128)S(1)}, u32[]{:S(2)}, u32[]{:S(2)}) %collective-permute-start.18) | collective-permute-done | bytes 4128 | tf_op jit(solution)/shard_map/ppermute | solution.py:29
  59.6 1.7 %collective-permute-start.19 = (f32[8,128]{1,0:T(8,128)S(1)}, f32[8,128]{1,0:T(8,128)S(1)}, u32[]{:S(2)}, u32[]{:S(2)}) collective-permute-start(f32[8,128]{1,0:T(8,128)S(1)} %planes.1.a), channel_id=1, source_target_pairs={{0,160},{1,97},{2,162},{3,99},{4,164},{5,101},{6,166},{7,103},{8,1... | collective-permute-start | bytes 12296 | tf_op jit(solution)/shard_map/ppermute | solution.py:36
  61.3 0.0 collective-permute-done.21.late
  61.3 1.6 %grad.1 = (bf16[256,768]{1,0:T(8,128)(2,1)}, bf16[256,768]{1,0:T(8,128)(2,1)}, f32[8,128]{1,0:T(8,128)S(1)}) custom-call(f32[1]{0:T(128)S(6)} %copy.8.scale, bf16[256,768]{1,0:T(8,128)(2,1)S(1)} %copy-done.1, bf16[256,768]{1,0:T(8,128)(2,1)S(1)} %copy-done.3, f32[256,768]{1,0:T(8,128)S(1)} %get-tuple-element.72.img_back, ...), custom_call_target="tpu_custom_call" | custom-call | flops 1760000000 | bytes 5115908 | tf_op jit(solution)/shard_map/grad/pallas_call | solution.py:63
  62.9 2.2 %collective-permute-done.19.b = f32[8,128]{1,0:T(8,128)S(1)} collective-permute-done((f32[8,128]{1,0:T(8,128)S(1)}, f32[8,128]{1,0:T(8,128)S(1)}, u32[]{:S(2)}, u32[]{:S(2)}) %collective-permute-start.19) | collective-permute-done | bytes 4128 | tf_op jit(solution)/shard_map/ppermute | solution.py:36
  65.1 0.1 collective-permute-start.23
  65.2 1.1 %collective-permute-done.23.other = f32[8,128]{1,0:T(8,128)S(1)} collective-permute-done((f32[8,128]{1,0:T(8,128)S(1)}, f32[8,128]{1,0:T(8,128)S(1)}, u32[]{:S(2)}, u32[]{:S(2)}) %collective-permute-start.23) | collective-permute-done | bytes 4128 | tf_op jit(solution)/shard_map/ppermute | solution.py:29
  66.3 0.7 scalar.1
  (17 shorter events, 0.1 us)
Async XLA Ops:
  0.6 11.5 %collective-permute-start.1 = (bf16[256,768]{1,0:T(8,128)(2,1)}, bf16[256,768]{1,0:T(8,128)(2,1)S(1)}, u32[]{:S(2)}, u32[]{:S(2)}) collective-permute-start(bf16[256,768]{1,0:T(8,128)(2,1)} %image.5), channel_id=1, source_target_pairs={{0,12},{1,13},{2,14},{3,15},{4,8},{5,9},{6,10},{7,11},{8,4},{9,5},... | collective-permute-start | bytes 1179656 | tf_op jit(solution)/shard_map/ppermute | solution.py:29
  4.0 9.9 %collective-permute-start = (bf16[256,768]{1,0:T(8,128)(2,1)}, bf16[256,768]{1,0:T(8,128)(2,1)S(1)}, u32[]{:S(2)}, u32[]{:S(2)}) collective-permute-start(bf16[256,768]{1,0:T(8,128)(2,1)} %image.5), channel_id=1, source_target_pairs={{0,4},{1,5},{2,6},{3,7},{4,0},{5,1},{6,2},{7,3},{8,12},{9,13},{10,... | collective-permute-start | bytes 1179656 | tf_op jit(solution)/shard_map/ppermute | solution.py:29
  4.0 11.5 %collective-permute-start.3 = (bf16[256,768]{1,0:T(8,128)(2,1)}, bf16[256,768]{1,0:T(8,128)(2,1)S(1)}, u32[]{:S(2)}, u32[]{:S(2)}) collective-permute-start(bf16[256,768]{1,0:T(8,128)(2,1)} %text.5), channel_id=1, source_target_pairs={{0,2},{1,3},{2,0},{3,1},{4,6},{5,7},{6,4},{7,5},{8,10},{9,11},{10,... | collective-permute-start | bytes 1179656 | tf_op jit(solution)/shard_map/ppermute | solution.py:29
  6.9 10.3 %collective-permute-start.5 = (bf16[256,768]{1,0:T(8,128)(2,1)}, bf16[256,768]{1,0:T(8,128)(2,1)S(1)}, u32[]{:S(2)}, u32[]{:S(2)}) collective-permute-start(bf16[256,768]{1,0:T(8,128)(2,1)} %text.5), channel_id=1, source_target_pairs={{0,1},{1,0},{2,3},{3,2},{4,5},{5,4},{6,7},{7,6},{8,9},{9,8},{10,11... | collective-permute-start | bytes 1179656 | tf_op jit(solution)/shard_map/ppermute | solution.py:29
  9.1 1.0 %copy-start = (bf16[256,768]{1,0:T(8,128)(2,1)S(1)}, bf16[256,768]{1,0:T(8,128)(2,1)}, u32[]{:S(2)}) copy-start(bf16[256,768]{1,0:T(8,128)(2,1)} %image.5) | copy-start | bytes 1179652
  10.1 1.0 %copy-start.2 = (bf16[256,768]{1,0:T(8,128)(2,1)S(1)}, bf16[256,768]{1,0:T(8,128)(2,1)}, u32[]{:S(2)}) copy-start(bf16[256,768]{1,0:T(8,128)(2,1)} %text.5) | copy-start | bytes 1179652
  13.9 3.4 %copy-start.4 = (s32[256]{0:T(256)S(1)}, s32[256]{0:T(256)}, u32[]{:S(2)}) copy-start(s32[256]{0:T(256)} %param.6) | copy-start | bytes 3076
  13.9 7.9 %collective-permute-start.2 = (bf16[256,768]{1,0:T(8,128)(2,1)S(1)}, bf16[256,768]{1,0:T(8,128)(2,1)S(1)}, u32[]{:S(2)}, u32[]{:S(2)}) collective-permute-start(bf16[256,768]{1,0:T(8,128)(2,1)S(1)} %pick.1), channel_id=1, source_target_pairs={{0,4},{1,13},{2,6},{3,15},{4,0},{5,9},{6,2},{7,11},{8,12},{9,5},{1... | collective-permute-start | bytes 1179656 | tf_op jit(solution)/shard_map/ppermute | solution.py:36
  15.6 4.3 %collective-permute-start.4 = (bf16[256,768]{1,0:T(8,128)(2,1)S(1)}, bf16[256,768]{1,0:T(8,128)(2,1)S(1)}, u32[]{:S(2)}, u32[]{:S(2)}) collective-permute-start(bf16[256,768]{1,0:T(8,128)(2,1)S(1)} %collective-permute-done.3.t2), channel_id=1, source_target_pairs={{0,1},{1,0},{2,3},{3,2},{4,5},{5,4},{6,7},{7,6},{8,9},{9,8},{10,11... | collective-permute-start | bytes 1179656 | tf_op jit(solution)/shard_map/ppermute | solution.py:29
  23.0 2.7 %collective-permute-start.8 = (f32[4,1024]{1,0:T(4,128)S(1)}, f32[4,1024]{1,0:T(4,128)S(1)}, u32[]{:S(2)}, u32[]{:S(2)}) collective-permute-start(f32[4,1024]{1,0:T(4,128)S(1)} %get-tuple-element.52.mine), channel_id=1, source_target_pairs={{0,1},{1,0},{2,3},{3,2},{4,5},{5,4},{6,7},{7,6},{8,9},{9,8},{10,11... | collective-permute-start | bytes 49160 | tf_op jit(solution)/shard_map/ppermute | solution.py:29
  24.9 3.9 %collective-permute-start.6 = (f32[4,1024]{1,0:T(4,128)S(1)}, f32[4,1024]{1,0:T(4,128)S(1)}, u32[]{:S(2)}, u32[]{:S(2)}) collective-permute-start(f32[4,1024]{1,0:T(4,128)S(1)} %get-tuple-element.51.mine), channel_id=1, source_target_pairs={{0,4},{1,5},{2,6},{3,7},{4,0},{5,1},{6,2},{7,3},{8,12},{9,13},{10,... | collective-permute-start | bytes 49160 | tf_op jit(solution)/shard_map/ppermute | solution.py:29
  25.8 6.9 %collective-permute-start.9 = (f32[8,1024]{1,0:T(8,128)S(1)}, f32[8,1024]{1,0:T(8,128)S(1)}, u32[]{:S(2)}, u32[]{:S(2)}) collective-permute-start(f32[8,1024]{1,0:T(8,128)S(1)} %join.3.col), channel_id=1, source_target_pairs={{0,2},{1,3},{2,0},{3,1},{4,6},{5,7},{6,4},{7,5},{8,10},{9,11},{10,... | collective-permute-start | bytes 98312 | tf_op jit(solution)/shard_map/ppermute | solution.py:29
  28.8 3.9 %collective-permute-start.7 = (f32[4,1024]{1,0:T(4,128)S(1)}, f32[4,1024]{1,0:T(4,128)S(1)}, u32[]{:S(2)}, u32[]{:S(2)}) collective-permute-start(f32[4,1024]{1,0:T(4,128)S(1)} %join.2.row), channel_id=1, source_target_pairs={{0,12},{1,13},{2,14},{3,15},{4,8},{5,9},{6,10},{7,11},{8,4},{9,5},... | collective-permute-start | bytes 49160 | tf_op jit(solution)/shard_map/ppermute | solution.py:29
  32.9 4.6 %collective-permute-start.10 = (f32[8,128]{1,0:T(8,128)S(1)}, f32[8,128]{1,0:T(8,128)S(1)}, u32[]{:S(2)}, u32[]{:S(2)}) collective-permute-start(f32[8,128]{1,0:T(8,128)S(1)} %get-tuple-element.53.row), channel_id=1, source_target_pairs={{0,1},{1,0},{2,3},{3,2},{4,5},{5,4},{6,7},{7,6},{8,9},{9,8},{10,11... | collective-permute-start | bytes 12296 | tf_op jit(solution)/shard_map/ppermute | solution.py:29
  34.7 2.7 %collective-permute-start.11 = (f32[8,128]{1,0:T(8,128)S(1)}, f32[8,128]{1,0:T(8,128)S(1)}, u32[]{:S(2)}, u32[]{:S(2)}) collective-permute-start(f32[8,128]{1,0:T(8,128)S(1)} %get-tuple-element.54.col), channel_id=1, source_target_pairs={{0,4},{1,5},{2,6},{3,7},{4,0},{5,1},{6,2},{7,3},{8,12},{9,13},{10,... | collective-permute-start | bytes 12296 | tf_op jit(solution)/shard_map/ppermute | solution.py:29
  37.5 9.1 %collective-permute-start.14 = (bf16[512,768]{1,0:T(8,128)(2,1)S(1)}, bf16[512,768]{1,0:T(8,128)(2,1)S(1)}, u32[]{:S(2)}, u32[]{:S(2)}) collective-permute-start(bf16[512,768]{1,0:T(8,128)(2,1)S(1)} %get-tuple-element.67), channel_id=1, source_target_pairs={{0,1},{1,0},{2,3},{3,2},{4,5},{5,4},{6,7},{7,6},{8,9},{9,8},{10,11... | collective-permute-start | bytes 2359304 | tf_op jit(solution)/shard_map/ppermute | solution.py:29
  38.8 7.8 %collective-permute-start.15 = (bf16[256,768]{1,0:T(8,128)(2,1)S(1)}, bf16[256,768]{1,0:T(8,128)(2,1)S(1)}, u32[]{:S(2)}, u32[]{:S(2)}) collective-permute-start(bf16[256,768]{1,0:T(8,128)(2,1)S(1)} %get-tuple-element.71), channel_id=1, source_target_pairs={{0,4},{1,13},{2,6},{3,15},{4,0},{5,9},{6,2},{7,11},{8,12},{9,5},{1... | collective-permute-start | bytes 1179656 | tf_op jit(solution)/shard_map/ppermute | solution.py:36
  40.0 2.8 %collective-permute-start.12 = (f32[8,128]{1,0:T(8,128)S(1)}, f32[8,128]{1,0:T(8,128)S(1)}, u32[]{:S(2)}, u32[]{:S(2)}) collective-permute-start(f32[8,128]{1,0:T(8,128)S(1)} %get-tuple-element.64.before.a), channel_id=1, source_target_pairs={{0,16},{16,0},{32,48},{48,32},{64,80},{80,64},{96,112},{112,96},{1... | collective-permute-start | bytes 12296 | tf_op jit(solution)/shard_map/ppermute | solution.py:29
  42.8 4.0 %collective-permute-start.13 = (f32[8,128]{1,0:T(8,128)S(1)}, f32[8,128]{1,0:T(8,128)S(1)}, u32[]{:S(2)}, u32[]{:S(2)}) collective-permute-start(f32[8,128]{1,0:T(8,128)S(1)} %side.3.before.a), channel_id=1, source_target_pairs={{0,18},{1,13},{2,16},{3,15},{4,22},{5,9},{6,20},{7,11},{8,26},{9,5... | collective-permute-start | bytes 12296 | tf_op jit(solution)/shard_map/ppermute | solution.py:36
  46.8 4.5 %collective-permute-start.16 = (f32[8,128]{1,0:T(8,128)S(1)}, f32[8,128]{1,0:T(8,128)S(1)}, u32[]{:S(2)}, u32[]{:S(2)}) collective-permute-start(f32[8,128]{1,0:T(8,128)S(1)} %side.4.mine), channel_id=1, source_target_pairs={{0,1},{1,0},{2,3},{3,2},{4,5},{5,4},{6,7},{7,6},{8,9},{9,8},{10,11... | collective-permute-start | bytes 12296 | tf_op jit(solution)/shard_map/ppermute | solution.py:29
  48.5 12.9 %collective-permute-start.21 = (bf16[256,768]{1,0:T(8,128)(2,1)S(1)}, bf16[256,768]{1,0:T(8,128)(2,1)S(1)}, u32[]{:S(2)}, u32[]{:S(2)}) collective-permute-start(bf16[256,768]{1,0:T(8,128)(2,1)S(1)} %late.1.before_too), channel_id=1, source_target_pairs={{0,12},{1,5},{2,14},{3,7},{4,8},{5,1},{6,10},{7,3},{8,4},{9,13},{1... | collective-permute-start | bytes 1179656 | tf_op jit(solution)/shard_map/ppermute | solution.py:36
  49.1 12.3 %collective-permute-start.22 = (bf16[256,768]{1,0:T(8,128)(2,1)S(1)}, bf16[256,768]{1,0:T(8,128)(2,1)S(1)}, u32[]{:S(2)}, u32[]{:S(2)}) collective-permute-start(bf16[256,768]{1,0:T(8,128)(2,1)S(1)} %get-tuple-element.69.before), channel_id=1, source_target_pairs={{0,2},{1,3},{2,0},{3,1},{4,6},{5,7},{6,4},{7,5},{8,10},{9,11},{10,... | collective-permute-start | bytes 1179656 | tf_op jit(solution)/shard_map/ppermute | solution.py:29
  50.1 11.2 %copy-start.1 = (bf16[256,768]{1,0:T(8,128)(2,1)S(1)}, bf16[256,768]{1,0:T(8,128)(2,1)}, u32[]{:S(2)}) copy-start(bf16[256,768]{1,0:T(8,128)(2,1)} %image.5) | copy-start | bytes 1179652
  50.1 11.2 %copy-start.3 = (bf16[256,768]{1,0:T(8,128)(2,1)S(1)}, bf16[256,768]{1,0:T(8,128)(2,1)}, u32[]{:S(2)}) copy-start(bf16[256,768]{1,0:T(8,128)(2,1)} %text.5) | copy-start | bytes 1179652
  50.1 11.2 %collective-permute-start.20 = (bf16[256,768]{1,0:T(8,128)(2,1)S(1)}, bf16[256,768]{1,0:T(8,128)(2,1)S(1)}, u32[]{:S(2)}, u32[]{:S(2)}) collective-permute-start(bf16[256,768]{1,0:T(8,128)(2,1)S(1)} %get-tuple-element.74), channel_id=1, source_target_pairs={{0,4},{1,13},{2,6},{3,15},{4,0},{5,9},{6,2},{7,11},{8,12},{9,5},{1... | collective-permute-start | bytes 1179656 | tf_op jit(solution)/shard_map/ppermute | solution.py:36
  51.5 7.0 %collective-permute-start.17 = (f32[8,128]{1,0:T(8,128)S(1)}, f32[8,128]{1,0:T(8,128)S(1)}, u32[]{:S(2)}, u32[]{:S(2)}) collective-permute-start(f32[8,128]{1,0:T(8,128)S(1)} %total.1.a), channel_id=1, source_target_pairs={{0,32},{1,225},{2,34},{3,227},{4,36},{5,229},{6,38},{7,231},{8,40}... | collective-permute-start | bytes 12296 | tf_op jit(solution)/shard_map/ppermute | solution.py:36
  58.4 1.2 %collective-permute-start.18 = (f32[8,128]{1,0:T(8,128)S(1)}, f32[8,128]{1,0:T(8,128)S(1)}, u32[]{:S(2)}, u32[]{:S(2)}) collective-permute-start(f32[8,128]{1,0:T(8,128)S(1)} %add.1.held), channel_id=1, source_target_pairs={{0,1},{1,0},{2,3},{3,2},{4,5},{5,4},{6,7},{7,6},{8,9},{9,8},{10,11... | collective-permute-start | bytes 12296 | tf_op jit(solution)/shard_map/ppermute | solution.py:29
  59.6 5.5 %collective-permute-start.19 = (f32[8,128]{1,0:T(8,128)S(1)}, f32[8,128]{1,0:T(8,128)S(1)}, u32[]{:S(2)}, u32[]{:S(2)}) collective-permute-start(f32[8,128]{1,0:T(8,128)S(1)} %planes.1.a), channel_id=1, source_target_pairs={{0,160},{1,97},{2,162},{3,99},{4,164},{5,101},{6,166},{7,103},{8,1... | collective-permute-start | bytes 12296 | tf_op jit(solution)/shard_map/ppermute | solution.py:36
  65.1 1.2 %collective-permute-start.23 = (f32[8,128]{1,0:T(8,128)S(1)}, f32[8,128]{1,0:T(8,128)S(1)}, u32[]{:S(2)}, u32[]{:S(2)}) collective-permute-start(f32[8,128]{1,0:T(8,128)S(1)} %side.5.held), channel_id=1, source_target_pairs={{0,1},{1,0},{2,3},{3,2},{4,5},{5,4},{6,7},{7,6},{8,9},{9,8},{10,11... | collective-permute-start | bytes 12296 | tf_op jit(solution)/shard_map/ppermute | solution.py:29

commit v5 on v4

--- a/solution.py
+++ b/solution.py
@@ -16,7 +16,7 @@
 SLOTS = 4
 LOW = -1e30
 COST = {
-    "total": 30,
+    "sides": 10, "total": 10,
     "pick": 5.0,
     "own": 0.25, "first": 12, "second": 8, "third": 1.15, "lse": 0.15, "weight": 1.3,
     "image": 1.1, "text": 1.1, "early": 1.4, "half": 0.3, "across": 0.2, "late": 0.2, "grad": 1.6,
@@ -323,7 +323,7 @@
     part_y[...] = total.astype(part_y.dtype)
 
 
-def late_kernel(late, relayed, out):
+def late_kernel(late, relayed, before, out):
     out[...] = (late[...] + relayed[...].astype(jnp.float32)).astype(out.dtype)
 
 
@@ -340,7 +340,7 @@
     return (lane - lax.axis_index("dp") // 2 + 8) % 8, lane < 8
 
 
-def total_kernel(mine, other, held):
+def total_kernel(mine, other, before, held):
     sums = mine[0:1, :] + other[0:1, :]
     line = lax.broadcasted_iota(jnp.int32, held.shape, 0)
     value = jnp.where(line == 0, sums[:, 0:1], jnp.where(line == 1, sums[:, 1:2], 0.0))
@@ -427,18 +427,19 @@
     txt_back, txt_next, token = call(
         text_kernel, "text", [wide, wide, few], w01, w23, near, far, sums
     )
-    (sums,) = call(side_kernel, "side", [few], sums, swapped(sums, 1, "dp"), token, token)
-    sums_got = moved(sums, by_sides)
     img_back, first, late = call(
         image_kernel, "image", [wide, block, wide], w01, w23, txts, sums
     )
+    (sums,) = call(side_kernel, "side", [few], sums, swapped(sums, 1, "dp"), token, late)
+    sums_got = moved(sums, by_sides)
     part_y, first = call(
         across_kernel, "across", [block] * 2, txt_next, core_part, first, sums
     )
-    (late,) = call(late_kernel, "late", [block], late, relayed)
-    (sums,) = call(side_kernel, "side", [few], sums, sums_got, part_y, late)
-    part_y, first, late = swapped(part_y, Y), moved(first, relay), moved(late, other_way)
-    (held,) = call(total_kernel, "total", [few], sums, swapped(sums, CORE))
+    (sums,) = call(side_kernel, "sides", [few], sums, sums_got, part_y, relayed)
+    part_y, first = swapped(part_y, Y), moved(first, relay)
+    (late,) = call(late_kernel, "late", [block], late, relayed, sums)
+    (held,) = call(total_kernel, "total", [few], sums, swapped(sums, CORE), late)
+    late = moved(late, other_way)
     (held,) = call(add_kernel, "add", [few], held, moved(held, by_planes))
     (held,) = call(planes_kernel, "planes", [few], held, swapped(held, CORE))
     image_grad, text_grad, token = call(

time: 67.3 us -> 66.4 us (0.987)
  waiting for transfers between devices: 14.7 us -> 12.1 us
  starting transfers between devices: 35.8 us -> 37.5 us
    ppermute x17, starting transfers between devices: 22.2 us -> 24.1 us  [swapped(): lax.ppermute(value, axis, [(i, i ^ bits) for i in range(lax.axis_size(axi...]
    ppermute x7, waiting for transfers between devices: 5.42 us -> 4.09 us  [moved(): return lax.ppermute(value, ('dp', 'blk'), pairs)]
    ppermute x17, waiting for transfers between devices: 9.31 us -> 7.99 us  [swapped(): lax.ppermute(value, axis, [(i, i ^ bits) for i in range(lax.axis_size(axi...]
  transfers between devices with their start and end apart: 24 -> 24, of which waited for: 11 -> 9; matrix products, arithmetic and copies ran while one was open for 0% -> 0% of each run, Pallas kernels for 16% -> 17%
where the time goes in v5:
time: 66.4 us; the launch traced here: 66.3 us
  starting transfers between devices  37.5 us (56%)
  Pallas kernels  13 us (20%)
  waiting for transfers between devices  12.1 us (18%)
  local copies, waits for them, and re-layouts  2 us (3%)
  between operations  1.65 us (2%)
    ppermute x17, starting transfers between devices, swapped(): lax.ppermute(value, axis, [(i, i ^ bits) for i in range(lax.axis_size(axi...  24.1 us
    ppermute x7, starting transfers between devices, moved(): return lax.ppermute(value, ('dp', 'blk'), pairs)  13.4 us
    pallas_call x22, Pallas kernels, call(): pl.pallas_call(kernel, out_shape=[jax.ShapeDtypeStruct(s, d) for s, d in...  12.4 us
    ppermute x17, waiting for transfers between devices, swapped(): lax.ppermute(value, axis, [(i, i ^ bits) for i in range(lax.axis_size(axi...  7.99 us
    ppermute x7, waiting for transfers between devices, moved(): return lax.ppermute(value, ('dp', 'blk'), pairs)  4.09 us
    unnamed x10, local copies, waits for them, and re-layouts  2 us
  transfers between devices with their start and end apart: 24, of which 9 were waited for; matrix products, arithmetic and copies ran while one was open for 0% of the time, Pallas kernels for 17%

profile of v5, /device:TPU:1, one launch (start us, length us, event | category | flops | bytes accessed | tf_op | source)
XLA Modules:
  0.0 66.3 jit_solution(7146933603104129576)
XLA Ops:
  0.6 3.4 %collective-permute-start.1 = (bf16[256,768]{1,0:T(8,128)(2,1)}, bf16[256,768]{1,0:T(8,128)(2,1)S(1)}, u32[]{:S(2)}, u32[]{:S(2)}) collective-permute-start(bf16[256,768]{1,0:T(8,128)(2,1)} %image.5), channel_id=1, source_target_pairs={{0,12},{1,13},{2,14},{3,15},{4,8},{5,9},{6,10},{7,11},{8,4},{9,5},... | collective-permute-start | bytes 1179656 | tf_op jit(solution)/shard_map/ppermute | solution.py:29
  4.0 0.0 collective-permute-start
  4.0 2.9 %collective-permute-start.3 = (bf16[256,768]{1,0:T(8,128)(2,1)}, bf16[256,768]{1,0:T(8,128)(2,1)S(1)}, u32[]{:S(2)}, u32[]{:S(2)}) collective-permute-start(bf16[256,768]{1,0:T(8,128)(2,1)} %text.5), channel_id=1, source_target_pairs={{0,2},{1,3},{2,0},{3,1},{4,6},{5,7},{6,4},{7,5},{8,10},{9,11},{10,... | collective-permute-start | bytes 1179656 | tf_op jit(solution)/shard_map/ppermute | solution.py:29
  6.9 1.5 %collective-permute-start.5 = (bf16[256,768]{1,0:T(8,128)(2,1)}, bf16[256,768]{1,0:T(8,128)(2,1)S(1)}, u32[]{:S(2)}, u32[]{:S(2)}) collective-permute-start(bf16[256,768]{1,0:T(8,128)(2,1)} %text.5), channel_id=1, source_target_pairs={{0,1},{1,0},{2,3},{3,2},{4,5},{5,4},{6,7},{7,6},{8,9},{9,8},{10,11... | collective-permute-start | bytes 1179656 | tf_op jit(solution)/shard_map/ppermute | solution.py:29
  9.1 0.0 copy-start
  9.1 1.0 %copy-done = bf16[256,768]{1,0:T(8,128)(2,1)S(1)} copy-done((bf16[256,768]{1,0:T(8,128)(2,1)S(1)}, bf16[256,768]{1,0:T(8,128)(2,1)}, u32[]{:S(2)}) %copy-start) | copy-done | bytes 393240
  10.1 1.0 %copy-done.2 = bf16[256,768]{1,0:T(8,128)(2,1)S(1)} copy-done((bf16[256,768]{1,0:T(8,128)(2,1)S(1)}, bf16[256,768]{1,0:T(8,128)(2,1)}, u32[]{:S(2)}) %copy-start.2) | copy-done | bytes 393240
  11.0 0.2 own.1
  11.3 0.8 %collective-permute-done.1.i3 = bf16[256,768]{1,0:T(8,128)(2,1)S(1)} collective-permute-done((bf16[256,768]{1,0:T(8,128)(2,1)}, bf16[256,768]{1,0:T(8,128)(2,1)S(1)}, u32[]{:S(2)}, u32[]{:S(2)}) %collective-permute-start.1) | collective-permute-done | bytes 393248 | tf_op jit(solution)/shard_map/ppermute | solution.py:29
  12.1 1.8 %collective-permute-done.i1 = bf16[256,768]{1,0:T(8,128)(2,1)S(1)} collective-permute-done((bf16[256,768]{1,0:T(8,128)(2,1)}, bf16[256,768]{1,0:T(8,128)(2,1)S(1)}, u32[]{:S(2)}, u32[]{:S(2)}) %collective-permute-start) | collective-permute-done | bytes 393248 | tf_op jit(solution)/shard_map/ppermute | solution.py:29
  13.9 1.6 %collective-permute-start.2 = (bf16[256,768]{1,0:T(8,128)(2,1)S(1)}, bf16[256,768]{1,0:T(8,128)(2,1)S(1)}, u32[]{:S(2)}, u32[]{:S(2)}) collective-permute-start(bf16[256,768]{1,0:T(8,128)(2,1)S(1)} %pick.1), channel_id=1, source_target_pairs={{0,4},{1,13},{2,6},{3,15},{4,0},{5,9},{6,2},{7,11},{8,12},{9,5},{1... | collective-permute-start | bytes 1179656 | tf_op jit(solution)/shard_map/ppermute | solution.py:36
  15.6 0.0 collective-permute-done.3.t2
  15.6 1.7 %collective-permute-start.4 = (bf16[256,768]{1,0:T(8,128)(2,1)S(1)}, bf16[256,768]{1,0:T(8,128)(2,1)S(1)}, u32[]{:S(2)}, u32[]{:S(2)}) collective-permute-start(bf16[256,768]{1,0:T(8,128)(2,1)S(1)} %collective-permute-done.3.t2), channel_id=1, source_target_pairs={{0,1},{1,0},{2,3},{3,2},{4,5},{5,4},{6,7},{7,6},{8,9},{9,8},{10,11... | collective-permute-start | bytes 1179656 | tf_op jit(solution)/shard_map/ppermute | solution.py:29
  17.3 0.0 collective-permute-done.5.t1
  17.3 2.5 %first.1 = (bf16[768,768]{1,0:T(8,128)(2,1)S(1)}, bf16[768,768]{1,0:T(8,128)(2,1)S(1)}, f32[768,768]{1,0:T(8,128)S(1)}, f32[4,1024]{1,0:T(4,128)S(1)}, f32[4,1024]{1,0:T(4,128)S(1)}) custom-call(f32[1]{0:T(128)S(6)} %copy.8.scale, bf16[256,768]{1,0:T(8,128)(2,1)S(1)} %get-tuple-element.42.before.i0, bf16[256,768]{1,0:T(8,128)(2,1)S(1)} %get-tuple-element.43.t0, ...), custom_call_target="tpu_custom_call" | custom-call | flops 13200000000 | bytes 7111684 | tf_op jit(solution)/shard_map/first/pallas_call | solution.py:63
  19.8 0.0 collective-permute-done.4.t3
  19.8 1.1 %second.1 = (bf16[1024,768]{1,0:T(8,128)(2,1)S(1)}, f32[768,256]{1,0:T(8,128)S(1)}, f32[4,1024]{1,0:T(4,128)S(1)}, f32[4,1024]{1,0:T(4,128)S(1)}) custom-call(f32[1]{0:T(128)S(6)} %copy.8.scale, bf16[256,768]{1,0:T(8,128)(2,1)S(1)} %collective-permute-done.4.t3, bf16[768,768]{1,0:T(8,128)(2,1)S(1)} %get-tuple-element.44.near, ...), custom_call_target="tpu_custom_call" | custom-call | flops 8800000000 | bytes 5177348 | tf_op jit(solution)/shard_map/second/pallas_call | solution.py:63
  20.9 0.9 %collective-permute-done.2.i2 = bf16[256,768]{1,0:T(8,128)(2,1)S(1)} collective-permute-done((bf16[256,768]{1,0:T(8,128)(2,1)S(1)}, bf16[256,768]{1,0:T(8,128)(2,1)S(1)}, u32[]{:S(2)}, u32[]{:S(2)}) %collective-permute-start.2) | collective-permute-done | bytes 393248 | tf_op jit(solution)/shard_map/ppermute | solution.py:36
  21.9 1.2 %third.1 = (bf16[256,768]{1,0:T(8,128)(2,1)S(1)}, f32[256,1024]{1,0:T(8,128)S(1)}, f32[4,1024]{1,0:T(4,128)S(1)}, f32[4,1024]{1,0:T(4,128)S(1)}) custom-call(f32[1]{0:T(128)S(6)} %copy.8.scale, bf16[256,768]{1,0:T(8,128)(2,1)S(1)} %collective-permute-done.2.i2, bf16[1024,768]{1,0:T(8,128)(2,1)S(1)} %get-tuple-element.48.txts, ...), custom_call_target="tpu_custom_call" | custom-call | flops 1264999936 | bytes 3473412 | tf_op jit(solution)/shard_map/third/pallas_call | solution.py:63
  23.0 1.9 %collective-permute-start.8 = (f32[4,1024]{1,0:T(4,128)S(1)}, f32[4,1024]{1,0:T(4,128)S(1)}, u32[]{:S(2)}, u32[]{:S(2)}) collective-permute-start(f32[4,1024]{1,0:T(4,128)S(1)} %get-tuple-element.52.mine), channel_id=1, source_target_pairs={{0,1},{1,0},{2,3},{3,2},{4,5},{5,4},{6,7},{7,6},{8,9},{9,8},{10,11... | collective-permute-start | bytes 49160 | tf_op jit(solution)/shard_map/ppermute | solution.py:29
  24.9 0.0 collective-permute-start.6
  25.0 0.8 %collective-permute-done.8.other = f32[4,1024]{1,0:T(4,128)S(1)} collective-permute-done((f32[4,1024]{1,0:T(4,128)S(1)}, f32[4,1024]{1,0:T(4,128)S(1)}, u32[]{:S(2)}, u32[]{:S(2)}) %collective-permute-start.8) | collective-permute-done | bytes 16416 | tf_op jit(solution)/shard_map/ppermute | solution.py:29
  25.8 3.0 %collective-permute-start.9 = (f32[8,1024]{1,0:T(8,128)S(1)}, f32[8,1024]{1,0:T(8,128)S(1)}, u32[]{:S(2)}, u32[]{:S(2)}) collective-permute-start(f32[8,1024]{1,0:T(8,128)S(1)} %join.3.col), channel_id=1, source_target_pairs={{0,2},{1,3},{2,0},{3,1},{4,6},{5,7},{6,4},{7,5},{8,10},{9,11},{10,... | collective-permute-start | bytes 98312 | tf_op jit(solution)/shard_map/ppermute | solution.py:29
  28.8 1.3 %collective-permute-start.7 = (f32[4,1024]{1,0:T(4,128)S(1)}, f32[4,1024]{1,0:T(4,128)S(1)}, u32[]{:S(2)}, u32[]{:S(2)}) collective-permute-start(f32[4,1024]{1,0:T(4,128)S(1)} %join.2.row), channel_id=1, source_target_pairs={{0,12},{1,13},{2,14},{3,15},{4,8},{5,9},{6,10},{7,11},{8,4},{9,5},... | collective-permute-start | bytes 49160 | tf_op jit(solution)/shard_map/ppermute | solution.py:29
  30.1 2.6 %collective-permute-done.7.row3 = f32[4,1024]{1,0:T(4,128)S(1)} collective-permute-done((f32[4,1024]{1,0:T(4,128)S(1)}, f32[4,1024]{1,0:T(4,128)S(1)}, u32[]{:S(2)}, u32[]{:S(2)}) %collective-permute-start.7) | collective-permute-done | bytes 16416 | tf_op jit(solution)/shard_map/ppermute | solution.py:29
  32.7 0.0 collective-permute-done.9.col2
  32.7 0.1 lse.1
  32.9 1.9 %collective-permute-start.10 = (f32[8,128]{1,0:T(8,128)S(1)}, f32[8,128]{1,0:T(8,128)S(1)}, u32[]{:S(2)}, u32[]{:S(2)}) collective-permute-start(f32[8,128]{1,0:T(8,128)S(1)} %get-tuple-element.53.row), channel_id=1, source_target_pairs={{0,1},{1,0},{2,3},{3,2},{4,5},{5,4},{6,7},{7,6},{8,9},{9,8},{10,11... | collective-permute-start | bytes 12296 | tf_op jit(solution)/shard_map/ppermute | solution.py:29
  34.7 0.0 collective-permute-start.11
  34.7 1.3 %weight.1 = (bf16[512,1024]{1,0:T(8,128)(2,1)S(1)}, bf16[512,1024]{1,0:T(8,128)(2,1)S(1)}) custom-call(f32[768,768]{1,0:T(8,128)S(1)} %get-tuple-element.55.first, f32[768,256]{1,0:T(8,128)S(1)} %get-tuple-element.56.second, f32[256,1024]{1,0:T(8,128)S(1)} %get-tuple-element.57.third, f32[2,1024]{1,0:T(2,128)S(1)} %get-tuple-element.58.lse, s32[1,256]{1,0:T(1,128)S(1)} %bitcast.2), custom_call_target="tpu_custom_call" | custom-call | flops 1430000000 | bytes 6300672 | tf_op jit(solution)/shard_map/weight/pallas_call | solution.py:63
  36.0 1.4 %early.1 = (bf16[512,768]{1,0:T(8,128)(2,1)S(1)}, bf16[256,768]{1,0:T(8,128)(2,1)S(1)}) custom-call(bf16[512,1024]{1,0:T(8,128)(2,1)S(1)} %get-tuple-element.59.w01, bf16[512,1024]{1,0:T(8,128)(2,1)S(1)} %get-tuple-element.60.w23, bf16[768,768]{1,0:T(8,128)(2,1)S(1)} %get-tuple-element.44.near, bf16[256,768]{1,0:T(8,128)(2,1)S(1)} %get-tuple-element.61.far, ...), custom_call_target="tpu_custom_call" | custom-call | flops 1540000000 | bytes 6422528 | tf_op jit(solution)/shard_map/early/pallas_call | solution.py:63
  37.4 0.0 collective-permute-done.11.col1
  37.4 0.1 half.1
  37.5 1.2 %collective-permute-start.14 = (bf16[512,768]{1,0:T(8,128)(2,1)S(1)}, bf16[512,768]{1,0:T(8,128)(2,1)S(1)}, u32[]{:S(2)}, u32[]{:S(2)}) collective-permute-start(bf16[512,768]{1,0:T(8,128)(2,1)S(1)} %get-tuple-element.68), channel_id=1, source_target_pairs={{0,1},{1,0},{2,3},{3,2},{4,5},{5,4},{6,7},{7,6},{8,9},{9,8},{10,11... | collective-permute-start | bytes 2359304 | tf_op jit(solution)/shard_map/ppermute | solution.py:29
  38.8 1.2 %collective-permute-start.15 = (bf16[256,768]{1,0:T(8,128)(2,1)S(1)}, bf16[256,768]{1,0:T(8,128)(2,1)S(1)}, u32[]{:S(2)}, u32[]{:S(2)}) collective-permute-start(bf16[256,768]{1,0:T(8,128)(2,1)S(1)} %get-tuple-element.71), channel_id=1, source_target_pairs={{0,4},{1,13},{2,6},{3,15},{4,0},{5,9},{6,2},{7,11},{8,12},{9,5},{1... | collective-permute-start | bytes 1179656 | tf_op jit(solution)/shard_map/ppermute | solution.py:36
  40.0 0.6 collective-permute-start.12
  40.6 1.0 %text.4 = (f32[256,768]{1,0:T(8,128)S(1)}, f32[256,768]{1,0:T(8,128)S(1)}, f32[8,128]{1,0:T(8,128)S(1)}) custom-call(bf16[512,1024]{1,0:T(8,128)(2,1)S(1)} %get-tuple-element.59.w01, bf16[512,1024]{1,0:T(8,128)(2,1)S(1)} %get-tuple-element.60.w23, bf16[768,768]{1,0:T(8,128)(2,1)S(1)} %get-tuple-element.44.near, bf16[256,768]{1,0:T(8,128)(2,1)S(1)} %get-tuple-element.61.far, ...), custom_call_target="tpu_custom_call" | custom-call | flops 1210000000 | bytes 5251072 | tf_op jit(solution)/shard_map/text/pallas_call | solution.py:63
  41.7 1.4 %image.4 = (f32[256,768]{1,0:T(8,128)S(1)}, bf16[256,768]{1,0:T(8,128)(2,1)S(1)}, f32[256,768]{1,0:T(8,128)S(1)}) custom-call(bf16[512,1024]{1,0:T(8,128)(2,1)S(1)} %get-tuple-element.59.w01, bf16[512,1024]{1,0:T(8,128)(2,1)S(1)} %get-tuple-element.60.w23, bf16[1024,768]{1,0:T(8,128)(2,1)S(1)} %get-tuple-element.48.txts, f32[8,128]{1,0:T(8,128)S(1)} %get-tuple-element.64.before.a), custom_call_target="tpu_custom_call" | custom-call | flops 1210000000 | bytes 5640192 | tf_op jit(solution)/shard_map/image/pallas_call | solution.py:63
  43.1 0.0 collective-permute-done.12.b
  43.1 1.5 %collective-permute-start.13 = (f32[8,128]{1,0:T(8,128)S(1)}, f32[8,128]{1,0:T(8,128)S(1)}, u32[]{:S(2)}, u32[]{:S(2)}) collective-permute-start(f32[8,128]{1,0:T(8,128)S(1)} %side.2.before.a), channel_id=1, source_target_pairs={{0,18},{1,13},{2,16},{3,15},{4,22},{5,9},{6,20},{7,11},{8,26},{9,5... | collective-permute-start | bytes 12296 | tf_op jit(solution)/shard_map/ppermute | solution.py:36
  44.7 0.1 across.1
  44.8 2.7 %collective-permute-start.22 = (bf16[256,768]{1,0:T(8,128)(2,1)S(1)}, bf16[256,768]{1,0:T(8,128)(2,1)S(1)}, u32[]{:S(2)}, u32[]{:S(2)}) collective-permute-start(bf16[256,768]{1,0:T(8,128)(2,1)S(1)} %get-tuple-element.70.before), channel_id=1, source_target_pairs={{0,2},{1,3},{2,0},{3,1},{4,6},{5,7},{6,4},{7,5},{8,10},{9,11},{10,... | collective-permute-start | bytes 1179656 | tf_op jit(solution)/shard_map/ppermute | solution.py:29
  47.5 0.0 collective-permute-done.13.b
  47.5 0.0 collective-permute-done.15.before_too.relayed
  47.5 1.0 %collective-permute-start.16 = (f32[8,128]{1,0:T(8,128)S(1)}, f32[8,128]{1,0:T(8,128)S(1)}, u32[]{:S(2)}, u32[]{:S(2)}) collective-permute-start(f32[8,128]{1,0:T(8,128)S(1)} %sides.1.before.mine), channel_id=1, source_target_pairs={{0,1},{1,0},{2,3},{3,2},{4,5},{5,4},{6,7},{7,6},{8,9},{9,8},{10,11... | collective-permute-start | bytes 12296 | tf_op jit(solution)/shard_map/ppermute | solution.py:29
  48.5 1.2 %collective-permute-start.20 = (bf16[256,768]{1,0:T(8,128)(2,1)S(1)}, bf16[256,768]{1,0:T(8,128)(2,1)S(1)}, u32[]{:S(2)}, u32[]{:S(2)}) collective-permute-start(bf16[256,768]{1,0:T(8,128)(2,1)S(1)} %get-tuple-element.74), channel_id=1, source_target_pairs={{0,4},{1,13},{2,6},{3,15},{4,0},{5,9},{6,2},{7,11},{8,12},{9,5},{1... | collective-permute-start | bytes 1179656 | tf_op jit(solution)/shard_map/ppermute | solution.py:36
  49.7 0.1 late.1.before
  49.8 0.0 copy-start.1
  49.8 0.0 copy-start.3
  49.8 0.1 collective-permute-start.21
  49.9 0.1 total.1.a
  50.0 5.7 %collective-permute-start.17 = (f32[8,128]{1,0:T(8,128)S(1)}, f32[8,128]{1,0:T(8,128)S(1)}, u32[]{:S(2)}, u32[]{:S(2)}) collective-permute-start(f32[8,128]{1,0:T(8,128)S(1)} %total.1.a), channel_id=1, source_target_pairs={{0,32},{1,225},{2,34},{3,227},{4,36},{5,229},{6,38},{7,231},{8,40}... | collective-permute-start | bytes 12296 | tf_op jit(solution)/shard_map/ppermute | solution.py:36
  55.7 1.3 %collective-permute-done.17.b = f32[8,128]{1,0:T(8,128)S(1)} collective-permute-done((f32[8,128]{1,0:T(8,128)S(1)}, f32[8,128]{1,0:T(8,128)S(1)}, u32[]{:S(2)}, u32[]{:S(2)}) %collective-permute-start.17) | collective-permute-done | bytes 4128 | tf_op jit(solution)/shard_map/ppermute | solution.py:36
  57.0 0.0 collective-permute-start.18
  57.0 1.2 %collective-permute-done.18.other = f32[8,128]{1,0:T(8,128)S(1)} collective-permute-done((f32[8,128]{1,0:T(8,128)S(1)}, f32[8,128]{1,0:T(8,128)S(1)}, u32[]{:S(2)}, u32[]{:S(2)}) %collective-permute-start.18) | collective-permute-done | bytes 4128 | tf_op jit(solution)/shard_map/ppermute | solution.py:29
  58.1 2.1 %collective-permute-start.19 = (f32[8,128]{1,0:T(8,128)S(1)}, f32[8,128]{1,0:T(8,128)S(1)}, u32[]{:S(2)}, u32[]{:S(2)}) collective-permute-start(f32[8,128]{1,0:T(8,128)S(1)} %planes.1.a), channel_id=1, source_target_pairs={{0,160},{1,97},{2,162},{3,99},{4,164},{5,101},{6,166},{7,103},{8,1... | collective-permute-start | bytes 12296 | tf_op jit(solution)/shard_map/ppermute | solution.py:36
  60.2 0.0 collective-permute-done.20.first
  60.2 0.0 collective-permute-done.21.late
  60.2 0.0 collective-permute-done.22.py
  60.2 1.6 %grad.1 = (bf16[256,768]{1,0:T(8,128)(2,1)}, bf16[256,768]{1,0:T(8,128)(2,1)}, f32[8,128]{1,0:T(8,128)S(1)}) custom-call(f32[1]{0:T(128)S(6)} %copy.8.scale, bf16[256,768]{1,0:T(8,128)(2,1)S(1)} %copy-done.1, bf16[256,768]{1,0:T(8,128)(2,1)S(1)} %copy-done.3, f32[256,768]{1,0:T(8,128)S(1)} %get-tuple-element.72.img_back, ...), custom_call_target="tpu_custom_call" | custom-call | flops 1760000000 | bytes 5115908 | tf_op jit(solution)/shard_map/grad/pallas_call | solution.py:63
  61.8 1.8 %collective-permute-done.19.b = f32[8,128]{1,0:T(8,128)S(1)} collective-permute-done((f32[8,128]{1,0:T(8,128)S(1)}, f32[8,128]{1,0:T(8,128)S(1)}, u32[]{:S(2)}, u32[]{:S(2)}) %collective-permute-start.19) | collective-permute-done | bytes 4128 | tf_op jit(solution)/shard_map/ppermute | solution.py:36
  63.7 0.9 %collective-permute-start.23 = (f32[8,128]{1,0:T(8,128)S(1)}, f32[8,128]{1,0:T(8,128)S(1)}, u32[]{:S(2)}, u32[]{:S(2)}) collective-permute-start(f32[8,128]{1,0:T(8,128)S(1)} %side.3.held), channel_id=1, source_target_pairs={{0,1},{1,0},{2,3},{3,2},{4,5},{5,4},{6,7},{7,6},{8,9},{9,8},{10,11... | collective-permute-start | bytes 12296 | tf_op jit(solution)/shard_map/ppermute | solution.py:29
  64.6 0.8 %collective-permute-done.23.other = f32[8,128]{1,0:T(8,128)S(1)} collective-permute-done((f32[8,128]{1,0:T(8,128)S(1)}, f32[8,128]{1,0:T(8,128)S(1)}, u32[]{:S(2)}, u32[]{:S(2)}) %collective-permute-start.23) | collective-permute-done | bytes 4128 | tf_op jit(solution)/shard_map/ppermute | solution.py:29
  65.4 0.7 scalar.1
  (17 shorter events, 0.1 us)
Async XLA Ops:
  0.6 11.5 %collective-permute-start.1 = (bf16[256,768]{1,0:T(8,128)(2,1)}, bf16[256,768]{1,0:T(8,128)(2,1)S(1)}, u32[]{:S(2)}, u32[]{:S(2)}) collective-permute-start(bf16[256,768]{1,0:T(8,128)(2,1)} %image.5), channel_id=1, source_target_pairs={{0,12},{1,13},{2,14},{3,15},{4,8},{5,9},{6,10},{7,11},{8,4},{9,5},... | collective-permute-start | bytes 1179656 | tf_op jit(solution)/shard_map/ppermute | solution.py:29
  4.0 9.9 %collective-permute-start = (bf16[256,768]{1,0:T(8,128)(2,1)}, bf16[256,768]{1,0:T(8,128)(2,1)S(1)}, u32[]{:S(2)}, u32[]{:S(2)}) collective-permute-start(bf16[256,768]{1,0:T(8,128)(2,1)} %image.5), channel_id=1, source_target_pairs={{0,4},{1,5},{2,6},{3,7},{4,0},{5,1},{6,2},{7,3},{8,12},{9,13},{10,... | collective-permute-start | bytes 1179656 | tf_op jit(solution)/shard_map/ppermute | solution.py:29
  4.0 11.5 %collective-permute-start.3 = (bf16[256,768]{1,0:T(8,128)(2,1)}, bf16[256,768]{1,0:T(8,128)(2,1)S(1)}, u32[]{:S(2)}, u32[]{:S(2)}) collective-permute-start(bf16[256,768]{1,0:T(8,128)(2,1)} %text.5), channel_id=1, source_target_pairs={{0,2},{1,3},{2,0},{3,1},{4,6},{5,7},{6,4},{7,5},{8,10},{9,11},{10,... | collective-permute-start | bytes 1179656 | tf_op jit(solution)/shard_map/ppermute | solution.py:29
  6.9 10.3 %collective-permute-start.5 = (bf16[256,768]{1,0:T(8,128)(2,1)}, bf16[256,768]{1,0:T(8,128)(2,1)S(1)}, u32[]{:S(2)}, u32[]{:S(2)}) collective-permute-start(bf16[256,768]{1,0:T(8,128)(2,1)} %text.5), channel_id=1, source_target_pairs={{0,1},{1,0},{2,3},{3,2},{4,5},{5,4},{6,7},{7,6},{8,9},{9,8},{10,11... | collective-permute-start | bytes 1179656 | tf_op jit(solution)/shard_map/ppermute | solution.py:29
  9.1 1.0 %copy-start = (bf16[256,768]{1,0:T(8,128)(2,1)S(1)}, bf16[256,768]{1,0:T(8,128)(2,1)}, u32[]{:S(2)}) copy-start(bf16[256,768]{1,0:T(8,128)(2,1)} %image.5) | copy-start | bytes 1179652
  10.1 1.0 %copy-start.2 = (bf16[256,768]{1,0:T(8,128)(2,1)S(1)}, bf16[256,768]{1,0:T(8,128)(2,1)}, u32[]{:S(2)}) copy-start(bf16[256,768]{1,0:T(8,128)(2,1)} %text.5) | copy-start | bytes 1179652
  13.9 3.4 %copy-start.4 = (s32[256]{0:T(256)S(1)}, s32[256]{0:T(256)}, u32[]{:S(2)}) copy-start(s32[256]{0:T(256)} %param.6) | copy-start | bytes 3076
  13.9 7.9 %collective-permute-start.2 = (bf16[256,768]{1,0:T(8,128)(2,1)S(1)}, bf16[256,768]{1,0:T(8,128)(2,1)S(1)}, u32[]{:S(2)}, u32[]{:S(2)}) collective-permute-start(bf16[256,768]{1,0:T(8,128)(2,1)S(1)} %pick.1), channel_id=1, source_target_pairs={{0,4},{1,13},{2,6},{3,15},{4,0},{5,9},{6,2},{7,11},{8,12},{9,5},{1... | collective-permute-start | bytes 1179656 | tf_op jit(solution)/shard_map/ppermute | solution.py:36
  15.6 4.3 %collective-permute-start.4 = (bf16[256,768]{1,0:T(8,128)(2,1)S(1)}, bf16[256,768]{1,0:T(8,128)(2,1)S(1)}, u32[]{:S(2)}, u32[]{:S(2)}) collective-permute-start(bf16[256,768]{1,0:T(8,128)(2,1)S(1)} %collective-permute-done.3.t2), channel_id=1, source_target_pairs={{0,1},{1,0},{2,3},{3,2},{4,5},{5,4},{6,7},{7,6},{8,9},{9,8},{10,11... | collective-permute-start | bytes 1179656 | tf_op jit(solution)/shard_map/ppermute | solution.py:29
  23.0 2.7 %collective-permute-start.8 = (f32[4,1024]{1,0:T(4,128)S(1)}, f32[4,1024]{1,0:T(4,128)S(1)}, u32[]{:S(2)}, u32[]{:S(2)}) collective-permute-start(f32[4,1024]{1,0:T(4,128)S(1)} %get-tuple-element.52.mine), channel_id=1, source_target_pairs={{0,1},{1,0},{2,3},{3,2},{4,5},{5,4},{6,7},{7,6},{8,9},{9,8},{10,11... | collective-permute-start | bytes 49160 | tf_op jit(solution)/shard_map/ppermute | solution.py:29
  24.9 3.9 %collective-permute-start.6 = (f32[4,1024]{1,0:T(4,128)S(1)}, f32[4,1024]{1,0:T(4,128)S(1)}, u32[]{:S(2)}, u32[]{:S(2)}) collective-permute-start(f32[4,1024]{1,0:T(4,128)S(1)} %get-tuple-element.51.mine), channel_id=1, source_target_pairs={{0,4},{1,5},{2,6},{3,7},{4,0},{5,1},{6,2},{7,3},{8,12},{9,13},{10,... | collective-permute-start | bytes 49160 | tf_op jit(solution)/shard_map/ppermute | solution.py:29
  25.8 6.9 %collective-permute-start.9 = (f32[8,1024]{1,0:T(8,128)S(1)}, f32[8,1024]{1,0:T(8,128)S(1)}, u32[]{:S(2)}, u32[]{:S(2)}) collective-permute-start(f32[8,1024]{1,0:T(8,128)S(1)} %join.3.col), channel_id=1, source_target_pairs={{0,2},{1,3},{2,0},{3,1},{4,6},{5,7},{6,4},{7,5},{8,10},{9,11},{10,... | collective-permute-start | bytes 98312 | tf_op jit(solution)/shard_map/ppermute | solution.py:29
  28.8 3.9 %collective-permute-start.7 = (f32[4,1024]{1,0:T(4,128)S(1)}, f32[4,1024]{1,0:T(4,128)S(1)}, u32[]{:S(2)}, u32[]{:S(2)}) collective-permute-start(f32[4,1024]{1,0:T(4,128)S(1)} %join.2.row), channel_id=1, source_target_pairs={{0,12},{1,13},{2,14},{3,15},{4,8},{5,9},{6,10},{7,11},{8,4},{9,5},... | collective-permute-start | bytes 49160 | tf_op jit(solution)/shard_map/ppermute | solution.py:29
  32.9 4.6 %collective-permute-start.10 = (f32[8,128]{1,0:T(8,128)S(1)}, f32[8,128]{1,0:T(8,128)S(1)}, u32[]{:S(2)}, u32[]{:S(2)}) collective-permute-start(f32[8,128]{1,0:T(8,128)S(1)} %get-tuple-element.53.row), channel_id=1, source_target_pairs={{0,1},{1,0},{2,3},{3,2},{4,5},{5,4},{6,7},{7,6},{8,9},{9,8},{10,11... | collective-permute-start | bytes 12296 | tf_op jit(solution)/shard_map/ppermute | solution.py:29
  34.7 2.7 %collective-permute-start.11 = (f32[8,128]{1,0:T(8,128)S(1)}, f32[8,128]{1,0:T(8,128)S(1)}, u32[]{:S(2)}, u32[]{:S(2)}) collective-permute-start(f32[8,128]{1,0:T(8,128)S(1)} %get-tuple-element.54.col), channel_id=1, source_target_pairs={{0,4},{1,5},{2,6},{3,7},{4,0},{5,1},{6,2},{7,3},{8,12},{9,13},{10,... | collective-permute-start | bytes 12296 | tf_op jit(solution)/shard_map/ppermute | solution.py:29
  37.5 7.1 %collective-permute-start.14 = (bf16[512,768]{1,0:T(8,128)(2,1)S(1)}, bf16[512,768]{1,0:T(8,128)(2,1)S(1)}, u32[]{:S(2)}, u32[]{:S(2)}) collective-permute-start(bf16[512,768]{1,0:T(8,128)(2,1)S(1)} %get-tuple-element.68), channel_id=1, source_target_pairs={{0,1},{1,0},{2,3},{3,2},{4,5},{5,4},{6,7},{7,6},{8,9},{9,8},{10,11... | collective-permute-start | bytes 2359304 | tf_op jit(solution)/shard_map/ppermute | solution.py:29
  38.8 8.7 %collective-permute-start.15 = (bf16[256,768]{1,0:T(8,128)(2,1)S(1)}, bf16[256,768]{1,0:T(8,128)(2,1)S(1)}, u32[]{:S(2)}, u32[]{:S(2)}) collective-permute-start(bf16[256,768]{1,0:T(8,128)(2,1)S(1)} %get-tuple-element.71), channel_id=1, source_target_pairs={{0,4},{1,13},{2,6},{3,15},{4,0},{5,9},{6,2},{7,11},{8,12},{9,5},{1... | collective-permute-start | bytes 1179656 | tf_op jit(solution)/shard_map/ppermute | solution.py:36
  40.0 3.1 %collective-permute-start.12 = (f32[8,128]{1,0:T(8,128)S(1)}, f32[8,128]{1,0:T(8,128)S(1)}, u32[]{:S(2)}, u32[]{:S(2)}) collective-permute-start(f32[8,128]{1,0:T(8,128)S(1)} %get-tuple-element.64.before.a), channel_id=1, source_target_pairs={{0,16},{16,0},{32,48},{48,32},{64,80},{80,64},{96,112},{112,96},{1... | collective-permute-start | bytes 12296 | tf_op jit(solution)/shard_map/ppermute | solution.py:29
  43.1 4.4 %collective-permute-start.13 = (f32[8,128]{1,0:T(8,128)S(1)}, f32[8,128]{1,0:T(8,128)S(1)}, u32[]{:S(2)}, u32[]{:S(2)}) collective-permute-start(f32[8,128]{1,0:T(8,128)S(1)} %side.2.before.a), channel_id=1, source_target_pairs={{0,18},{1,13},{2,16},{3,15},{4,22},{5,9},{6,20},{7,11},{8,26},{9,5... | collective-permute-start | bytes 12296 | tf_op jit(solution)/shard_map/ppermute | solution.py:36
  44.8 15.4 %collective-permute-start.22 = (bf16[256,768]{1,0:T(8,128)(2,1)S(1)}, bf16[256,768]{1,0:T(8,128)(2,1)S(1)}, u32[]{:S(2)}, u32[]{:S(2)}) collective-permute-start(bf16[256,768]{1,0:T(8,128)(2,1)S(1)} %get-tuple-element.70.before), channel_id=1, source_target_pairs={{0,2},{1,3},{2,0},{3,1},{4,6},{5,7},{6,4},{7,5},{8,10},{9,11},{10,... | collective-permute-start | bytes 1179656 | tf_op jit(solution)/shard_map/ppermute | solution.py:29
  47.5 2.4 %collective-permute-start.16 = (f32[8,128]{1,0:T(8,128)S(1)}, f32[8,128]{1,0:T(8,128)S(1)}, u32[]{:S(2)}, u32[]{:S(2)}) collective-permute-start(f32[8,128]{1,0:T(8,128)S(1)} %sides.1.before.mine), channel_id=1, source_target_pairs={{0,1},{1,0},{2,3},{3,2},{4,5},{5,4},{6,7},{7,6},{8,9},{9,8},{10,11... | collective-permute-start | bytes 12296 | tf_op jit(solution)/shard_map/ppermute | solution.py:29
  48.5 11.7 %collective-permute-start.20 = (bf16[256,768]{1,0:T(8,128)(2,1)S(1)}, bf16[256,768]{1,0:T(8,128)(2,1)S(1)}, u32[]{:S(2)}, u32[]{:S(2)}) collective-permute-start(bf16[256,768]{1,0:T(8,128)(2,1)S(1)} %get-tuple-element.74), channel_id=1, source_target_pairs={{0,4},{1,13},{2,6},{3,15},{4,0},{5,9},{6,2},{7,11},{8,12},{9,5},{1... | collective-permute-start | bytes 1179656 | tf_op jit(solution)/shard_map/ppermute | solution.py:36
  49.8 10.5 %copy-start.1 = (bf16[256,768]{1,0:T(8,128)(2,1)S(1)}, bf16[256,768]{1,0:T(8,128)(2,1)}, u32[]{:S(2)}) copy-start(bf16[256,768]{1,0:T(8,128)(2,1)} %image.5) | copy-start | bytes 1179652
  49.8 10.5 %copy-start.3 = (bf16[256,768]{1,0:T(8,128)(2,1)S(1)}, bf16[256,768]{1,0:T(8,128)(2,1)}, u32[]{:S(2)}) copy-start(bf16[256,768]{1,0:T(8,128)(2,1)} %text.5) | copy-start | bytes 1179652
  49.8 10.4 %collective-permute-start.21 = (bf16[256,768]{1,0:T(8,128)(2,1)S(1)}, bf16[256,768]{1,0:T(8,128)(2,1)S(1)}, u32[]{:S(2)}, u32[]{:S(2)}) collective-permute-start(bf16[256,768]{1,0:T(8,128)(2,1)S(1)} %late.1.before), channel_id=1, source_target_pairs={{0,12},{1,5},{2,14},{3,7},{4,8},{5,1},{6,10},{7,3},{8,4},{9,13},{1... | collective-permute-start | bytes 1179656 | tf_op jit(solution)/shard_map/ppermute | solution.py:36
  50.0 6.9 %collective-permute-start.17 = (f32[8,128]{1,0:T(8,128)S(1)}, f32[8,128]{1,0:T(8,128)S(1)}, u32[]{:S(2)}, u32[]{:S(2)}) collective-permute-start(f32[8,128]{1,0:T(8,128)S(1)} %total.1.a), channel_id=1, source_target_pairs={{0,32},{1,225},{2,34},{3,227},{4,36},{5,229},{6,38},{7,231},{8,40}... | collective-permute-start | bytes 12296 | tf_op jit(solution)/shard_map/ppermute | solution.py:36
  57.0 1.2 %collective-permute-start.18 = (f32[8,128]{1,0:T(8,128)S(1)}, f32[8,128]{1,0:T(8,128)S(1)}, u32[]{:S(2)}, u32[]{:S(2)}) collective-permute-start(f32[8,128]{1,0:T(8,128)S(1)} %add.1.held), channel_id=1, source_target_pairs={{0,1},{1,0},{2,3},{3,2},{4,5},{5,4},{6,7},{7,6},{8,9},{9,8},{10,11... | collective-permute-start | bytes 12296 | tf_op jit(solution)/shard_map/ppermute | solution.py:29
  58.1 5.5 %collective-permute-start.19 = (f32[8,128]{1,0:T(8,128)S(1)}, f32[8,128]{1,0:T(8,128)S(1)}, u32[]{:S(2)}, u32[]{:S(2)}) collective-permute-start(f32[8,128]{1,0:T(8,128)S(1)} %planes.1.a), channel_id=1, source_target_pairs={{0,160},{1,97},{2,162},{3,99},{4,164},{5,101},{6,166},{7,103},{8,1... | collective-permute-start | bytes 12296 | tf_op jit(solution)/shard_map/ppermute | solution.py:36
  63.7 1.7 %collective-permute-start.23 = (f32[8,128]{1,0:T(8,128)S(1)}, f32[8,128]{1,0:T(8,128)S(1)}, u32[]{:S(2)}, u32[]{:S(2)}) collective-permute-start(f32[8,128]{1,0:T(8,128)S(1)} %side.3.held), channel_id=1, source_target_pairs={{0,1},{1,0},{2,3},{3,2},{4,5},{5,4},{6,7},{7,6},{8,9},{9,8},{10,11... | collective-permute-start | bytes 12296 | tf_op jit(solution)/shard_map/ppermute | solution.py:29

commit v6 on v5

--- a/solution.py
+++ b/solution.py
@@ -19,7 +19,7 @@
     "sides": 10, "total": 10,
     "pick": 5.0,
     "own": 0.25, "first": 12, "second": 8, "third": 1.15, "lse": 0.15, "weight": 1.3,
-    "image": 1.1, "text": 1.1, "early": 1.4, "half": 0.3, "across": 0.2, "late": 0.2, "grad": 1.6,
+    "image": 1.1, "text": 1.1, "early": 1.4, "half": 0.3, "across": 0.2, "late": 0.2, "text_grad": 0.8, "image_grad": 0.8,
 }
 NEAR = (0, 1, 3)
 X1, X2, X3, Y, CORE = 4, 8, 12, 2, 1
@@ -226,8 +226,8 @@
     return value, mean, mine[2:3, :] + swap(2)
 
 
-def join_kernel(mine, other, out):
-    out[0:1, :], out[1:2, :], out[2:3, :] = joined(mine, other, 1)
+def join_kernel(bits, mine, other, out):
+    out[0:1, :], out[1:2, :], out[2:3, :] = joined(mine, other, bits)
     out[3:, :] = jnp.zeros((out.shape[0] - 3, out.shape[1]), jnp.float32)
 
 
@@ -237,9 +237,9 @@
     return (at[0] + at[1]) + (at[2] + at[3])
 
 
-def lse_kernel(row, row3, col, col2, lse, row_sums, col_sums):
+def lse_kernel(row, row1, col, col2, lse, row_sums, col_sums):
     lane = lax.broadcasted_iota(jnp.int32, row_sums.shape, 1)
-    sides = ((joined(row, row3, 3), row_sums), (joined(col, col2, 2), col_sums))
+    sides = ((joined(row, row1, 1), row_sums), (joined(col, col2, 2), col_sums))
     for at, ((value, mean, matched), out) in enumerate(sides):
         lse[at : at + 1, :] = value
         loss, slope = slot_sum(0.5 * value - matched), slot_sum(0.5 * mean - matched)
@@ -358,23 +358,21 @@
     out[...] = union(held, other, (0,))
 
 
-def scalar_kernel(total_rows, scale, held, other, loss, scale_grad):
+def scalar_kernel(total_rows, scale, held, other, before, loss, scale_grad):
     sums = jnp.sum(union(held, other, (0, 1, 4, 7)), axis=1, keepdims=True)
     loss[0] = sums[0, 0] / total_rows
     scale_grad[0] = sums[1, 0] / (total_rows * scale[0])
 
 
-def grad_kernel(scale, image, text, img_back, txt_back, core_part, first, late, py, image_grad, text_grad, token):
+def grad_kernel(scale, values, *refs):
+    parts, out, token = refs[:-2], refs[-2], refs[-1]
     token[...] = jnp.zeros(token.shape, jnp.float32)
-    for values, parts, out in (
-        (image, (img_back, first, late), image_grad), (text, (txt_back, core_part, py), text_grad),
-    ):
-        direction, inverse = unit_rows(values[...])
-        incoming = scale[0] * sum(
-            part[pl.ds(0, direction.shape[0]), :].astype(jnp.float32) for part in parts
-        )
-        along = jnp.sum(direction * incoming, axis=-1, keepdims=True)
-        out[...] = ((incoming - direction * along) * inverse).astype(out.dtype)
+    direction, inverse = unit_rows(values[...])
+    incoming = scale[0] * sum(
+        part[pl.ds(0, direction.shape[0]), :].astype(jnp.float32) for part in parts
+    )
+    along = jnp.sum(direction * incoming, axis=-1, keepdims=True)
+    out[...] = ((incoming - direction * along) * inverse).astype(out.dtype)
 
 
 def shards(image, text, positive, logit_scale):
@@ -404,12 +402,17 @@
         third_kernel, "third", [block, ((rows, group), f32), parts, parts],
         logit_scale, i2, txts, row_part, col_part, scalar=True,
     )
-    (col_part,) = call(join_kernel, "join", [((2 * SLOTS, group), f32)], col_part, swapped(col_part, CORE))
+    (col_part,) = call(
+        functools.partial(join_kernel, 1), "join", [((2 * SLOTS, group), f32)],
+        col_part, swapped(col_part, CORE),
+    )
     col_y = swapped(col_part, Y)
-    (row_part,) = call(join_kernel, "join", [parts], row_part, swapped(row_part, X1))
+    (row_part,) = call(
+        functools.partial(join_kernel, 3), "join", [parts], row_part, swapped(row_part, X3)
+    )
     lse, row_sums, col_sums = call(
         lse_kernel, "lse", [((2, group), f32), few, few],
-        row_part, swapped(row_part, X3), col_part, col_y,
+        row_part, swapped(row_part, X1), col_part, col_y,
     )
     row_core, col1 = swapped(row_sums, CORE), swapped(col_sums, X1)
     heavy = ((2 * rows, group), bf16)
@@ -442,20 +445,24 @@
     late = moved(late, other_way)
     (held,) = call(add_kernel, "add", [few], held, moved(held, by_planes))
     (held,) = call(planes_kernel, "planes", [few], held, swapped(held, CORE))
-    image_grad, text_grad, token = call(
-        grad_kernel, "grad", [block] * 2 + [few],
-        logit_scale, image, text, img_back, txt_back, core_part, first, late, part_y, scalar=True,
+    text_grad, text_token = call(
+        grad_kernel, "text_grad", [block, few],
+        logit_scale, text, txt_back, core_part, part_y, scalar=True,
+    )
+    image_grad, image_token = call(
+        grad_kernel, "image_grad", [block, few],
+        logit_scale, image, img_back, first, late, scalar=True,
     )
     (held,) = call(
-        side_kernel, "side", [few], held, moved(held, by_far_planes), token, token
+        side_kernel, "side", [few], held, moved(held, by_far_planes), text_token, text_token
     )
     total_rows = rows * lax.axis_size("blk") * lax.axis_size("dp")
     loss, scale_grad = pl.pallas_call(
         functools.partial(scalar_kernel, total_rows), name="scalar",
         out_shape=[jax.ShapeDtypeStruct((1,), f32)] * 2,
-        in_specs=[SMEM, VMEM, VMEM], out_specs=[SMEM] * 2,
+        in_specs=[SMEM, VMEM, VMEM, VMEM], out_specs=[SMEM] * 2,
         compiler_params=PARAMS,
-    )(logit_scale, held, swapped(held, CORE))
+    )(logit_scale, held, swapped(held, CORE), image_token)
     return (loss, scale_grad, image_grad, text_grad)
 
 

time: 66.4 us -> 66.3 us (level)
  waiting for transfers between devices: 12.1 us -> 10.9 us
  Pallas kernels: 13 us -> 13.8 us
    ppermute x17, waiting for transfers between devices: 7.99 us -> 6.38 us  [swapped(): lax.ppermute(value, axis, [(i, i ^ bits) for i in range(lax.axis_size(axi...]
    pallas_call x22 -> x23, Pallas kernels: 12.4 us -> 13.1 us  [call(): pl.pallas_call(kernel, out_shape=[jax.ShapeDtypeStruct(s, d) for s, d in...]
  transfers between devices with their start and end apart: 24 -> 24, of which waited for: 9 -> 7; matrix products, arithmetic and copies ran while one was open for 0% -> 0% of each run, Pallas kernels for 17% -> 18%
where the time goes in v6:
time: 66.3 us; the launch traced here: 66.2 us
  starting transfers between devices  37.9 us (57%)
  Pallas kernels  13.8 us (21%)
  waiting for transfers between devices  10.9 us (16%)
  local copies, waits for them, and re-layouts  2 us (3%)
  between operations  1.63 us (2%)
    ppermute x17, starting transfers between devices, swapped(): lax.ppermute(value, axis, [(i, i ^ bits) for i in range(lax.axis_size(axi...  24.3 us
    ppermute x7, starting transfers between devices, moved(): return lax.ppermute(value, ('dp', 'blk'), pairs)  13.5 us
    pallas_call x23, Pallas kernels, call(): pl.pallas_call(kernel, out_shape=[jax.ShapeDtypeStruct(s, d) for s, d in...  13.1 us
    ppermute x17, waiting for transfers between devices, swapped(): lax.ppermute(value, axis, [(i, i ^ bits) for i in range(lax.axis_size(axi...  6.38 us
    ppermute x7, waiting for transfers between devices, moved(): return lax.ppermute(value, ('dp', 'blk'), pairs)  4.54 us
    unnamed x10, local copies, waits for them, and re-layouts  2 us
  transfers between devices with their start and end apart: 24, of which 7 were waited for; matrix products, arithmetic and copies ran while one was open for 0% of the time, Pallas kernels for 18%

profile of v6, /device:TPU:1, one launch (start us, length us, event | category | flops | bytes accessed | tf_op | source)
XLA Modules:
  0.0 66.2 jit_solution(3948801200712275407)
XLA Ops:
  0.6 3.4 %collective-permute-start.1 = (bf16[256,768]{1,0:T(8,128)(2,1)}, bf16[256,768]{1,0:T(8,128)(2,1)S(1)}, u32[]{:S(2)}, u32[]{:S(2)}) collective-permute-start(bf16[256,768]{1,0:T(8,128)(2,1)} %values.3), channel_id=1, source_target_pairs={{0,12},{1,13},{2,14},{3,15},{4,8},{5,9},{6,10},{7,11},{8,4},{9,5},... | collective-permute-start | bytes 1179656 | tf_op jit(solution)/shard_map/ppermute | solution.py:29
  4.0 2.9 %collective-permute-start.3 = (bf16[256,768]{1,0:T(8,128)(2,1)}, bf16[256,768]{1,0:T(8,128)(2,1)S(1)}, u32[]{:S(2)}, u32[]{:S(2)}) collective-permute-start(bf16[256,768]{1,0:T(8,128)(2,1)} %values.2), channel_id=1, source_target_pairs={{0,2},{1,3},{2,0},{3,1},{4,6},{5,7},{6,4},{7,5},{8,10},{9,11},{10,... | collective-permute-start | bytes 1179656 | tf_op jit(solution)/shard_map/ppermute | solution.py:29
  6.9 1.5 %collective-permute-start.5 = (bf16[256,768]{1,0:T(8,128)(2,1)}, bf16[256,768]{1,0:T(8,128)(2,1)S(1)}, u32[]{:S(2)}, u32[]{:S(2)}) collective-permute-start(bf16[256,768]{1,0:T(8,128)(2,1)} %values.2), channel_id=1, source_target_pairs={{0,1},{1,0},{2,3},{3,2},{4,5},{5,4},{6,7},{7,6},{8,9},{9,8},{10,11... | collective-permute-start | bytes 1179656 | tf_op jit(solution)/shard_map/ppermute | solution.py:29
  9.1 1.0 %copy-done = bf16[256,768]{1,0:T(8,128)(2,1)S(1)} copy-done((bf16[256,768]{1,0:T(8,128)(2,1)S(1)}, bf16[256,768]{1,0:T(8,128)(2,1)}, u32[]{:S(2)}) %copy-start) | copy-done | bytes 393240
  10.1 1.0 %copy-done.2 = bf16[256,768]{1,0:T(8,128)(2,1)S(1)} copy-done((bf16[256,768]{1,0:T(8,128)(2,1)S(1)}, bf16[256,768]{1,0:T(8,128)(2,1)}, u32[]{:S(2)}) %copy-start.2) | copy-done | bytes 393240
  11.0 0.2 own.1
  11.3 0.8 %collective-permute-done.1.i3 = bf16[256,768]{1,0:T(8,128)(2,1)S(1)} collective-permute-done((bf16[256,768]{1,0:T(8,128)(2,1)}, bf16[256,768]{1,0:T(8,128)(2,1)S(1)}, u32[]{:S(2)}, u32[]{:S(2)}) %collective-permute-start.1) | collective-permute-done | bytes 393248 | tf_op jit(solution)/shard_map/ppermute | solution.py:29
  12.1 1.8 %collective-permute-done.i1 = bf16[256,768]{1,0:T(8,128)(2,1)S(1)} collective-permute-done((bf16[256,768]{1,0:T(8,128)(2,1)}, bf16[256,768]{1,0:T(8,128)(2,1)S(1)}, u32[]{:S(2)}, u32[]{:S(2)}) %collective-permute-start) | collective-permute-done | bytes 393248 | tf_op jit(solution)/shard_map/ppermute | solution.py:29
  13.9 1.6 %collective-permute-start.2 = (bf16[256,768]{1,0:T(8,128)(2,1)S(1)}, bf16[256,768]{1,0:T(8,128)(2,1)S(1)}, u32[]{:S(2)}, u32[]{:S(2)}) collective-permute-start(bf16[256,768]{1,0:T(8,128)(2,1)S(1)} %pick.1), channel_id=1, source_target_pairs={{0,4},{1,13},{2,6},{3,15},{4,0},{5,9},{6,2},{7,11},{8,12},{9,5},{1... | collective-permute-start | bytes 1179656 | tf_op jit(solution)/shard_map/ppermute | solution.py:36
  15.6 0.0 collective-permute-done.3.t2
  15.6 1.7 %collective-permute-start.4 = (bf16[256,768]{1,0:T(8,128)(2,1)S(1)}, bf16[256,768]{1,0:T(8,128)(2,1)S(1)}, u32[]{:S(2)}, u32[]{:S(2)}) collective-permute-start(bf16[256,768]{1,0:T(8,128)(2,1)S(1)} %collective-permute-done.3.t2), channel_id=1, source_target_pairs={{0,1},{1,0},{2,3},{3,2},{4,5},{5,4},{6,7},{7,6},{8,9},{9,8},{10,11... | collective-permute-start | bytes 1179656 | tf_op jit(solution)/shard_map/ppermute | solution.py:29
  17.3 0.0 collective-permute-done.5.t1
  17.3 2.5 %first.1 = (bf16[768,768]{1,0:T(8,128)(2,1)S(1)}, bf16[768,768]{1,0:T(8,128)(2,1)S(1)}, f32[768,768]{1,0:T(8,128)S(1)}, f32[4,1024]{1,0:T(4,128)S(1)}, f32[4,1024]{1,0:T(4,128)S(1)}) custom-call(f32[1]{0:T(128)S(6)} %copy.8.scale, bf16[256,768]{1,0:T(8,128)(2,1)S(1)} %get-tuple-element.43.before.i0, bf16[256,768]{1,0:T(8,128)(2,1)S(1)} %get-tuple-element.44.t0, ...), custom_call_target="tpu_custom_call" | custom-call | flops 13200000000 | bytes 7111684 | tf_op jit(solution)/shard_map/first/pallas_call | solution.py:63
  19.8 0.0 collective-permute-done.4.t3
  19.8 1.1 %second.1 = (bf16[1024,768]{1,0:T(8,128)(2,1)S(1)}, f32[768,256]{1,0:T(8,128)S(1)}, f32[4,1024]{1,0:T(4,128)S(1)}, f32[4,1024]{1,0:T(4,128)S(1)}) custom-call(f32[1]{0:T(128)S(6)} %copy.8.scale, bf16[256,768]{1,0:T(8,128)(2,1)S(1)} %collective-permute-done.4.t3, bf16[768,768]{1,0:T(8,128)(2,1)S(1)} %get-tuple-element.45.near, ...), custom_call_target="tpu_custom_call" | custom-call | flops 8800000000 | bytes 5177348 | tf_op jit(solution)/shard_map/second/pallas_call | solution.py:63
  20.9 0.9 %collective-permute-done.2.i2 = bf16[256,768]{1,0:T(8,128)(2,1)S(1)} collective-permute-done((bf16[256,768]{1,0:T(8,128)(2,1)S(1)}, bf16[256,768]{1,0:T(8,128)(2,1)S(1)}, u32[]{:S(2)}, u32[]{:S(2)}) %collective-permute-start.2) | collective-permute-done | bytes 393248 | tf_op jit(solution)/shard_map/ppermute | solution.py:36
  21.9 1.2 %third.1 = (bf16[256,768]{1,0:T(8,128)(2,1)S(1)}, f32[256,1024]{1,0:T(8,128)S(1)}, f32[4,1024]{1,0:T(4,128)S(1)}, f32[4,1024]{1,0:T(4,128)S(1)}) custom-call(f32[1]{0:T(128)S(6)} %copy.8.scale, bf16[256,768]{1,0:T(8,128)(2,1)S(1)} %collective-permute-done.2.i2, bf16[1024,768]{1,0:T(8,128)(2,1)S(1)} %get-tuple-element.49.txts, ...), custom_call_target="tpu_custom_call" | custom-call | flops 1264999936 | bytes 3473412 | tf_op jit(solution)/shard_map/third/pallas_call | solution.py:63
  23.0 1.9 %collective-permute-start.8 = (f32[4,1024]{1,0:T(4,128)S(1)}, f32[4,1024]{1,0:T(4,128)S(1)}, u32[]{:S(2)}, u32[]{:S(2)}) collective-permute-start(f32[4,1024]{1,0:T(4,128)S(1)} %get-tuple-element.53.mine), channel_id=1, source_target_pairs={{0,1},{1,0},{2,3},{3,2},{4,5},{5,4},{6,7},{7,6},{8,9},{9,8},{10,11... | collective-permute-start | bytes 49160 | tf_op jit(solution)/shard_map/ppermute | solution.py:29
  24.9 1.2 %collective-permute-start.6 = (f32[4,1024]{1,0:T(4,128)S(1)}, f32[4,1024]{1,0:T(4,128)S(1)}, u32[]{:S(2)}, u32[]{:S(2)}) collective-permute-start(f32[4,1024]{1,0:T(4,128)S(1)} %get-tuple-element.52.mine), channel_id=1, source_target_pairs={{0,12},{1,13},{2,14},{3,15},{4,8},{5,9},{6,10},{7,11},{8,4},{9,5},... | collective-permute-start | bytes 49160 | tf_op jit(solution)/shard_map/ppermute | solution.py:29
  26.1 0.0 collective-permute-done.8.other
  26.2 3.0 %collective-permute-start.9 = (f32[8,1024]{1,0:T(8,128)S(1)}, f32[8,1024]{1,0:T(8,128)S(1)}, u32[]{:S(2)}, u32[]{:S(2)}) collective-permute-start(f32[8,1024]{1,0:T(8,128)S(1)} %join.3.col), channel_id=1, source_target_pairs={{0,2},{1,3},{2,0},{3,1},{4,6},{5,7},{6,4},{7,5},{8,10},{9,11},{10,... | collective-permute-start | bytes 98312 | tf_op jit(solution)/shard_map/ppermute | solution.py:29
  29.2 0.0 collective-permute-done.6.other
  29.2 0.1 collective-permute-start.7
  29.3 2.6 %collective-permute-done.7.row1 = f32[4,1024]{1,0:T(4,128)S(1)} collective-permute-done((f32[4,1024]{1,0:T(4,128)S(1)}, f32[4,1024]{1,0:T(4,128)S(1)}, u32[]{:S(2)}, u32[]{:S(2)}) %collective-permute-start.7) | collective-permute-done | bytes 16416 | tf_op jit(solution)/shard_map/ppermute | solution.py:29
  31.9 0.0 collective-permute-done.9.col2
  31.9 0.1 lse.1
  32.0 2.0 %collective-permute-start.10 = (f32[8,128]{1,0:T(8,128)S(1)}, f32[8,128]{1,0:T(8,128)S(1)}, u32[]{:S(2)}, u32[]{:S(2)}) collective-permute-start(f32[8,128]{1,0:T(8,128)S(1)} %get-tuple-element.54.row), channel_id=1, source_target_pairs={{0,1},{1,0},{2,3},{3,2},{4,5},{5,4},{6,7},{7,6},{8,9},{9,8},{10,11... | collective-permute-start | bytes 12296 | tf_op jit(solution)/shard_map/ppermute | solution.py:29
  34.1 0.0 collective-permute-start.11
  34.1 1.3 %weight.1 = (bf16[512,1024]{1,0:T(8,128)(2,1)S(1)}, bf16[512,1024]{1,0:T(8,128)(2,1)S(1)}) custom-call(f32[768,768]{1,0:T(8,128)S(1)} %get-tuple-element.56.first, f32[768,256]{1,0:T(8,128)S(1)} %get-tuple-element.57.second, f32[256,1024]{1,0:T(8,128)S(1)} %get-tuple-element.58.third, f32[2,1024]{1,0:T(2,128)S(1)} %get-tuple-element.59.lse, s32[1,256]{1,0:T(1,128)S(1)} %bitcast.2), custom_call_target="tpu_custom_call" | custom-call | flops 1430000000 | bytes 6300672 | tf_op jit(solution)/shard_map/weight/pallas_call | solution.py:63
  35.3 1.4 %early.1 = (bf16[512,768]{1,0:T(8,128)(2,1)S(1)}, bf16[256,768]{1,0:T(8,128)(2,1)S(1)}) custom-call(bf16[512,1024]{1,0:T(8,128)(2,1)S(1)} %get-tuple-element.60.w01, bf16[512,1024]{1,0:T(8,128)(2,1)S(1)} %get-tuple-element.61.w23, bf16[768,768]{1,0:T(8,128)(2,1)S(1)} %get-tuple-element.45.near, bf16[256,768]{1,0:T(8,128)(2,1)S(1)} %get-tuple-element.62.far, ...), custom_call_target="tpu_custom_call" | custom-call | flops 1540000000 | bytes 6422528 | tf_op jit(solution)/shard_map/early/pallas_call | solution.py:63
  36.8 0.0 collective-permute-done.10.row_core
  36.8 0.0 collective-permute-done.11.col1
  36.8 0.1 half.1
  36.9 1.2 %collective-permute-start.14 = (bf16[512,768]{1,0:T(8,128)(2,1)S(1)}, bf16[512,768]{1,0:T(8,128)(2,1)S(1)}, u32[]{:S(2)}, u32[]{:S(2)}) collective-permute-start(bf16[512,768]{1,0:T(8,128)(2,1)S(1)} %get-tuple-element.69), channel_id=1, source_target_pairs={{0,1},{1,0},{2,3},{3,2},{4,5},{5,4},{6,7},{7,6},{8,9},{9,8},{10,11... | collective-permute-start | bytes 2359304 | tf_op jit(solution)/shard_map/ppermute | solution.py:29
  38.1 1.3 %collective-permute-start.15 = (bf16[256,768]{1,0:T(8,128)(2,1)S(1)}, bf16[256,768]{1,0:T(8,128)(2,1)S(1)}, u32[]{:S(2)}, u32[]{:S(2)}) collective-permute-start(bf16[256,768]{1,0:T(8,128)(2,1)S(1)} %get-tuple-element.72), channel_id=1, source_target_pairs={{0,4},{1,13},{2,6},{3,15},{4,0},{5,9},{6,2},{7,11},{8,12},{9,5},{1... | collective-permute-start | bytes 1179656 | tf_op jit(solution)/shard_map/ppermute | solution.py:36
  39.4 1.2 %collective-permute-start.12 = (f32[8,128]{1,0:T(8,128)S(1)}, f32[8,128]{1,0:T(8,128)S(1)}, u32[]{:S(2)}, u32[]{:S(2)}) collective-permute-start(f32[8,128]{1,0:T(8,128)S(1)} %get-tuple-element.65.before.a), channel_id=1, source_target_pairs={{0,16},{16,0},{32,48},{48,32},{64,80},{80,64},{96,112},{112,96},{1... | collective-permute-start | bytes 12296 | tf_op jit(solution)/shard_map/ppermute | solution.py:29
  40.6 1.0 %text.3 = (f32[256,768]{1,0:T(8,128)S(1)}, f32[256,768]{1,0:T(8,128)S(1)}, f32[8,128]{1,0:T(8,128)S(1)}) custom-call(bf16[512,1024]{1,0:T(8,128)(2,1)S(1)} %get-tuple-element.60.w01, bf16[512,1024]{1,0:T(8,128)(2,1)S(1)} %get-tuple-element.61.w23, bf16[768,768]{1,0:T(8,128)(2,1)S(1)} %get-tuple-element.45.near, bf16[256,768]{1,0:T(8,128)(2,1)S(1)} %get-tuple-element.62.far, ...), custom_call_target="tpu_custom_call" | custom-call | flops 1210000000 | bytes 5251072 | tf_op jit(solution)/shard_map/text/pallas_call | solution.py:63
  41.7 1.4 %image.3 = (f32[256,768]{1,0:T(8,128)S(1)}, bf16[256,768]{1,0:T(8,128)(2,1)S(1)}, f32[256,768]{1,0:T(8,128)S(1)}) custom-call(bf16[512,1024]{1,0:T(8,128)(2,1)S(1)} %get-tuple-element.60.w01, bf16[512,1024]{1,0:T(8,128)(2,1)S(1)} %get-tuple-element.61.w23, bf16[1024,768]{1,0:T(8,128)(2,1)S(1)} %get-tuple-element.49.txts, f32[8,128]{1,0:T(8,128)S(1)} %get-tuple-element.65.before.a), custom_call_target="tpu_custom_call" | custom-call | flops 1210000000 | bytes 5640192 | tf_op jit(solution)/shard_map/image/pallas_call | solution.py:63
  43.1 0.0 collective-permute-done.12.b
  43.1 1.5 %collective-permute-start.13 = (f32[8,128]{1,0:T(8,128)S(1)}, f32[8,128]{1,0:T(8,128)S(1)}, u32[]{:S(2)}, u32[]{:S(2)}) collective-permute-start(f32[8,128]{1,0:T(8,128)S(1)} %side.2.before.a), channel_id=1, source_target_pairs={{0,18},{1,13},{2,16},{3,15},{4,22},{5,9},{6,20},{7,11},{8,26},{9,5... | collective-permute-start | bytes 12296 | tf_op jit(solution)/shard_map/ppermute | solution.py:36
  44.7 0.1 across.1
  44.8 2.7 %collective-permute-start.20 = (bf16[256,768]{1,0:T(8,128)(2,1)S(1)}, bf16[256,768]{1,0:T(8,128)(2,1)S(1)}, u32[]{:S(2)}, u32[]{:S(2)}) collective-permute-start(bf16[256,768]{1,0:T(8,128)(2,1)S(1)} %get-tuple-element.71.before), channel_id=1, source_target_pairs={{0,2},{1,3},{2,0},{3,1},{4,6},{5,7},{6,4},{7,5},{8,10},{9,11},{10,... | collective-permute-start | bytes 1179656 | tf_op jit(solution)/shard_map/ppermute | solution.py:29
  47.5 0.0 collective-permute-done.13.b
  47.5 0.0 collective-permute-done.15.before_too.relayed
  47.5 0.9 %collective-permute-start.16 = (f32[8,128]{1,0:T(8,128)S(1)}, f32[8,128]{1,0:T(8,128)S(1)}, u32[]{:S(2)}, u32[]{:S(2)}) collective-permute-start(f32[8,128]{1,0:T(8,128)S(1)} %sides.1.before.mine), channel_id=1, source_target_pairs={{0,1},{1,0},{2,3},{3,2},{4,5},{5,4},{6,7},{7,6},{8,9},{9,8},{10,11... | collective-permute-start | bytes 12296 | tf_op jit(solution)/shard_map/ppermute | solution.py:29
  48.4 1.2 %collective-permute-start.22 = (bf16[256,768]{1,0:T(8,128)(2,1)S(1)}, bf16[256,768]{1,0:T(8,128)(2,1)S(1)}, u32[]{:S(2)}, u32[]{:S(2)}) collective-permute-start(bf16[256,768]{1,0:T(8,128)(2,1)S(1)} %get-tuple-element.76), channel_id=1, source_target_pairs={{0,4},{1,13},{2,6},{3,15},{4,0},{5,9},{6,2},{7,11},{8,12},{9,5},{1... | collective-permute-start | bytes 1179656 | tf_op jit(solution)/shard_map/ppermute | solution.py:36
  49.6 0.1 late.1.before
  49.6 0.0 copy-start.1
  49.7 0.1 collective-permute-start.23
  49.8 0.0 collective-permute-done.16.other
  49.8 0.1 total.1.a
  49.9 5.7 %collective-permute-start.17 = (f32[8,128]{1,0:T(8,128)S(1)}, f32[8,128]{1,0:T(8,128)S(1)}, u32[]{:S(2)}, u32[]{:S(2)}) collective-permute-start(f32[8,128]{1,0:T(8,128)S(1)} %total.1.a), channel_id=1, source_target_pairs={{0,32},{1,225},{2,34},{3,227},{4,36},{5,229},{6,38},{7,231},{8,40}... | collective-permute-start | bytes 12296 | tf_op jit(solution)/shard_map/ppermute | solution.py:36
  55.5 1.3 %collective-permute-done.17.b = f32[8,128]{1,0:T(8,128)S(1)} collective-permute-done((f32[8,128]{1,0:T(8,128)S(1)}, f32[8,128]{1,0:T(8,128)S(1)}, u32[]{:S(2)}, u32[]{:S(2)}) %collective-permute-start.17) | collective-permute-done | bytes 4128 | tf_op jit(solution)/shard_map/ppermute | solution.py:36
  56.8 0.0 collective-permute-start.18
  56.8 1.2 %collective-permute-done.18.other = f32[8,128]{1,0:T(8,128)S(1)} collective-permute-done((f32[8,128]{1,0:T(8,128)S(1)}, f32[8,128]{1,0:T(8,128)S(1)}, u32[]{:S(2)}, u32[]{:S(2)}) %collective-permute-start.18) | collective-permute-done | bytes 4128 | tf_op jit(solution)/shard_map/ppermute | solution.py:29
  58.0 2.1 %collective-permute-start.19 = (f32[8,128]{1,0:T(8,128)S(1)}, f32[8,128]{1,0:T(8,128)S(1)}, u32[]{:S(2)}, u32[]{:S(2)}) collective-permute-start(f32[8,128]{1,0:T(8,128)S(1)} %planes.1.a), channel_id=1, source_target_pairs={{0,160},{1,97},{2,162},{3,99},{4,164},{5,101},{6,166},{7,103},{8,1... | collective-permute-start | bytes 12296 | tf_op jit(solution)/shard_map/ppermute | solution.py:36
  60.1 1.2 %text_grad.1 = (bf16[256,768]{1,0:T(8,128)(2,1)}, f32[8,128]{1,0:T(8,128)S(1)}) custom-call(f32[1]{0:T(128)S(6)} %copy.8.scale, bf16[256,768]{1,0:T(8,128)(2,1)S(1)} %copy-done.1, f32[256,768]{1,0:T(8,128)S(1)} %get-tuple-element.73.refs_0_, bf16[512,768]{1,0:T(8,128)(2,1)S(1)} %collective-permute-done.14.core_part.refs_1_, ...), custom_call_target="tpu_custom_call" | custom-call | flops 880000000 | bytes 2756612 | tf_op jit(solution)/shard_map/text_grad/pallas_call | solution.py:63
  61.3 2.3 %collective-permute-done.19.b = f32[8,128]{1,0:T(8,128)S(1)} collective-permute-done((f32[8,128]{1,0:T(8,128)S(1)}, f32[8,128]{1,0:T(8,128)S(1)}, u32[]{:S(2)}, u32[]{:S(2)}) %collective-permute-start.19) | collective-permute-done | bytes 4128 | tf_op jit(solution)/shard_map/ppermute | solution.py:36
  63.6 0.6 collective-permute-start.21
  64.2 0.0 collective-permute-done.22.refs_1_
  64.2 0.0 collective-permute-done.23.refs_2_
  64.2 1.2 %image_grad.1 = (bf16[256,768]{1,0:T(8,128)(2,1)}, f32[8,128]{1,0:T(8,128)S(1)}) custom-call(f32[1]{0:T(128)S(6)} %copy.8.scale, bf16[256,768]{1,0:T(8,128)(2,1)S(1)} %copy-done.3, f32[256,768]{1,0:T(8,128)S(1)} %get-tuple-element.75.refs_0_, bf16[256,768]{1,0:T(8,128)(2,1)S(1)} %collective-permute-done.22.refs_1_, ...), custom_call_target="tpu_custom_call" | custom-call | flops 880000000 | bytes 2363396 | tf_op jit(solution)/shard_map/image_grad/pallas_call | solution.py:63
  65.3 0.0 collective-permute-done.21.other
  65.4 0.7 scalar.1
  (18 shorter events, 0.1 us)
Async XLA Ops:
  0.6 11.5 %collective-permute-start.1 = (bf16[256,768]{1,0:T(8,128)(2,1)}, bf16[256,768]{1,0:T(8,128)(2,1)S(1)}, u32[]{:S(2)}, u32[]{:S(2)}) collective-permute-start(bf16[256,768]{1,0:T(8,128)(2,1)} %values.3), channel_id=1, source_target_pairs={{0,12},{1,13},{2,14},{3,15},{4,8},{5,9},{6,10},{7,11},{8,4},{9,5},... | collective-permute-start | bytes 1179656 | tf_op jit(solution)/shard_map/ppermute | solution.py:29
  4.0 9.9 %collective-permute-start = (bf16[256,768]{1,0:T(8,128)(2,1)}, bf16[256,768]{1,0:T(8,128)(2,1)S(1)}, u32[]{:S(2)}, u32[]{:S(2)}) collective-permute-start(bf16[256,768]{1,0:T(8,128)(2,1)} %values.3), channel_id=1, source_target_pairs={{0,4},{1,5},{2,6},{3,7},{4,0},{5,1},{6,2},{7,3},{8,12},{9,13},{10,... | collective-permute-start | bytes 1179656 | tf_op jit(solution)/shard_map/ppermute | solution.py:29
  4.0 11.5 %collective-permute-start.3 = (bf16[256,768]{1,0:T(8,128)(2,1)}, bf16[256,768]{1,0:T(8,128)(2,1)S(1)}, u32[]{:S(2)}, u32[]{:S(2)}) collective-permute-start(bf16[256,768]{1,0:T(8,128)(2,1)} %values.2), channel_id=1, source_target_pairs={{0,2},{1,3},{2,0},{3,1},{4,6},{5,7},{6,4},{7,5},{8,10},{9,11},{10,... | collective-permute-start | bytes 1179656 | tf_op jit(solution)/shard_map/ppermute | solution.py:29
  6.9 10.3 %collective-permute-start.5 = (bf16[256,768]{1,0:T(8,128)(2,1)}, bf16[256,768]{1,0:T(8,128)(2,1)S(1)}, u32[]{:S(2)}, u32[]{:S(2)}) collective-permute-start(bf16[256,768]{1,0:T(8,128)(2,1)} %values.2), channel_id=1, source_target_pairs={{0,1},{1,0},{2,3},{3,2},{4,5},{5,4},{6,7},{7,6},{8,9},{9,8},{10,11... | collective-permute-start | bytes 1179656 | tf_op jit(solution)/shard_map/ppermute | solution.py:29
  9.1 1.0 %copy-start = (bf16[256,768]{1,0:T(8,128)(2,1)S(1)}, bf16[256,768]{1,0:T(8,128)(2,1)}, u32[]{:S(2)}) copy-start(bf16[256,768]{1,0:T(8,128)(2,1)} %values.2) | copy-start | bytes 1179652
  10.0 1.0 %copy-start.2 = (bf16[256,768]{1,0:T(8,128)(2,1)S(1)}, bf16[256,768]{1,0:T(8,128)(2,1)}, u32[]{:S(2)}) copy-start(bf16[256,768]{1,0:T(8,128)(2,1)} %values.3) | copy-start | bytes 1179652
  13.9 3.4 %copy-start.4 = (s32[256]{0:T(256)S(1)}, s32[256]{0:T(256)}, u32[]{:S(2)}) copy-start(s32[256]{0:T(256)} %param.6) | copy-start | bytes 3076
  13.9 7.9 %collective-permute-start.2 = (bf16[256,768]{1,0:T(8,128)(2,1)S(1)}, bf16[256,768]{1,0:T(8,128)(2,1)S(1)}, u32[]{:S(2)}, u32[]{:S(2)}) collective-permute-start(bf16[256,768]{1,0:T(8,128)(2,1)S(1)} %pick.1), channel_id=1, source_target_pairs={{0,4},{1,13},{2,6},{3,15},{4,0},{5,9},{6,2},{7,11},{8,12},{9,5},{1... | collective-permute-start | bytes 1179656 | tf_op jit(solution)/shard_map/ppermute | solution.py:36
  15.6 4.3 %collective-permute-start.4 = (bf16[256,768]{1,0:T(8,128)(2,1)S(1)}, bf16[256,768]{1,0:T(8,128)(2,1)S(1)}, u32[]{:S(2)}, u32[]{:S(2)}) collective-permute-start(bf16[256,768]{1,0:T(8,128)(2,1)S(1)} %collective-permute-done.3.t2), channel_id=1, source_target_pairs={{0,1},{1,0},{2,3},{3,2},{4,5},{5,4},{6,7},{7,6},{8,9},{9,8},{10,11... | collective-permute-start | bytes 1179656 | tf_op jit(solution)/shard_map/ppermute | solution.py:29
  23.0 3.1 %collective-permute-start.8 = (f32[4,1024]{1,0:T(4,128)S(1)}, f32[4,1024]{1,0:T(4,128)S(1)}, u32[]{:S(2)}, u32[]{:S(2)}) collective-permute-start(f32[4,1024]{1,0:T(4,128)S(1)} %get-tuple-element.53.mine), channel_id=1, source_target_pairs={{0,1},{1,0},{2,3},{3,2},{4,5},{5,4},{6,7},{7,6},{8,9},{9,8},{10,11... | collective-permute-start | bytes 49160 | tf_op jit(solution)/shard_map/ppermute | solution.py:29
  24.9 4.3 %collective-permute-start.6 = (f32[4,1024]{1,0:T(4,128)S(1)}, f32[4,1024]{1,0:T(4,128)S(1)}, u32[]{:S(2)}, u32[]{:S(2)}) collective-permute-start(f32[4,1024]{1,0:T(4,128)S(1)} %get-tuple-element.52.mine), channel_id=1, source_target_pairs={{0,12},{1,13},{2,14},{3,15},{4,8},{5,9},{6,10},{7,11},{8,4},{9,5},... | collective-permute-start | bytes 49160 | tf_op jit(solution)/shard_map/ppermute | solution.py:29
  26.2 5.7 %collective-permute-start.9 = (f32[8,1024]{1,0:T(8,128)S(1)}, f32[8,1024]{1,0:T(8,128)S(1)}, u32[]{:S(2)}, u32[]{:S(2)}) collective-permute-start(f32[8,1024]{1,0:T(8,128)S(1)} %join.3.col), channel_id=1, source_target_pairs={{0,2},{1,3},{2,0},{3,1},{4,6},{5,7},{6,4},{7,5},{8,10},{9,11},{10,... | collective-permute-start | bytes 98312 | tf_op jit(solution)/shard_map/ppermute | solution.py:29
  29.2 2.7 %collective-permute-start.7 = (f32[4,1024]{1,0:T(4,128)S(1)}, f32[4,1024]{1,0:T(4,128)S(1)}, u32[]{:S(2)}, u32[]{:S(2)}) collective-permute-start(f32[4,1024]{1,0:T(4,128)S(1)} %join.2.row), channel_id=1, source_target_pairs={{0,4},{1,5},{2,6},{3,7},{4,0},{5,1},{6,2},{7,3},{8,12},{9,13},{10,... | collective-permute-start | bytes 49160 | tf_op jit(solution)/shard_map/ppermute | solution.py:29
  32.0 4.7 %collective-permute-start.10 = (f32[8,128]{1,0:T(8,128)S(1)}, f32[8,128]{1,0:T(8,128)S(1)}, u32[]{:S(2)}, u32[]{:S(2)}) collective-permute-start(f32[8,128]{1,0:T(8,128)S(1)} %get-tuple-element.54.row), channel_id=1, source_target_pairs={{0,1},{1,0},{2,3},{3,2},{4,5},{5,4},{6,7},{7,6},{8,9},{9,8},{10,11... | collective-permute-start | bytes 12296 | tf_op jit(solution)/shard_map/ppermute | solution.py:29
  34.1 2.7 %collective-permute-start.11 = (f32[8,128]{1,0:T(8,128)S(1)}, f32[8,128]{1,0:T(8,128)S(1)}, u32[]{:S(2)}, u32[]{:S(2)}) collective-permute-start(f32[8,128]{1,0:T(8,128)S(1)} %get-tuple-element.55.col), channel_id=1, source_target_pairs={{0,4},{1,5},{2,6},{3,7},{4,0},{5,1},{6,2},{7,3},{8,12},{9,13},{10,... | collective-permute-start | bytes 12296 | tf_op jit(solution)/shard_map/ppermute | solution.py:29
  36.9 7.8 %collective-permute-start.14 = (bf16[512,768]{1,0:T(8,128)(2,1)S(1)}, bf16[512,768]{1,0:T(8,128)(2,1)S(1)}, u32[]{:S(2)}, u32[]{:S(2)}) collective-permute-start(bf16[512,768]{1,0:T(8,128)(2,1)S(1)} %get-tuple-element.69), channel_id=1, source_target_pairs={{0,1},{1,0},{2,3},{3,2},{4,5},{5,4},{6,7},{7,6},{8,9},{9,8},{10,11... | collective-permute-start | bytes 2359304 | tf_op jit(solution)/shard_map/ppermute | solution.py:29
  38.1 9.4 %collective-permute-start.15 = (bf16[256,768]{1,0:T(8,128)(2,1)S(1)}, bf16[256,768]{1,0:T(8,128)(2,1)S(1)}, u32[]{:S(2)}, u32[]{:S(2)}) collective-permute-start(bf16[256,768]{1,0:T(8,128)(2,1)S(1)} %get-tuple-element.72), channel_id=1, source_target_pairs={{0,4},{1,13},{2,6},{3,15},{4,0},{5,9},{6,2},{7,11},{8,12},{9,5},{1... | collective-permute-start | bytes 1179656 | tf_op jit(solution)/shard_map/ppermute | solution.py:36
  39.4 3.7 %collective-permute-start.12 = (f32[8,128]{1,0:T(8,128)S(1)}, f32[8,128]{1,0:T(8,128)S(1)}, u32[]{:S(2)}, u32[]{:S(2)}) collective-permute-start(f32[8,128]{1,0:T(8,128)S(1)} %get-tuple-element.65.before.a), channel_id=1, source_target_pairs={{0,16},{16,0},{32,48},{48,32},{64,80},{80,64},{96,112},{112,96},{1... | collective-permute-start | bytes 12296 | tf_op jit(solution)/shard_map/ppermute | solution.py:29
  43.1 4.4 %collective-permute-start.13 = (f32[8,128]{1,0:T(8,128)S(1)}, f32[8,128]{1,0:T(8,128)S(1)}, u32[]{:S(2)}, u32[]{:S(2)}) collective-permute-start(f32[8,128]{1,0:T(8,128)S(1)} %side.2.before.a), channel_id=1, source_target_pairs={{0,18},{1,13},{2,16},{3,15},{4,22},{5,9},{6,20},{7,11},{8,26},{9,5... | collective-permute-start | bytes 12296 | tf_op jit(solution)/shard_map/ppermute | solution.py:36
  44.8 15.3 %collective-permute-start.20 = (bf16[256,768]{1,0:T(8,128)(2,1)S(1)}, bf16[256,768]{1,0:T(8,128)(2,1)S(1)}, u32[]{:S(2)}, u32[]{:S(2)}) collective-permute-start(bf16[256,768]{1,0:T(8,128)(2,1)S(1)} %get-tuple-element.71.before), channel_id=1, source_target_pairs={{0,2},{1,3},{2,0},{3,1},{4,6},{5,7},{6,4},{7,5},{8,10},{9,11},{10,... | collective-permute-start | bytes 1179656 | tf_op jit(solution)/shard_map/ppermute | solution.py:29
  47.5 2.3 %collective-permute-start.16 = (f32[8,128]{1,0:T(8,128)S(1)}, f32[8,128]{1,0:T(8,128)S(1)}, u32[]{:S(2)}, u32[]{:S(2)}) collective-permute-start(f32[8,128]{1,0:T(8,128)S(1)} %sides.1.before.mine), channel_id=1, source_target_pairs={{0,1},{1,0},{2,3},{3,2},{4,5},{5,4},{6,7},{7,6},{8,9},{9,8},{10,11... | collective-permute-start | bytes 12296 | tf_op jit(solution)/shard_map/ppermute | solution.py:29
  48.4 15.8 %collective-permute-start.22 = (bf16[256,768]{1,0:T(8,128)(2,1)S(1)}, bf16[256,768]{1,0:T(8,128)(2,1)S(1)}, u32[]{:S(2)}, u32[]{:S(2)}) collective-permute-start(bf16[256,768]{1,0:T(8,128)(2,1)S(1)} %get-tuple-element.76), channel_id=1, source_target_pairs={{0,4},{1,13},{2,6},{3,15},{4,0},{5,9},{6,2},{7,11},{8,12},{9,5},{1... | collective-permute-start | bytes 1179656 | tf_op jit(solution)/shard_map/ppermute | solution.py:36
  49.6 10.5 %copy-start.1 = (bf16[256,768]{1,0:T(8,128)(2,1)S(1)}, bf16[256,768]{1,0:T(8,128)(2,1)}, u32[]{:S(2)}) copy-start(bf16[256,768]{1,0:T(8,128)(2,1)} %values.2) | copy-start | bytes 1179652
  49.7 14.5 %collective-permute-start.23 = (bf16[256,768]{1,0:T(8,128)(2,1)S(1)}, bf16[256,768]{1,0:T(8,128)(2,1)S(1)}, u32[]{:S(2)}, u32[]{:S(2)}) collective-permute-start(bf16[256,768]{1,0:T(8,128)(2,1)S(1)} %late.1.before), channel_id=1, source_target_pairs={{0,12},{1,5},{2,14},{3,7},{4,8},{5,1},{6,10},{7,3},{8,4},{9,13},{1... | collective-permute-start | bytes 1179656 | tf_op jit(solution)/shard_map/ppermute | solution.py:36
  49.9 6.9 %collective-permute-start.17 = (f32[8,128]{1,0:T(8,128)S(1)}, f32[8,128]{1,0:T(8,128)S(1)}, u32[]{:S(2)}, u32[]{:S(2)}) collective-permute-start(f32[8,128]{1,0:T(8,128)S(1)} %total.1.a), channel_id=1, source_target_pairs={{0,32},{1,225},{2,34},{3,227},{4,36},{5,229},{6,38},{7,231},{8,40}... | collective-permute-start | bytes 12296 | tf_op jit(solution)/shard_map/ppermute | solution.py:36
  56.8 1.2 %collective-permute-start.18 = (f32[8,128]{1,0:T(8,128)S(1)}, f32[8,128]{1,0:T(8,128)S(1)}, u32[]{:S(2)}, u32[]{:S(2)}) collective-permute-start(f32[8,128]{1,0:T(8,128)S(1)} %add.1.held), channel_id=1, source_target_pairs={{0,1},{1,0},{2,3},{3,2},{4,5},{5,4},{6,7},{7,6},{8,9},{9,8},{10,11... | collective-permute-start | bytes 12296 | tf_op jit(solution)/shard_map/ppermute | solution.py:29
  58.0 5.5 %collective-permute-start.19 = (f32[8,128]{1,0:T(8,128)S(1)}, f32[8,128]{1,0:T(8,128)S(1)}, u32[]{:S(2)}, u32[]{:S(2)}) collective-permute-start(f32[8,128]{1,0:T(8,128)S(1)} %planes.1.a), channel_id=1, source_target_pairs={{0,160},{1,97},{2,162},{3,99},{4,164},{5,101},{6,166},{7,103},{8,1... | collective-permute-start | bytes 12296 | tf_op jit(solution)/shard_map/ppermute | solution.py:36
  60.1 4.1 %copy-start.3 = (bf16[256,768]{1,0:T(8,128)(2,1)S(1)}, bf16[256,768]{1,0:T(8,128)(2,1)}, u32[]{:S(2)}) copy-start(bf16[256,768]{1,0:T(8,128)(2,1)} %values.3) | copy-start | bytes 1179652
  63.6 1.8 %collective-permute-start.21 = (f32[8,128]{1,0:T(8,128)S(1)}, f32[8,128]{1,0:T(8,128)S(1)}, u32[]{:S(2)}, u32[]{:S(2)}) collective-permute-start(f32[8,128]{1,0:T(8,128)S(1)} %side.3.held), channel_id=1, source_target_pairs={{0,1},{1,0},{2,3},{3,2},{4,5},{5,4},{6,7},{7,6},{8,9},{9,8},{10,11... | collective-permute-start | bytes 12296 | tf_op jit(solution)/shard_map/ppermute | solution.py:29

commit v7 on v5

--- a/solution.py
+++ b/solution.py
@@ -226,8 +226,8 @@
     return value, mean, mine[2:3, :] + swap(2)
 
 
-def join_kernel(mine, other, out):
-    out[0:1, :], out[1:2, :], out[2:3, :] = joined(mine, other, 1)
+def join_kernel(bits, mine, other, out):
+    out[0:1, :], out[1:2, :], out[2:3, :] = joined(mine, other, bits)
     out[3:, :] = jnp.zeros((out.shape[0] - 3, out.shape[1]), jnp.float32)
 
 
@@ -237,9 +237,9 @@
     return (at[0] + at[1]) + (at[2] + at[3])
 
 
-def lse_kernel(row, row3, col, col2, lse, row_sums, col_sums):
+def lse_kernel(row, row1, col, col2, lse, row_sums, col_sums):
     lane = lax.broadcasted_iota(jnp.int32, row_sums.shape, 1)
-    sides = ((joined(row, row3, 3), row_sums), (joined(col, col2, 2), col_sums))
+    sides = ((joined(row, row1, 1), row_sums), (joined(col, col2, 2), col_sums))
     for at, ((value, mean, matched), out) in enumerate(sides):
         lse[at : at + 1, :] = value
         loss, slope = slot_sum(0.5 * value - matched), slot_sum(0.5 * mean - matched)
@@ -404,12 +404,17 @@
         third_kernel, "third", [block, ((rows, group), f32), parts, parts],
         logit_scale, i2, txts, row_part, col_part, scalar=True,
     )
-    (col_part,) = call(join_kernel, "join", [((2 * SLOTS, group), f32)], col_part, swapped(col_part, CORE))
+    (col_part,) = call(
+        functools.partial(join_kernel, 1), "join", [((2 * SLOTS, group), f32)],
+        col_part, swapped(col_part, CORE),
+    )
     col_y = swapped(col_part, Y)
-    (row_part,) = call(join_kernel, "join", [parts], row_part, swapped(row_part, X1))
+    (row_part,) = call(
+        functools.partial(join_kernel, 3), "join", [parts], row_part, swapped(row_part, X3)
+    )
     lse, row_sums, col_sums = call(
         lse_kernel, "lse", [((2, group), f32), few, few],
-        row_part, swapped(row_part, X3), col_part, col_y,
+        row_part, swapped(row_part, X1), col_part, col_y,
     )
     row_core, col1 = swapped(row_sums, CORE), swapped(col_sums, X1)
     heavy = ((2 * rows, group), bf16)

time: 66.4 us -> 66.3 us (level)
  waiting for transfers between devices: 12.1 us -> 11.3 us
  starting transfers between devices: 37.5 us -> 38.2 us
    ppermute x17, waiting for transfers between devices: 7.99 us -> 7.2 us  [swapped(): lax.ppermute(value, axis, [(i, i ^ bits) for i in range(lax.axis_size(axi...]
  transfers between devices with their start and end apart: 24 -> 24, of which waited for: 9 -> 8; matrix products, arithmetic and copies ran while one was open for 0% -> 0% of each run, Pallas kernels for 17% -> 17%
where the time goes in v7:
time: 66.3 us; the launch traced here: 66.1 us
  starting transfers between devices  38.2 us (58%)
  Pallas kernels  13 us (20%)
  waiting for transfers between devices  11.3 us (17%)
  local copies, waits for them, and re-layouts  2 us (3%)
  between operations  1.65 us (2%)
    ppermute x17, starting transfers between devices, swapped(): lax.ppermute(value, axis, [(i, i ^ bits) for i in range(lax.axis_size(axi...  24.6 us
    ppermute x7, starting transfers between devices, moved(): return lax.ppermute(value, ('dp', 'blk'), pairs)  13.5 us
    pallas_call x22, Pallas kernels, call(): pl.pallas_call(kernel, out_shape=[jax.ShapeDtypeStruct(s, d) for s, d in...  12.4 us
    ppermute x17, waiting for transfers between devices, swapped(): lax.ppermute(value, axis, [(i, i ^ bits) for i in range(lax.axis_size(axi...  7.2 us
    ppermute x7, waiting for transfers between devices, moved(): return lax.ppermute(value, ('dp', 'blk'), pairs)  4.08 us
    unnamed x10, local copies, waits for them, and re-layouts  2 us
  transfers between devices with their start and end apart: 24, of which 8 were waited for; matrix products, arithmetic and copies ran while one was open for 0% of the time, Pallas kernels for 17%

profile of v7, /device:TPU:1, one launch (start us, length us, event | category | flops | bytes accessed | tf_op | source)
XLA Modules:
  0.0 66.1 jit_solution(11962330885722319351)
XLA Ops:
  0.6 3.4 %collective-permute-start.1 = (bf16[256,768]{1,0:T(8,128)(2,1)}, bf16[256,768]{1,0:T(8,128)(2,1)S(1)}, u32[]{:S(2)}, u32[]{:S(2)}) collective-permute-start(bf16[256,768]{1,0:T(8,128)(2,1)} %image.5), channel_id=1, source_target_pairs={{0,12},{1,13},{2,14},{3,15},{4,8},{5,9},{6,10},{7,11},{8,4},{9,5},... | collective-permute-start | bytes 1179656 | tf_op jit(solution)/shard_map/ppermute | solution.py:29
  4.0 0.0 collective-permute-start
  4.0 2.9 %collective-permute-start.3 = (bf16[256,768]{1,0:T(8,128)(2,1)}, bf16[256,768]{1,0:T(8,128)(2,1)S(1)}, u32[]{:S(2)}, u32[]{:S(2)}) collective-permute-start(bf16[256,768]{1,0:T(8,128)(2,1)} %text.5), channel_id=1, source_target_pairs={{0,2},{1,3},{2,0},{3,1},{4,6},{5,7},{6,4},{7,5},{8,10},{9,11},{10,... | collective-permute-start | bytes 1179656 | tf_op jit(solution)/shard_map/ppermute | solution.py:29
  6.9 1.5 %collective-permute-start.5 = (bf16[256,768]{1,0:T(8,128)(2,1)}, bf16[256,768]{1,0:T(8,128)(2,1)S(1)}, u32[]{:S(2)}, u32[]{:S(2)}) collective-permute-start(bf16[256,768]{1,0:T(8,128)(2,1)} %text.5), channel_id=1, source_target_pairs={{0,1},{1,0},{2,3},{3,2},{4,5},{5,4},{6,7},{7,6},{8,9},{9,8},{10,11... | collective-permute-start | bytes 1179656 | tf_op jit(solution)/shard_map/ppermute | solution.py:29
  9.1 0.0 copy-start
  9.1 1.0 %copy-done = bf16[256,768]{1,0:T(8,128)(2,1)S(1)} copy-done((bf16[256,768]{1,0:T(8,128)(2,1)S(1)}, bf16[256,768]{1,0:T(8,128)(2,1)}, u32[]{:S(2)}) %copy-start) | copy-done | bytes 393240
  10.1 1.0 %copy-done.2 = bf16[256,768]{1,0:T(8,128)(2,1)S(1)} copy-done((bf16[256,768]{1,0:T(8,128)(2,1)S(1)}, bf16[256,768]{1,0:T(8,128)(2,1)}, u32[]{:S(2)}) %copy-start.2) | copy-done | bytes 393240
  11.0 0.2 own.1
  11.3 0.8 %collective-permute-done.1.i3 = bf16[256,768]{1,0:T(8,128)(2,1)S(1)} collective-permute-done((bf16[256,768]{1,0:T(8,128)(2,1)}, bf16[256,768]{1,0:T(8,128)(2,1)S(1)}, u32[]{:S(2)}, u32[]{:S(2)}) %collective-permute-start.1) | collective-permute-done | bytes 393248 | tf_op jit(solution)/shard_map/ppermute | solution.py:29
  12.1 1.8 %collective-permute-done.i1 = bf16[256,768]{1,0:T(8,128)(2,1)S(1)} collective-permute-done((bf16[256,768]{1,0:T(8,128)(2,1)}, bf16[256,768]{1,0:T(8,128)(2,1)S(1)}, u32[]{:S(2)}, u32[]{:S(2)}) %collective-permute-start) | collective-permute-done | bytes 393248 | tf_op jit(solution)/shard_map/ppermute | solution.py:29
  13.9 1.6 %collective-permute-start.2 = (bf16[256,768]{1,0:T(8,128)(2,1)S(1)}, bf16[256,768]{1,0:T(8,128)(2,1)S(1)}, u32[]{:S(2)}, u32[]{:S(2)}) collective-permute-start(bf16[256,768]{1,0:T(8,128)(2,1)S(1)} %pick.1), channel_id=1, source_target_pairs={{0,4},{1,13},{2,6},{3,15},{4,0},{5,9},{6,2},{7,11},{8,12},{9,5},{1... | collective-permute-start | bytes 1179656 | tf_op jit(solution)/shard_map/ppermute | solution.py:36
  15.6 0.0 collective-permute-done.3.t2
  15.6 1.7 %collective-permute-start.4 = (bf16[256,768]{1,0:T(8,128)(2,1)S(1)}, bf16[256,768]{1,0:T(8,128)(2,1)S(1)}, u32[]{:S(2)}, u32[]{:S(2)}) collective-permute-start(bf16[256,768]{1,0:T(8,128)(2,1)S(1)} %collective-permute-done.3.t2), channel_id=1, source_target_pairs={{0,1},{1,0},{2,3},{3,2},{4,5},{5,4},{6,7},{7,6},{8,9},{9,8},{10,11... | collective-permute-start | bytes 1179656 | tf_op jit(solution)/shard_map/ppermute | solution.py:29
  17.3 0.0 collective-permute-done.5.t1
  17.3 2.5 %first.1 = (bf16[768,768]{1,0:T(8,128)(2,1)S(1)}, bf16[768,768]{1,0:T(8,128)(2,1)S(1)}, f32[768,768]{1,0:T(8,128)S(1)}, f32[4,1024]{1,0:T(4,128)S(1)}, f32[4,1024]{1,0:T(4,128)S(1)}) custom-call(f32[1]{0:T(128)S(6)} %copy.8.scale, bf16[256,768]{1,0:T(8,128)(2,1)S(1)} %get-tuple-element.42.before.i0, bf16[256,768]{1,0:T(8,128)(2,1)S(1)} %get-tuple-element.43.t0, ...), custom_call_target="tpu_custom_call" | custom-call | flops 13200000000 | bytes 7111684 | tf_op jit(solution)/shard_map/first/pallas_call | solution.py:63
  19.8 0.0 collective-permute-done.4.t3
  19.8 1.1 %second.1 = (bf16[1024,768]{1,0:T(8,128)(2,1)S(1)}, f32[768,256]{1,0:T(8,128)S(1)}, f32[4,1024]{1,0:T(4,128)S(1)}, f32[4,1024]{1,0:T(4,128)S(1)}) custom-call(f32[1]{0:T(128)S(6)} %copy.8.scale, bf16[256,768]{1,0:T(8,128)(2,1)S(1)} %collective-permute-done.4.t3, bf16[768,768]{1,0:T(8,128)(2,1)S(1)} %get-tuple-element.44.near, ...), custom_call_target="tpu_custom_call" | custom-call | flops 8800000000 | bytes 5177348 | tf_op jit(solution)/shard_map/second/pallas_call | solution.py:63
  20.9 0.9 %collective-permute-done.2.i2 = bf16[256,768]{1,0:T(8,128)(2,1)S(1)} collective-permute-done((bf16[256,768]{1,0:T(8,128)(2,1)S(1)}, bf16[256,768]{1,0:T(8,128)(2,1)S(1)}, u32[]{:S(2)}, u32[]{:S(2)}) %collective-permute-start.2) | collective-permute-done | bytes 393248 | tf_op jit(solution)/shard_map/ppermute | solution.py:36
  21.9 1.2 %third.1 = (bf16[256,768]{1,0:T(8,128)(2,1)S(1)}, f32[256,1024]{1,0:T(8,128)S(1)}, f32[4,1024]{1,0:T(4,128)S(1)}, f32[4,1024]{1,0:T(4,128)S(1)}) custom-call(f32[1]{0:T(128)S(6)} %copy.8.scale, bf16[256,768]{1,0:T(8,128)(2,1)S(1)} %collective-permute-done.2.i2, bf16[1024,768]{1,0:T(8,128)(2,1)S(1)} %get-tuple-element.48.txts, ...), custom_call_target="tpu_custom_call" | custom-call | flops 1264999936 | bytes 3473412 | tf_op jit(solution)/shard_map/third/pallas_call | solution.py:63
  23.0 1.9 %collective-permute-start.8 = (f32[4,1024]{1,0:T(4,128)S(1)}, f32[4,1024]{1,0:T(4,128)S(1)}, u32[]{:S(2)}, u32[]{:S(2)}) collective-permute-start(f32[4,1024]{1,0:T(4,128)S(1)} %get-tuple-element.52.mine), channel_id=1, source_target_pairs={{0,1},{1,0},{2,3},{3,2},{4,5},{5,4},{6,7},{7,6},{8,9},{9,8},{10,11... | collective-permute-start | bytes 49160 | tf_op jit(solution)/shard_map/ppermute | solution.py:29
  24.9 1.2 %collective-permute-start.6 = (f32[4,1024]{1,0:T(4,128)S(1)}, f32[4,1024]{1,0:T(4,128)S(1)}, u32[]{:S(2)}, u32[]{:S(2)}) collective-permute-start(f32[4,1024]{1,0:T(4,128)S(1)} %get-tuple-element.51.mine), channel_id=1, source_target_pairs={{0,12},{1,13},{2,14},{3,15},{4,8},{5,9},{6,10},{7,11},{8,4},{9,5},... | collective-permute-start | bytes 49160 | tf_op jit(solution)/shard_map/ppermute | solution.py:29
  26.1 0.0 collective-permute-done.8.other
  26.2 3.0 %collective-permute-start.9 = (f32[8,1024]{1,0:T(8,128)S(1)}, f32[8,1024]{1,0:T(8,128)S(1)}, u32[]{:S(2)}, u32[]{:S(2)}) collective-permute-start(f32[8,1024]{1,0:T(8,128)S(1)} %join.3.col), channel_id=1, source_target_pairs={{0,2},{1,3},{2,0},{3,1},{4,6},{5,7},{6,4},{7,5},{8,10},{9,11},{10,... | collective-permute-start | bytes 98312 | tf_op jit(solution)/shard_map/ppermute | solution.py:29
  29.2 0.0 collective-permute-done.6.other
  29.2 0.1 collective-permute-start.7
  29.3 2.6 %collective-permute-done.7.row1 = f32[4,1024]{1,0:T(4,128)S(1)} collective-permute-done((f32[4,1024]{1,0:T(4,128)S(1)}, f32[4,1024]{1,0:T(4,128)S(1)}, u32[]{:S(2)}, u32[]{:S(2)}) %collective-permute-start.7) | collective-permute-done | bytes 16416 | tf_op jit(solution)/shard_map/ppermute | solution.py:29
  31.9 0.0 collective-permute-done.9.col2
  31.9 0.1 lse.1
  32.0 2.0 %collective-permute-start.10 = (f32[8,128]{1,0:T(8,128)S(1)}, f32[8,128]{1,0:T(8,128)S(1)}, u32[]{:S(2)}, u32[]{:S(2)}) collective-permute-start(f32[8,128]{1,0:T(8,128)S(1)} %get-tuple-element.53.row), channel_id=1, source_target_pairs={{0,1},{1,0},{2,3},{3,2},{4,5},{5,4},{6,7},{7,6},{8,9},{9,8},{10,11... | collective-permute-start | bytes 12296 | tf_op jit(solution)/shard_map/ppermute | solution.py:29
  34.1 0.0 collective-permute-start.11
  34.1 1.3 %weight.1 = (bf16[512,1024]{1,0:T(8,128)(2,1)S(1)}, bf16[512,1024]{1,0:T(8,128)(2,1)S(1)}) custom-call(f32[768,768]{1,0:T(8,128)S(1)} %get-tuple-element.55.first, f32[768,256]{1,0:T(8,128)S(1)} %get-tuple-element.56.second, f32[256,1024]{1,0:T(8,128)S(1)} %get-tuple-element.57.third, f32[2,1024]{1,0:T(2,128)S(1)} %get-tuple-element.58.lse, s32[1,256]{1,0:T(1,128)S(1)} %bitcast.2), custom_call_target="tpu_custom_call" | custom-call | flops 1430000000 | bytes 6300672 | tf_op jit(solution)/shard_map/weight/pallas_call | solution.py:63
  35.3 1.4 %early.1 = (bf16[512,768]{1,0:T(8,128)(2,1)S(1)}, bf16[256,768]{1,0:T(8,128)(2,1)S(1)}) custom-call(bf16[512,1024]{1,0:T(8,128)(2,1)S(1)} %get-tuple-element.59.w01, bf16[512,1024]{1,0:T(8,128)(2,1)S(1)} %get-tuple-element.60.w23, bf16[768,768]{1,0:T(8,128)(2,1)S(1)} %get-tuple-element.44.near, bf16[256,768]{1,0:T(8,128)(2,1)S(1)} %get-tuple-element.61.far, ...), custom_call_target="tpu_custom_call" | custom-call | flops 1540000000 | bytes 6422528 | tf_op jit(solution)/shard_map/early/pallas_call | solution.py:63
  36.8 0.0 collective-permute-done.10.row_core
  36.8 0.0 collective-permute-done.11.col1
  36.8 0.1 half.1
  36.9 1.2 %collective-permute-start.14 = (bf16[512,768]{1,0:T(8,128)(2,1)S(1)}, bf16[512,768]{1,0:T(8,128)(2,1)S(1)}, u32[]{:S(2)}, u32[]{:S(2)}) collective-permute-start(bf16[512,768]{1,0:T(8,128)(2,1)S(1)} %get-tuple-element.68), channel_id=1, source_target_pairs={{0,1},{1,0},{2,3},{3,2},{4,5},{5,4},{6,7},{7,6},{8,9},{9,8},{10,11... | collective-permute-start | bytes 2359304 | tf_op jit(solution)/shard_map/ppermute | solution.py:29
  38.1 1.3 %collective-permute-start.15 = (bf16[256,768]{1,0:T(8,128)(2,1)S(1)}, bf16[256,768]{1,0:T(8,128)(2,1)S(1)}, u32[]{:S(2)}, u32[]{:S(2)}) collective-permute-start(bf16[256,768]{1,0:T(8,128)(2,1)S(1)} %get-tuple-element.71), channel_id=1, source_target_pairs={{0,4},{1,13},{2,6},{3,15},{4,0},{5,9},{6,2},{7,11},{8,12},{9,5},{1... | collective-permute-start | bytes 1179656 | tf_op jit(solution)/shard_map/ppermute | solution.py:36
  39.4 1.2 %collective-permute-start.12 = (f32[8,128]{1,0:T(8,128)S(1)}, f32[8,128]{1,0:T(8,128)S(1)}, u32[]{:S(2)}, u32[]{:S(2)}) collective-permute-start(f32[8,128]{1,0:T(8,128)S(1)} %get-tuple-element.64.before.a), channel_id=1, source_target_pairs={{0,16},{16,0},{32,48},{48,32},{64,80},{80,64},{96,112},{112,96},{1... | collective-permute-start | bytes 12296 | tf_op jit(solution)/shard_map/ppermute | solution.py:29
  40.6 1.0 %text.4 = (f32[256,768]{1,0:T(8,128)S(1)}, f32[256,768]{1,0:T(8,128)S(1)}, f32[8,128]{1,0:T(8,128)S(1)}) custom-call(bf16[512,1024]{1,0:T(8,128)(2,1)S(1)} %get-tuple-element.59.w01, bf16[512,1024]{1,0:T(8,128)(2,1)S(1)} %get-tuple-element.60.w23, bf16[768,768]{1,0:T(8,128)(2,1)S(1)} %get-tuple-element.44.near, bf16[256,768]{1,0:T(8,128)(2,1)S(1)} %get-tuple-element.61.far, ...), custom_call_target="tpu_custom_call" | custom-call | flops 1210000000 | bytes 5251072 | tf_op jit(solution)/shard_map/text/pallas_call | solution.py:63
  41.7 1.4 %image.4 = (f32[256,768]{1,0:T(8,128)S(1)}, bf16[256,768]{1,0:T(8,128)(2,1)S(1)}, f32[256,768]{1,0:T(8,128)S(1)}) custom-call(bf16[512,1024]{1,0:T(8,128)(2,1)S(1)} %get-tuple-element.59.w01, bf16[512,1024]{1,0:T(8,128)(2,1)S(1)} %get-tuple-element.60.w23, bf16[1024,768]{1,0:T(8,128)(2,1)S(1)} %get-tuple-element.48.txts, f32[8,128]{1,0:T(8,128)S(1)} %get-tuple-element.64.before.a), custom_call_target="tpu_custom_call" | custom-call | flops 1210000000 | bytes 5640192 | tf_op jit(solution)/shard_map/image/pallas_call | solution.py:63
  43.1 0.0 collective-permute-done.12.b
  43.1 1.5 %collective-permute-start.13 = (f32[8,128]{1,0:T(8,128)S(1)}, f32[8,128]{1,0:T(8,128)S(1)}, u32[]{:S(2)}, u32[]{:S(2)}) collective-permute-start(f32[8,128]{1,0:T(8,128)S(1)} %side.2.before.a), channel_id=1, source_target_pairs={{0,18},{1,13},{2,16},{3,15},{4,22},{5,9},{6,20},{7,11},{8,26},{9,5... | collective-permute-start | bytes 12296 | tf_op jit(solution)/shard_map/ppermute | solution.py:36
  44.7 0.0 collective-permute-done.14.core_part
  44.7 0.1 across.1
  44.8 2.7 %collective-permute-start.22 = (bf16[256,768]{1,0:T(8,128)(2,1)S(1)}, bf16[256,768]{1,0:T(8,128)(2,1)S(1)}, u32[]{:S(2)}, u32[]{:S(2)}) collective-permute-start(bf16[256,768]{1,0:T(8,128)(2,1)S(1)} %get-tuple-element.70.before), channel_id=1, source_target_pairs={{0,2},{1,3},{2,0},{3,1},{4,6},{5,7},{6,4},{7,5},{8,10},{9,11},{10,... | collective-permute-start | bytes 1179656 | tf_op jit(solution)/shard_map/ppermute | solution.py:29
  47.5 0.9 %collective-permute-start.16 = (f32[8,128]{1,0:T(8,128)S(1)}, f32[8,128]{1,0:T(8,128)S(1)}, u32[]{:S(2)}, u32[]{:S(2)}) collective-permute-start(f32[8,128]{1,0:T(8,128)S(1)} %sides.1.before.mine), channel_id=1, source_target_pairs={{0,1},{1,0},{2,3},{3,2},{4,5},{5,4},{6,7},{7,6},{8,9},{9,8},{10,11... | collective-permute-start | bytes 12296 | tf_op jit(solution)/shard_map/ppermute | solution.py:29
  48.4 1.2 %collective-permute-start.20 = (bf16[256,768]{1,0:T(8,128)(2,1)S(1)}, bf16[256,768]{1,0:T(8,128)(2,1)S(1)}, u32[]{:S(2)}, u32[]{:S(2)}) collective-permute-start(bf16[256,768]{1,0:T(8,128)(2,1)S(1)} %get-tuple-element.74), channel_id=1, source_target_pairs={{0,4},{1,13},{2,6},{3,15},{4,0},{5,9},{6,2},{7,11},{8,12},{9,5},{1... | collective-permute-start | bytes 1179656 | tf_op jit(solution)/shard_map/ppermute | solution.py:36
  49.6 0.1 late.1.before
  49.6 0.0 copy-start.1
  49.7 0.0 copy-start.3
  49.7 0.1 collective-permute-start.21
  49.8 0.0 collective-permute-done.16.other
  49.8 0.1 total.1.a
  49.9 5.7 %collective-permute-start.17 = (f32[8,128]{1,0:T(8,128)S(1)}, f32[8,128]{1,0:T(8,128)S(1)}, u32[]{:S(2)}, u32[]{:S(2)}) collective-permute-start(f32[8,128]{1,0:T(8,128)S(1)} %total.1.a), channel_id=1, source_target_pairs={{0,32},{1,225},{2,34},{3,227},{4,36},{5,229},{6,38},{7,231},{8,40}... | collective-permute-start | bytes 12296 | tf_op jit(solution)/shard_map/ppermute | solution.py:36
  55.5 1.3 %collective-permute-done.17.b = f32[8,128]{1,0:T(8,128)S(1)} collective-permute-done((f32[8,128]{1,0:T(8,128)S(1)}, f32[8,128]{1,0:T(8,128)S(1)}, u32[]{:S(2)}, u32[]{:S(2)}) %collective-permute-start.17) | collective-permute-done | bytes 4128 | tf_op jit(solution)/shard_map/ppermute | solution.py:36
  56.8 0.0 collective-permute-start.18
  56.8 1.2 %collective-permute-done.18.other = f32[8,128]{1,0:T(8,128)S(1)} collective-permute-done((f32[8,128]{1,0:T(8,128)S(1)}, f32[8,128]{1,0:T(8,128)S(1)}, u32[]{:S(2)}, u32[]{:S(2)}) %collective-permute-start.18) | collective-permute-done | bytes 4128 | tf_op jit(solution)/shard_map/ppermute | solution.py:29
  58.0 2.1 %collective-permute-start.19 = (f32[8,128]{1,0:T(8,128)S(1)}, f32[8,128]{1,0:T(8,128)S(1)}, u32[]{:S(2)}, u32[]{:S(2)}) collective-permute-start(f32[8,128]{1,0:T(8,128)S(1)} %planes.1.a), channel_id=1, source_target_pairs={{0,160},{1,97},{2,162},{3,99},{4,164},{5,101},{6,166},{7,103},{8,1... | collective-permute-start | bytes 12296 | tf_op jit(solution)/shard_map/ppermute | solution.py:36
  60.1 0.0 collective-permute-done.22.py
  60.1 1.6 %grad.1 = (bf16[256,768]{1,0:T(8,128)(2,1)}, bf16[256,768]{1,0:T(8,128)(2,1)}, f32[8,128]{1,0:T(8,128)S(1)}) custom-call(f32[1]{0:T(128)S(6)} %copy.8.scale, bf16[256,768]{1,0:T(8,128)(2,1)S(1)} %copy-done.1, bf16[256,768]{1,0:T(8,128)(2,1)S(1)} %copy-done.3, f32[256,768]{1,0:T(8,128)S(1)} %get-tuple-element.72.img_back, ...), custom_call_target="tpu_custom_call" | custom-call | flops 1760000000 | bytes 5115908 | tf_op jit(solution)/shard_map/grad/pallas_call | solution.py:63
  61.7 1.8 %collective-permute-done.19.b = f32[8,128]{1,0:T(8,128)S(1)} collective-permute-done((f32[8,128]{1,0:T(8,128)S(1)}, f32[8,128]{1,0:T(8,128)S(1)}, u32[]{:S(2)}, u32[]{:S(2)}) %collective-permute-start.19) | collective-permute-done | bytes 4128 | tf_op jit(solution)/shard_map/ppermute | solution.py:36
  63.6 0.9 %collective-permute-start.23 = (f32[8,128]{1,0:T(8,128)S(1)}, f32[8,128]{1,0:T(8,128)S(1)}, u32[]{:S(2)}, u32[]{:S(2)}) collective-permute-start(f32[8,128]{1,0:T(8,128)S(1)} %side.3.held), channel_id=1, source_target_pairs={{0,1},{1,0},{2,3},{3,2},{4,5},{5,4},{6,7},{7,6},{8,9},{9,8},{10,11... | collective-permute-start | bytes 12296 | tf_op jit(solution)/shard_map/ppermute | solution.py:29
  64.5 0.8 %collective-permute-done.23.other = f32[8,128]{1,0:T(8,128)S(1)} collective-permute-done((f32[8,128]{1,0:T(8,128)S(1)}, f32[8,128]{1,0:T(8,128)S(1)}, u32[]{:S(2)}, u32[]{:S(2)}) %collective-permute-start.23) | collective-permute-done | bytes 4128 | tf_op jit(solution)/shard_map/ppermute | solution.py:29
  65.3 0.7 scalar.1
  (17 shorter events, 0.1 us)
Async XLA Ops:
  0.6 11.5 %collective-permute-start.1 = (bf16[256,768]{1,0:T(8,128)(2,1)}, bf16[256,768]{1,0:T(8,128)(2,1)S(1)}, u32[]{:S(2)}, u32[]{:S(2)}) collective-permute-start(bf16[256,768]{1,0:T(8,128)(2,1)} %image.5), channel_id=1, source_target_pairs={{0,12},{1,13},{2,14},{3,15},{4,8},{5,9},{6,10},{7,11},{8,4},{9,5},... | collective-permute-start | bytes 1179656 | tf_op jit(solution)/shard_map/ppermute | solution.py:29
  4.0 9.9 %collective-permute-start = (bf16[256,768]{1,0:T(8,128)(2,1)}, bf16[256,768]{1,0:T(8,128)(2,1)S(1)}, u32[]{:S(2)}, u32[]{:S(2)}) collective-permute-start(bf16[256,768]{1,0:T(8,128)(2,1)} %image.5), channel_id=1, source_target_pairs={{0,4},{1,5},{2,6},{3,7},{4,0},{5,1},{6,2},{7,3},{8,12},{9,13},{10,... | collective-permute-start | bytes 1179656 | tf_op jit(solution)/shard_map/ppermute | solution.py:29
  4.0 11.5 %collective-permute-start.3 = (bf16[256,768]{1,0:T(8,128)(2,1)}, bf16[256,768]{1,0:T(8,128)(2,1)S(1)}, u32[]{:S(2)}, u32[]{:S(2)}) collective-permute-start(bf16[256,768]{1,0:T(8,128)(2,1)} %text.5), channel_id=1, source_target_pairs={{0,2},{1,3},{2,0},{3,1},{4,6},{5,7},{6,4},{7,5},{8,10},{9,11},{10,... | collective-permute-start | bytes 1179656 | tf_op jit(solution)/shard_map/ppermute | solution.py:29
  6.9 10.3 %collective-permute-start.5 = (bf16[256,768]{1,0:T(8,128)(2,1)}, bf16[256,768]{1,0:T(8,128)(2,1)S(1)}, u32[]{:S(2)}, u32[]{:S(2)}) collective-permute-start(bf16[256,768]{1,0:T(8,128)(2,1)} %text.5), channel_id=1, source_target_pairs={{0,1},{1,0},{2,3},{3,2},{4,5},{5,4},{6,7},{7,6},{8,9},{9,8},{10,11... | collective-permute-start | bytes 1179656 | tf_op jit(solution)/shard_map/ppermute | solution.py:29
  9.1 1.0 %copy-start = (bf16[256,768]{1,0:T(8,128)(2,1)S(1)}, bf16[256,768]{1,0:T(8,128)(2,1)}, u32[]{:S(2)}) copy-start(bf16[256,768]{1,0:T(8,128)(2,1)} %image.5) | copy-start | bytes 1179652
  10.1 1.0 %copy-start.2 = (bf16[256,768]{1,0:T(8,128)(2,1)S(1)}, bf16[256,768]{1,0:T(8,128)(2,1)}, u32[]{:S(2)}) copy-start(bf16[256,768]{1,0:T(8,128)(2,1)} %text.5) | copy-start | bytes 1179652
  13.9 3.4 %copy-start.4 = (s32[256]{0:T(256)S(1)}, s32[256]{0:T(256)}, u32[]{:S(2)}) copy-start(s32[256]{0:T(256)} %param.6) | copy-start | bytes 3076
  13.9 7.9 %collective-permute-start.2 = (bf16[256,768]{1,0:T(8,128)(2,1)S(1)}, bf16[256,768]{1,0:T(8,128)(2,1)S(1)}, u32[]{:S(2)}, u32[]{:S(2)}) collective-permute-start(bf16[256,768]{1,0:T(8,128)(2,1)S(1)} %pick.1), channel_id=1, source_target_pairs={{0,4},{1,13},{2,6},{3,15},{4,0},{5,9},{6,2},{7,11},{8,12},{9,5},{1... | collective-permute-start | bytes 1179656 | tf_op jit(solution)/shard_map/ppermute | solution.py:36
  15.6 4.3 %collective-permute-start.4 = (bf16[256,768]{1,0:T(8,128)(2,1)S(1)}, bf16[256,768]{1,0:T(8,128)(2,1)S(1)}, u32[]{:S(2)}, u32[]{:S(2)}) collective-permute-start(bf16[256,768]{1,0:T(8,128)(2,1)S(1)} %collective-permute-done.3.t2), channel_id=1, source_target_pairs={{0,1},{1,0},{2,3},{3,2},{4,5},{5,4},{6,7},{7,6},{8,9},{9,8},{10,11... | collective-permute-start | bytes 1179656 | tf_op jit(solution)/shard_map/ppermute | solution.py:29
  23.0 3.1 %collective-permute-start.8 = (f32[4,1024]{1,0:T(4,128)S(1)}, f32[4,1024]{1,0:T(4,128)S(1)}, u32[]{:S(2)}, u32[]{:S(2)}) collective-permute-start(f32[4,1024]{1,0:T(4,128)S(1)} %get-tuple-element.52.mine), channel_id=1, source_target_pairs={{0,1},{1,0},{2,3},{3,2},{4,5},{5,4},{6,7},{7,6},{8,9},{9,8},{10,11... | collective-permute-start | bytes 49160 | tf_op jit(solution)/shard_map/ppermute | solution.py:29
  24.9 4.3 %collective-permute-start.6 = (f32[4,1024]{1,0:T(4,128)S(1)}, f32[4,1024]{1,0:T(4,128)S(1)}, u32[]{:S(2)}, u32[]{:S(2)}) collective-permute-start(f32[4,1024]{1,0:T(4,128)S(1)} %get-tuple-element.51.mine), channel_id=1, source_target_pairs={{0,12},{1,13},{2,14},{3,15},{4,8},{5,9},{6,10},{7,11},{8,4},{9,5},... | collective-permute-start | bytes 49160 | tf_op jit(solution)/shard_map/ppermute | solution.py:29
  26.2 5.7 %collective-permute-start.9 = (f32[8,1024]{1,0:T(8,128)S(1)}, f32[8,1024]{1,0:T(8,128)S(1)}, u32[]{:S(2)}, u32[]{:S(2)}) collective-permute-start(f32[8,1024]{1,0:T(8,128)S(1)} %join.3.col), channel_id=1, source_target_pairs={{0,2},{1,3},{2,0},{3,1},{4,6},{5,7},{6,4},{7,5},{8,10},{9,11},{10,... | collective-permute-start | bytes 98312 | tf_op jit(solution)/shard_map/ppermute | solution.py:29
  29.2 2.7 %collective-permute-start.7 = (f32[4,1024]{1,0:T(4,128)S(1)}, f32[4,1024]{1,0:T(4,128)S(1)}, u32[]{:S(2)}, u32[]{:S(2)}) collective-permute-start(f32[4,1024]{1,0:T(4,128)S(1)} %join.2.row), channel_id=1, source_target_pairs={{0,4},{1,5},{2,6},{3,7},{4,0},{5,1},{6,2},{7,3},{8,12},{9,13},{10,... | collective-permute-start | bytes 49160 | tf_op jit(solution)/shard_map/ppermute | solution.py:29
  32.0 4.7 %collective-permute-start.10 = (f32[8,128]{1,0:T(8,128)S(1)}, f32[8,128]{1,0:T(8,128)S(1)}, u32[]{:S(2)}, u32[]{:S(2)}) collective-permute-start(f32[8,128]{1,0:T(8,128)S(1)} %get-tuple-element.53.row), channel_id=1, source_target_pairs={{0,1},{1,0},{2,3},{3,2},{4,5},{5,4},{6,7},{7,6},{8,9},{9,8},{10,11... | collective-permute-start | bytes 12296 | tf_op jit(solution)/shard_map/ppermute | solution.py:29
  34.1 2.7 %collective-permute-start.11 = (f32[8,128]{1,0:T(8,128)S(1)}, f32[8,128]{1,0:T(8,128)S(1)}, u32[]{:S(2)}, u32[]{:S(2)}) collective-permute-start(f32[8,128]{1,0:T(8,128)S(1)} %get-tuple-element.54.col), channel_id=1, source_target_pairs={{0,4},{1,5},{2,6},{3,7},{4,0},{5,1},{6,2},{7,3},{8,12},{9,13},{10,... | collective-permute-start | bytes 12296 | tf_op jit(solution)/shard_map/ppermute | solution.py:29
  36.9 7.8 %collective-permute-start.14 = (bf16[512,768]{1,0:T(8,128)(2,1)S(1)}, bf16[512,768]{1,0:T(8,128)(2,1)S(1)}, u32[]{:S(2)}, u32[]{:S(2)}) collective-permute-start(bf16[512,768]{1,0:T(8,128)(2,1)S(1)} %get-tuple-element.68), channel_id=1, source_target_pairs={{0,1},{1,0},{2,3},{3,2},{4,5},{5,4},{6,7},{7,6},{8,9},{9,8},{10,11... | collective-permute-start | bytes 2359304 | tf_op jit(solution)/shard_map/ppermute | solution.py:29
  38.1 9.4 %collective-permute-start.15 = (bf16[256,768]{1,0:T(8,128)(2,1)S(1)}, bf16[256,768]{1,0:T(8,128)(2,1)S(1)}, u32[]{:S(2)}, u32[]{:S(2)}) collective-permute-start(bf16[256,768]{1,0:T(8,128)(2,1)S(1)} %get-tuple-element.71), channel_id=1, source_target_pairs={{0,4},{1,13},{2,6},{3,15},{4,0},{5,9},{6,2},{7,11},{8,12},{9,5},{1... | collective-permute-start | bytes 1179656 | tf_op jit(solution)/shard_map/ppermute | solution.py:36
  39.4 3.7 %collective-permute-start.12 = (f32[8,128]{1,0:T(8,128)S(1)}, f32[8,128]{1,0:T(8,128)S(1)}, u32[]{:S(2)}, u32[]{:S(2)}) collective-permute-start(f32[8,128]{1,0:T(8,128)S(1)} %get-tuple-element.64.before.a), channel_id=1, source_target_pairs={{0,16},{16,0},{32,48},{48,32},{64,80},{80,64},{96,112},{112,96},{1... | collective-permute-start | bytes 12296 | tf_op jit(solution)/shard_map/ppermute | solution.py:29
  43.1 4.4 %collective-permute-start.13 = (f32[8,128]{1,0:T(8,128)S(1)}, f32[8,128]{1,0:T(8,128)S(1)}, u32[]{:S(2)}, u32[]{:S(2)}) collective-permute-start(f32[8,128]{1,0:T(8,128)S(1)} %side.2.before.a), channel_id=1, source_target_pairs={{0,18},{1,13},{2,16},{3,15},{4,22},{5,9},{6,20},{7,11},{8,26},{9,5... | collective-permute-start | bytes 12296 | tf_op jit(solution)/shard_map/ppermute | solution.py:36
  44.8 15.3 %collective-permute-start.22 = (bf16[256,768]{1,0:T(8,128)(2,1)S(1)}, bf16[256,768]{1,0:T(8,128)(2,1)S(1)}, u32[]{:S(2)}, u32[]{:S(2)}) collective-permute-start(bf16[256,768]{1,0:T(8,128)(2,1)S(1)} %get-tuple-element.70.before), channel_id=1, source_target_pairs={{0,2},{1,3},{2,0},{3,1},{4,6},{5,7},{6,4},{7,5},{8,10},{9,11},{10,... | collective-permute-start | bytes 1179656 | tf_op jit(solution)/shard_map/ppermute | solution.py:29
  47.5 2.3 %collective-permute-start.16 = (f32[8,128]{1,0:T(8,128)S(1)}, f32[8,128]{1,0:T(8,128)S(1)}, u32[]{:S(2)}, u32[]{:S(2)}) collective-permute-start(f32[8,128]{1,0:T(8,128)S(1)} %sides.1.before.mine), channel_id=1, source_target_pairs={{0,1},{1,0},{2,3},{3,2},{4,5},{5,4},{6,7},{7,6},{8,9},{9,8},{10,11... | collective-permute-start | bytes 12296 | tf_op jit(solution)/shard_map/ppermute | solution.py:29
  48.4 11.7 %collective-permute-start.20 = (bf16[256,768]{1,0:T(8,128)(2,1)S(1)}, bf16[256,768]{1,0:T(8,128)(2,1)S(1)}, u32[]{:S(2)}, u32[]{:S(2)}) collective-permute-start(bf16[256,768]{1,0:T(8,128)(2,1)S(1)} %get-tuple-element.74), channel_id=1, source_target_pairs={{0,4},{1,13},{2,6},{3,15},{4,0},{5,9},{6,2},{7,11},{8,12},{9,5},{1... | collective-permute-start | bytes 1179656 | tf_op jit(solution)/shard_map/ppermute | solution.py:36
  49.6 10.5 %copy-start.1 = (bf16[256,768]{1,0:T(8,128)(2,1)S(1)}, bf16[256,768]{1,0:T(8,128)(2,1)}, u32[]{:S(2)}) copy-start(bf16[256,768]{1,0:T(8,128)(2,1)} %image.5) | copy-start | bytes 1179652
  49.7 10.5 %copy-start.3 = (bf16[256,768]{1,0:T(8,128)(2,1)S(1)}, bf16[256,768]{1,0:T(8,128)(2,1)}, u32[]{:S(2)}) copy-start(bf16[256,768]{1,0:T(8,128)(2,1)} %text.5) | copy-start | bytes 1179652
  49.7 10.4 %collective-permute-start.21 = (bf16[256,768]{1,0:T(8,128)(2,1)S(1)}, bf16[256,768]{1,0:T(8,128)(2,1)S(1)}, u32[]{:S(2)}, u32[]{:S(2)}) collective-permute-start(bf16[256,768]{1,0:T(8,128)(2,1)S(1)} %late.1.before), channel_id=1, source_target_pairs={{0,12},{1,5},{2,14},{3,7},{4,8},{5,1},{6,10},{7,3},{8,4},{9,13},{1... | collective-permute-start | bytes 1179656 | tf_op jit(solution)/shard_map/ppermute | solution.py:36
  49.9 6.9 %collective-permute-start.17 = (f32[8,128]{1,0:T(8,128)S(1)}, f32[8,128]{1,0:T(8,128)S(1)}, u32[]{:S(2)}, u32[]{:S(2)}) collective-permute-start(f32[8,128]{1,0:T(8,128)S(1)} %total.1.a), channel_id=1, source_target_pairs={{0,32},{1,225},{2,34},{3,227},{4,36},{5,229},{6,38},{7,231},{8,40}... | collective-permute-start | bytes 12296 | tf_op jit(solution)/shard_map/ppermute | solution.py:36
  56.8 1.2 %collective-permute-start.18 = (f32[8,128]{1,0:T(8,128)S(1)}, f32[8,128]{1,0:T(8,128)S(1)}, u32[]{:S(2)}, u32[]{:S(2)}) collective-permute-start(f32[8,128]{1,0:T(8,128)S(1)} %add.1.held), channel_id=1, source_target_pairs={{0,1},{1,0},{2,3},{3,2},{4,5},{5,4},{6,7},{7,6},{8,9},{9,8},{10,11... | collective-permute-start | bytes 12296 | tf_op jit(solution)/shard_map/ppermute | solution.py:29
  58.0 5.5 %collective-permute-start.19 = (f32[8,128]{1,0:T(8,128)S(1)}, f32[8,128]{1,0:T(8,128)S(1)}, u32[]{:S(2)}, u32[]{:S(2)}) collective-permute-start(f32[8,128]{1,0:T(8,128)S(1)} %planes.1.a), channel_id=1, source_target_pairs={{0,160},{1,97},{2,162},{3,99},{4,164},{5,101},{6,166},{7,103},{8,1... | collective-permute-start | bytes 12296 | tf_op jit(solution)/shard_map/ppermute | solution.py:36
  63.6 1.8 %collective-permute-start.23 = (f32[8,128]{1,0:T(8,128)S(1)}, f32[8,128]{1,0:T(8,128)S(1)}, u32[]{:S(2)}, u32[]{:S(2)}) collective-permute-start(f32[8,128]{1,0:T(8,128)S(1)} %side.3.held), channel_id=1, source_target_pairs={{0,1},{1,0},{2,3},{3,2},{4,5},{5,4},{6,7},{7,6},{8,9},{9,8},{10,11... | collective-permute-start | bytes 12296 | tf_op jit(solution)/shard_map/ppermute | solution.py:29
